TPU v7x, 512 devices: a whole 4x8x8 slice. The times are simulated.
512 devices in a mesh: dp: 32 (over y_lo, x, core), tensor: 16 (over z, y_hi).
Axes of the slice: x: 4, y: 8 (y_hi: 2, y_lo: 4; y = y_hi * 4 + y_lo), z: 8, core: 2. Of those that a mesh axis runs over, the one named last changes fastest.
Arguments:
- norm_input: bfloat16 [65536, 8192], P(('dp', 'tensor')), may hold values from -6 to 6
- key_grad: bfloat16 [65536, 512], P(('dp', 'tensor')), may hold values from -100 to 100
- positions: int32 [65536], P(('dp', 'tensor')), may hold values from 0 to 8191
- norm_gain: bfloat16 [8192], replicated, may hold values from 0.25 to 1.75
- key_weight: bfloat16 [512, 8192], P('dp', 'tensor'), may hold values from -0.0625 to 0.0625
- first_moment: float32 [512, 8192], P('dp', 'tensor'), may hold values from -6 to 6
- second_moment: float32 [512, 8192], P('dp', 'tensor'), may hold values from 0.1 to 4
Outputs:
- input_grad: bfloat16 [65536, 8192], P(('dp', 'tensor'))
- new_weight: bfloat16 [512, 8192], P(None, 'tensor')
- new_first: float32 [512, 8192], P('dp', 'tensor')
- new_second: float32 [512, 8192], P('dp', 'tensor')
All inputs are finite; a program needn't handle non-finite values.
Results may differ from a plain program's by a relative error of at most 0.01.
Values may be sent and summed in bfloat16 or wider, within the bound.
No kernel may reach another device: no remote copies, remote signals or barrier semaphores. Data moves between devices by JAX's collectives and lax.ppermute only.
A program may use at most 64 MiB of HBM per device.

v0:
```python
import functools
import math

import jax
import jax.numpy as jnp
from jax import lax
from jax.sharding import Mesh
from jax.sharding import PartitionSpec as P

D = 8192
KV_HEADS = 4
HEAD = 128
TENSOR = ("tensor_0", "tensor_1")
DP = ("dp_0", "dp_1", "dp_2")
DP_TENSOR = ("dp_0", "dp_1", "dp_2", "tensor_0", "tensor_1")


eps_norm = 1e-05
beta_one = 0.9
beta_two = 0.95
learn_rate = 0.0003
decay_rate = 0.1
eps_adam = 1e-08


def whole_of(x, axes, dim):
    out = x
    for number in range(len(axes) - 1, -1, -1):
        out = lax.all_gather(out, axes[number], axis=dim, tiled=True)
    return out


def sent_to_all(x, axis):
    copies = jnp.broadcast_to(x, (lax.axis_size(axis), *x.shape))
    return lax.all_to_all(copies, axis, split_axis=0, concat_axis=0, tiled=True)


def joined_along(blocks, dim):
    dims = list(blocks.shape[1:])
    dims[dim] *= blocks.shape[0]
    return jnp.moveaxis(blocks, 0, dim).reshape(dims)


def gather_directly(x, axis, dim):
    blocks = sent_to_all(x, axis)
    return joined_along(blocks, dim)


def over_copies(x, axis):
    everything = sent_to_all(x, axis)
    return jnp.sum(everything, axis=0)


def together(arrays, axis):
    ends = [0]
    for a in arrays:
        ends.append(ends[-1] + a.size)
    total = over_copies(jnp.concatenate([a.ravel() for a in arrays]), axis)
    return tuple((total[b:e].reshape(a.shape) for a, b, e in zip(arrays, ends, ends[1:])))


def in_blocks(x, dim, count):
    dims = x.shape
    blocks = x.reshape(*dims[:dim], count, dims[dim] // count, *dims[dim + 1 :])
    return jnp.moveaxis(blocks, dim, 0)


def sum_at_owner(x, axis, dim):
    count = lax.axis_size(axis)
    blocks = lax.all_to_all(in_blocks(x, dim, count), axis, 0, 0, tiled=True)
    return jnp.sum(blocks.astype(jnp.float32), axis=0)


def one_axis_at_a_time(x, axes):
    return functools.reduce(lax.psum, axes, x)


def unrotate(incoming, positions):
    row_count = incoming.shape[0]
    half_width = HEAD // 2
    frequency = 500000.0 ** (-(2.0 * jnp.arange(half_width, dtype=jnp.float32)) / HEAD)
    angles = positions.astype(jnp.float32)[:, None] * frequency[None, :]
    cosine = jnp.cos(angles)[:, None, :]
    sine_table = jnp.sin(angles)[:, None, :]
    pieces = incoming.astype(jnp.float32).reshape(row_count, KV_HEADS, 2, half_width)
    first_half = pieces[:, :, 0, :]
    second_half = pieces[:, :, 1, :]
    upper_part = first_half * cosine + second_half * sine_table
    lower_part = second_half * cosine - first_half * sine_table
    return (
        jnp.stack([upper_part, lower_part], axis=2)
        .reshape(row_count, KV_HEADS * HEAD)
        .astype(jnp.bfloat16)
    )


def body(norm_input, key_grad, positions, norm_gain, key_weight, first_moment, second_moment):
    local_width = key_weight.shape[1]
    gain_full = norm_gain.astype(jnp.float32)
    gain_local = lax.dynamic_slice_in_dim(
        gain_full, lax.axis_index(TENSOR) * local_width, local_width, 0
    )
    rotated_back = unrotate(key_grad, positions)
    key_rows = whole_of(rotated_back, TENSOR, 0)
    upstream_local = jnp.dot(
        key_rows, gather_directly(key_weight, DP, 0), preferred_element_type=jnp.float32
    )
    received = lax.all_to_all(norm_input, TENSOR, split_axis=1, concat_axis=0, tiled=True)
    local_f32 = received.astype(jnp.float32)
    weighted = upstream_local * gain_local
    square_sum, cross_sum = together(
        (jnp.sum(local_f32 * local_f32, axis=1), jnp.sum(weighted * local_f32, axis=1)), TENSOR
    )
    scale_inv = lax.rsqrt(square_sum / D + eps_norm)[:, None]
    normalized = local_f32 * scale_inv
    feature_normed = (normalized * gain_local).astype(jnp.bfloat16)
    inner = scale_inv * (cross_sum / D)[:, None]
    local_grad = (scale_inv * (weighted - normalized * inner)).astype(jnp.bfloat16)
    input_grad = lax.all_to_all(local_grad, TENSOR, split_axis=0, concat_axis=1, tiled=True)
    grad_shard = sum_at_owner(
        lax.dot_general(
            key_rows, feature_normed, (((0,), (0,)), ((), ())), preferred_element_type=jnp.float32
        ).astype(jnp.bfloat16),
        DP,
        0,
    )
    total_square = one_axis_at_a_time(jnp.sum(grad_shard * grad_shard), DP_TENSOR)
    clip_limit = math.sqrt(KV_HEADS * HEAD * D)
    clip_factor = jnp.minimum(1.0, clip_limit / (jnp.sqrt(total_square) + 1e-06))
    clipped = grad_shard * clip_factor
    new_first = beta_one * first_moment + (1.0 - beta_one) * clipped
    new_second = beta_two * second_moment + (1.0 - beta_two) * clipped * clipped
    own_rows = key_weight.astype(jnp.float32)
    updated = (
        own_rows * (1.0 - learn_rate * decay_rate)
        - learn_rate * new_first / (jnp.sqrt(new_second) + eps_adam)
    ).astype(jnp.bfloat16)
    new_weight = gather_directly(updated, DP, 0)
    return (input_grad, new_weight, new_first, new_second)


def solution(mesh):
    split = Mesh(
        mesh.devices.reshape(4, 4, 2, 8, 2), ("dp_0", "dp_1", "dp_2", "tensor_0", "tensor_1")
    )
    placed = (
        P(DP_TENSOR, None),
        P(DP_TENSOR, None),
        P(DP_TENSOR),
        P(),
        P(DP, TENSOR),
        P(DP, TENSOR),
        P(DP, TENSOR),
    )
    return jax.shard_map(
        body,
        mesh=split,
        in_specs=placed,
        out_specs=(P(DP_TENSOR, None), P(None, TENSOR), P(DP, TENSOR), P(DP, TENSOR)),
        check_vma=False,
    )
```

profile of v0, /device:TPU:25, one launch (start us, length us, event | category | flops | bytes accessed | tf_op | source)
XLA Modules:
  0.0 381.5 jit_solution(15620456847139813691)
XLA Ops:
  7.2 3.1 copy.29
  10.3 12.8 %all-to-all-start = ((bf16[128,16,512]{2,0,1:T(8,128)(2,1)}), bf16[128,16,512]{2,0,1:T(8,128)(2,1)S(1)}, u32[]{:S(2)}, u32[]{:S(2)}) async-start(bf16[128,16,512]{2,0,1:T(8,128)(2,1)} %bitcast.40), calls=%async_computation | async-start | bytes 4194304 | tf_op jit(solution)/shard_map/all_to_all | solution.py:108
  23.7 82.9 %all_gather.6 = bf16[256,512]{0,1:T(8,128)(2,1)} all-gather(bf16[128,512]{0,1:T(8,128)(2,1)S(1)} %bitcast.46), channel_id=1, replica_groups=mesh['dp_0'=4,'dp_1'=4,'dp_2'=2,'tensor_0'=8,'tensor_1'=2] {'tensor_1'}, dimensions={0}, use_global_device_ids=true | all-gather | bytes 393216 | tf_op jit(solution)/shard_map/all_gather | solution.py:29
  106.6 0.9 broadcast_in_dim.6
  107.5 9.1 %all-to-all-start.1 = ((bf16[32,16,512]{2,1,0:T(8,128)(2,1)}), bf16[32,16,512]{2,1,0:T(8,128)(2,1)S(1)}, u32[]{:S(2)}, u32[]{:S(2)}) async-start(bf16[32,16,512]{2,1,0:T(8,128)(2,1)} %broadcast_in_dim.6), calls=%async_computation.1 | async-start | bytes 1048576 | tf_op jit(solution)/shard_map/all_to_all | solution.py:35
  116.6 0.8 dynamic-slice_convert_fusion
  117.8 13.1 %all-to-all-done.1 = bf16[32,16,512]{2,1,0:T(8,128)(2,1)S(1)} async-done(((bf16[32,16,512]{2,1,0:T(8,128)(2,1)}), bf16[32,16,512]{2,1,0:T(8,128)(2,1)S(1)}, u32[]{:S(2)}, u32[]{:S(2)}) %all-to-all-start.1) | async-done | bytes 524320 | tf_op jit(solution)/shard_map/all_to_all | solution.py:35
  130.9 23.0 %all-gather.2.cloned.1.call-done = bf16[2048,512]{0,1:T(8,128)(2,1)} async-done(((bf16[256,512]{0,1:T(8,128)(2,1)}), bf16[2048,512]{0,1:T(8,128)(2,1)}) %all-gather.2.cloned.1.call-update) | async-done | bytes 2097168 | tf_op jit(solution)/shard_map/all_gather | solution.py:29
  153.9 4.9 %fusion.7 = (f32[2048]{0:T(1024)S(1)}, f32[2048,512]{1,0:T(8,128)}) fusion(bf16[128,16,512]{2,0,1:T(8,128)(2,1)S(1)} %all-to-all-done, f32[512]{0:T(512)S(1)} %dynamic-slice_convert_fusion, bf16[2048,512]{0,1:T(8,128)(2,1)} %all-gather.2.cloned.1.call-done, bf16[512,512]{1,0:T(8,128)(2,1)S(1)} %bitcast.48), kind=kOutput, calls=%fused_computation.10 | convolution fusion | flops 1077934080 | bytes 8923136 | tf_op jit(solution)/shard_map/dot_general | solution.py:105
  159.0 18.1 %all_to_all.53 = f32[16,1,4096]{2,1,0:T(1,128)S(1)} all-to-all(f32[16,1,4096]{2,1,0:T(1,128)S(1)} %broadcast_in_dim.7), channel_id=1, replica_groups=mesh['dp_0'=4,'dp_1'=4,'dp_2'=2,'tensor_0'=8,'tensor_1'=2] {'tensor_0','..., dimensions={0} | all-to-all | bytes 524288 | tf_op jit(solution)/shard_map/all_to_all | solution.py:35
  177.3 4.0 %fusion.5 = (bf16[2048,512]{1,0:T(8,128)(2,1)S(1)}, bf16[2048,512]{1,0:T(8,128)(2,1)}) fusion(bf16[128,16,512]{2,0,1:T(8,128)(2,1)S(1)} %all-to-all-done, f32[2048]{0:T(1024)S(1)} %get-tuple-element.11, f32[512]{0:T(512)S(1)} %dynamic-slice_convert_fusion, f32[2048]{0:T(1024)S(1)} %get-tuple-element.12, f32[2048,512]{1,0:T(8,128)} %get-tuple-element.16), kind=kLoop, calls=%fused_computation.8 | loop fusion | flops 9437184 | bytes 10504192 | tf_op jit(solution)/shard_map/convert_element_type | solution.py:116
  181.3 1.2 convolution_convert_fusion
  182.6 29.6 %all_to_all.54 = bf16[32,16,512]{2,1,0:T(8,128)(2,1)S(1)} all-to-all(bf16[32,16,512]{2,1,0:T(8,128)(2,1)S(1)} %bitcast.49), channel_id=1, replica_groups=mesh['dp_0'=4,'dp_1'=4,'dp_2'=2,'tensor_0'=8,'tensor_1'=2] {'dp_0','dp_1..., dimensions={0} | all-to-all | bytes 1048576 | tf_op jit(solution)/shard_map/all_to_all | solution.py:70
  212.9 7.5 %psum.35 = f32[]{:T(128)} all-reduce(f32[]{:T(128)} %multiply_reduce_fusion), channel_id=1, replica_groups=mesh['dp_0'=4,'dp_1'=4,'dp_2'=2,'tensor_0'=8,'tensor_1'=2] {'dp_0'}, use_global_device_ids=true, to_apply=%region_5.0 | all-reduce | flops 1 | bytes 8 | tf_op jit(solution)/shard_map/psum | solution.py:75
  220.4 8.1 %psum.36 = f32[]{:T(128)} all-reduce(f32[]{:T(128)} %psum.35), channel_id=1, replica_groups=mesh['dp_0'=4,'dp_1'=4,'dp_2'=2,'tensor_0'=8,'tensor_1'=2] {'dp_1'}, use_global_device_ids=true, to_apply=%region_6.0 | all-reduce | flops 1 | bytes 8 | tf_op jit(solution)/shard_map/psum | solution.py:75
  228.4 6.6 %psum.37 = f32[]{:T(128)} all-reduce(f32[]{:T(128)} %psum.36), channel_id=1, replica_groups=mesh['dp_0'=4,'dp_1'=4,'dp_2'=2,'tensor_0'=8,'tensor_1'=2] {'dp_2'}, use_global_device_ids=true, to_apply=%region_7.0 | all-reduce | flops 1 | bytes 8 | tf_op jit(solution)/shard_map/psum | solution.py:75
  235.0 11.6 %psum.38 = f32[]{:T(128)} all-reduce(f32[]{:T(128)} %psum.37), channel_id=1, replica_groups=mesh['dp_0'=4,'dp_1'=4,'dp_2'=2,'tensor_0'=8,'tensor_1'=2] {'tensor_0'}, use_global_device_ids=true, to_apply=%region_8.0 | all-reduce | flops 1 | bytes 8 | tf_op jit(solution)/shard_map/psum | solution.py:75
  246.6 8.3 %psum.39 = f32[]{:T(128)} all-reduce(f32[]{:T(128)} %psum.38), channel_id=1, replica_groups=mesh['dp_0'=4,'dp_1'=4,'dp_2'=2,'tensor_0'=8,'tensor_1'=2] {'tensor_1'}, use_global_device_ids=true, to_apply=%region_9.0 | all-reduce | flops 1 | bytes 8 | tf_op jit(solution)/shard_map/psum | solution.py:75
  255.6 0.6 subtract_convert_fusion.1
  256.3 25.3 %all_to_all.55 = bf16[32,16,512]{2,1,0:T(8,128)(2,1)S(1)} all-to-all(bf16[32,16,512]{2,1,0:T(8,128)(2,1)S(1)} %broadcast_in_dim.8), channel_id=1, replica_groups=mesh['dp_0'=4,'dp_1'=4,'dp_2'=2,'tensor_0'=8,'tensor_1'=2] {'dp_0','dp_1..., dimensions={0} | all-to-all | bytes 1048576 | tf_op jit(solution)/shard_map/all_to_all | solution.py:35
  281.6 4.7 %all-to-all-start.3 = ((bf16[16,128,512]{2,1,0:T(8,128)(2,1)}), bf16[16,128,512]{2,1,0:T(8,128)(2,1)S(1)}, u32[]{:S(2)}, u32[]{:S(2)}) async-start(bf16[16,128,512]{2,1,0:T(8,128)(2,1)} %bitcast.42), calls=%async_computation.3 | async-start | bytes 4194304 | tf_op jit(solution)/shard_map/all_to_all | solution.py:119
  286.4 86.0 %all-to-all-done.3 = bf16[16,128,512]{2,1,0:T(8,128)(2,1)S(1)} async-done(((bf16[16,128,512]{2,1,0:T(8,128)(2,1)}), bf16[16,128,512]{2,1,0:T(8,128)(2,1)S(1)}, u32[]{:S(2)}, u32[]{:S(2)}) %all-to-all-start.3) | async-done | bytes 2097184 | tf_op jit(solution)/shard_map/all_to_all | solution.py:119
  372.3 1.5 copy.27
  373.9 0.8 copy.31
  (30 shorter events, 2.1 us)
Async XLA Ops:
  10.3 12.9 %copy-start.5 = (s32[128]{0:T(128)S(1)}, s32[128]{0:T(128)}, u32[]{:S(2)}) copy-start(s32[128]{0:T(128)} %param.9) | copy-start | bytes 1540
  10.3 12.9 %copy-start = (bf16[128,512]{1,0:T(8,128)(2,1)S(1)}, bf16[128,512]{1,0:T(8,128)(2,1)}, u32[]{:S(2)}) copy-start(bf16[128,512]{1,0:T(8,128)(2,1)} %param.8) | copy-start | bytes 393220
  10.3 96.3 %all-to-all-start = ((bf16[128,16,512]{2,0,1:T(8,128)(2,1)}), bf16[128,16,512]{2,0,1:T(8,128)(2,1)S(1)}, u32[]{:S(2)}, u32[]{:S(2)}) async-start(bf16[128,16,512]{2,0,1:T(8,128)(2,1)} %bitcast.40), calls=%async_computation | async-start | bytes 4194304 | tf_op jit(solution)/shard_map/all_to_all | solution.py:108
  23.2 83.4 %copy-start.1 = (bf16[16,512]{1,0:T(8,128)(2,1)S(1)}, bf16[16,512]{1,0:T(8,128)(2,1)}, u32[]{:S(2)}) copy-start(bf16[16,512]{1,0:T(8,128)(2,1)} %param.11) | copy-start | bytes 49156
  23.2 130.7 %all-gather.2.cloned.1.call-start = ((), (), s32[]{:S(2)}) async-start(), calls=%async_computation.6 | async-start | bytes 2359296 | tf_op jit(solution)/shard_map/all_gather | solution.py:29
  107.5 23.5 %all-to-all-start.1 = ((bf16[32,16,512]{2,1,0:T(8,128)(2,1)}), bf16[32,16,512]{2,1,0:T(8,128)(2,1)S(1)}, u32[]{:S(2)}, u32[]{:S(2)}) async-start(bf16[32,16,512]{2,1,0:T(8,128)(2,1)} %broadcast_in_dim.6), calls=%async_computation.1 | async-start | bytes 1048576 | tf_op jit(solution)/shard_map/all_to_all | solution.py:35
  177.3 4.0 %copy-start.4 = (bf16[2048,512]{0,1:T(8,128)(2,1)S(1)}, bf16[2048,512]{0,1:T(8,128)(2,1)}, u32[]{:S(2)}) copy-start(bf16[2048,512]{0,1:T(8,128)(2,1)} %all-gather.2.cloned.1.call-done) | copy-start | bytes 6291460
  181.3 74.3 %copy-start.2 = (f32[16,512]{1,0:T(8,128)S(1)}, f32[16,512]{1,0:T(8,128)}, u32[]{:S(2)}) copy-start(f32[16,512]{1,0:T(8,128)} %param.12) | copy-start | bytes 98308
  181.3 74.3 %copy-start.3 = (f32[16,512]{1,0:T(8,128)S(1)}, f32[16,512]{1,0:T(8,128)}, u32[]{:S(2)}) copy-start(f32[16,512]{1,0:T(8,128)} %param.13) | copy-start | bytes 98308
  281.6 90.7 %all-to-all-start.3 = ((bf16[16,128,512]{2,1,0:T(8,128)(2,1)}), bf16[16,128,512]{2,1,0:T(8,128)(2,1)S(1)}, u32[]{:S(2)}, u32[]{:S(2)}) async-start(bf16[16,128,512]{2,1,0:T(8,128)(2,1)} %bitcast.42), calls=%async_computation.3 | async-start | bytes 4194304 | tf_op jit(solution)/shard_map/all_to_all | solution.py:119
Sparse Core Ops, SparseCore 0:
  106.7 47.1 all-gather.1
where the time goes:
time: 383 us; the launch traced here: 381 us
  blocking collectives  198 us (52%)
  waiting for transfers between devices  122 us (32%)
  starting transfers between devices  26.7 us (7%)
  between operations  15 us (4%)
  other arithmetic  7 us (2%)
  local copies, waits for them, and re-layouts  6.72 us (2%)
  matrix products  6.16 us (2%)
    all_to_all x1, waiting for transfers between devices, body(): lax.all_to_all(local_grad, TENSOR, split_axis=0, concat_axis=1, tiled=True)  86 us
    all_gather x1, blocking collectives, whole_of(): out = lax.all_gather(out, axes[number], axis=dim, tiled=True)  82.9 us
    all_to_all x2, blocking collectives, sent_to_all(): return lax.all_to_all(copies, axis, split_axis=0, concat_axis=0, tiled=True)  43.4 us
    psum x5, blocking collectives, one_axis_at_a_time(): return functools.reduce(lax.psum, axes, x)  42 us
    all_to_all x1, blocking collectives, sum_at_owner(): blocks = lax.all_to_all(in_blocks(x, dim, count), axis, 0, 0, tiled=True)  29.6 us
    all_gather x1, waiting for transfers between devices, whole_of(): out = lax.all_gather(out, axes[number], axis=dim, tiled=True)  23 us
    all_to_all x1, waiting for transfers between devices, sent_to_all(): return lax.all_to_all(copies, axis, split_axis=0, concat_axis=0, tiled=True)  13.1 us
    all_to_all x1, starting transfers between devices, body(): lax.all_to_all(norm_input, TENSOR, split_axis=1, concat_axis=0, tiled=True)  12.8 us
  transfers between devices with their start and end apart: 4, of which 3 were waited for; matrix products, arithmetic and copies ran while one was open for 1% of the time, Pallas kernels for 0%

commit v1 on v0

v1 whole, which is shorter than its diff:
```python
import math

import jax
import jax.numpy as jnp
from jax import lax
from jax.experimental import pallas as pl
from jax.experimental.pallas import tpu as pltpu
from jax.sharding import Mesh
from jax.sharding import PartitionSpec as P

D = 8192
KV_HEADS = 4
HEAD = 128
KV = KV_HEADS * HEAD
DP = ("yl", "x", "c")
TENSOR = ("z", "yh")
DP_TENSOR = DP + TENSOR
GROUP = ("x", "c")
PLANE = ("yl", "z", "yh")
N_GROUP = 8
N_PLANE = 64
WIDE = D // N_GROUP
COLS = WIDE + KV

eps_norm = 1e-05
beta_one = 0.9
beta_two = 0.95
learn_rate = 0.0003
decay_rate = 0.1
eps_adam = 1e-08

bf16 = jnp.bfloat16
f32 = jnp.float32


def exchange(x, axes):
    return lax.all_to_all(x, axes, split_axis=0, concat_axis=0, tiled=True)


def copies_for(x, count):
    return jnp.broadcast_to(x, (count, *x.shape))


def sum_over(x, axes, count):
    return jnp.sum(exchange(copies_for(x, count), axes), axis=0)


def rotation(positions):
    half_width = HEAD // 2
    frequency = 500000.0 ** (-(2.0 * jnp.arange(half_width, dtype=f32)) / HEAD)
    angles = positions.astype(f32)[:, None] * frequency[None, :]
    cosine = jnp.cos(angles)
    sine = jnp.sin(angles)
    return jnp.concatenate([cosine, cosine], axis=1), jnp.concatenate([sine, -sine], axis=1)


def prepare_kernel(x_ref, key_ref, cos_ref, sin_ref, gain_ref, send_ref, key_out_ref, scale_ref):
    x = x_ref[...].astype(f32)
    scale = lax.rsqrt(jnp.sum(x * x, axis=1, keepdims=True) / D + eps_norm)
    scale_ref[...] = jnp.broadcast_to(scale, scale_ref.shape)
    normed = (x * scale * gain_ref[...]).astype(bf16)
    for j in range(N_GROUP):
        send_ref[j, :, :WIDE] = normed[:, j * WIDE : (j + 1) * WIDE]
    for h in range(KV_HEADS):
        part = key_ref[:, h * HEAD : (h + 1) * HEAD].astype(f32)
        turned = part * cos_ref[...] + pltpu.roll(part, HEAD // 2, 1) * sin_ref[...]
        turned = turned.astype(bf16)
        key_out_ref[:, h * HEAD : (h + 1) * HEAD] = turned
        for j in range(N_GROUP):
            send_ref[j, :, WIDE + h * HEAD : WIDE + (h + 1) * HEAD] = turned


def prepare(x, key_grad, cosine, sine, gain):
    tokens = x.shape[0]
    tile = 32
    return pl.pallas_call(
        prepare_kernel,
        grid=(tokens // tile,),
        in_specs=[
            pl.BlockSpec((tile, D), lambda i: (i, 0)),
            pl.BlockSpec((tile, KV), lambda i: (i, 0)),
            pl.BlockSpec((tile, HEAD), lambda i: (i, 0)),
            pl.BlockSpec((tile, HEAD), lambda i: (i, 0)),
            pl.BlockSpec((1, D), lambda i: (0, 0)),
        ],
        out_specs=[
            pl.BlockSpec((N_GROUP, tile, COLS), lambda i: (0, i, 0)),
            pl.BlockSpec((tile, KV), lambda i: (i, 0)),
            pl.BlockSpec((tile, HEAD), lambda i: (i, 0)),
        ],
        out_shape=[
            jax.ShapeDtypeStruct((N_GROUP, tokens, COLS), bf16),
            jax.ShapeDtypeStruct((tokens, KV), bf16),
            jax.ShapeDtypeStruct((tokens, HEAD), f32),
        ],
        compiler_params=pltpu.CompilerParams(vmem_limit_bytes=56 * 1024 * 1024),
        cost_estimate=pl.CostEstimate(flops=8 * tokens * D, bytes_accessed=6 * 1024 * 1024, transcendentals=0),
    )(x, key_grad, cosine, sine, gain)


def product_kernel(key_ref, normed_ref, out_ref):
    tokens = key_ref.shape[0] * key_ref.shape[1]
    keys = key_ref[...].reshape(tokens, KV)
    normed = normed_ref[...].reshape(tokens, normed_ref.shape[2])
    total = lax.dot_general(keys, normed, (((0,), (0,)), ((), ())), preferred_element_type=f32)
    out_ref[...] = total.astype(bf16).reshape(out_ref.shape)


def product(received):
    count, tokens, _ = received.shape
    half = WIDE // 2
    return pl.pallas_call(
        product_kernel,
        grid=(2,),
        in_specs=[
            pl.BlockSpec((count, tokens, KV), lambda h: (0, 0, WIDE // KV)),
            pl.BlockSpec((count, tokens, half), lambda h: (0, 0, h)),
        ],
        out_specs=pl.BlockSpec((32, 1, 16, half), lambda h: (0, h, 0, 0)),
        out_shape=jax.ShapeDtypeStruct((32, 2, 16, half), bf16),
        compiler_params=pltpu.CompilerParams(vmem_limit_bytes=32 * 1024 * 1024),
        cost_estimate=pl.CostEstimate(
            flops=2 * count * tokens * KV * WIDE, bytes_accessed=4 * 1024 * 1024, transcendentals=0
        ),
    )(received, received)


def backward_kernel(core_ref, key_ref, own_ref, other_ref, x_ref, scale_ref, gain_ref, out_ref, held, cross):
    step = pl.program_id(0)
    core = core_ref[0]
    tokens = key_ref.shape[0]
    half = own_ref.shape[4]

    @pl.when(step == 0)
    def _():
        cross[...] = jnp.zeros_like(cross)

    for side, ref in ((core, own_ref), (1 - core, other_ref)):
        inside = pl.ds(pl.multiple_of(side * half, half), half)
        columns = pl.ds(pl.multiple_of(step * 2 * half + side * half, half), half)
        up = jnp.dot(key_ref[...], ref[...].reshape(KV, half), preferred_element_type=f32)
        weighted = up * gain_ref[:, inside]
        held[step, :, inside] = weighted
        term = jnp.sum(weighted * x_ref[:, columns].astype(f32), axis=1, keepdims=True)
        cross[...] += jnp.broadcast_to(term, (tokens, HEAD))

    @pl.when(step == pl.num_programs(0) - 1)
    def _():
        scale = scale_ref[:, :1]
        inner = scale * (cross[:, :1] / D)
        width = 2 * half
        for t in range(D // width):
            part = slice(t * width, (t + 1) * width)
            xhat = x_ref[:, part].astype(f32) * scale
            out_ref[:, part] = (scale * (held[t] - xhat * inner)).astype(bf16)


def backward(core, keys, own, other, x, scale, gain):
    tokens = x.shape[0]
    width = 512
    steps = D // width
    weights = pl.BlockSpec((1, 4, 1, 128, width // 2), lambda t, core: (t % 2, 0, t // 2, 0, 0))
    whole = lambda a: pl.BlockSpec(a.shape, lambda t, core: (0, 0))
    return pl.pallas_call(
        backward_kernel,
        grid_spec=pltpu.PrefetchScalarGridSpec(
            num_scalar_prefetch=1,
            grid=(steps,),
            in_specs=[
                whole(keys),
                weights,
                weights,
                whole(x),
                whole(scale),
                pl.BlockSpec((1, width), lambda t, core: (0, t)),
            ],
            out_specs=pl.BlockSpec((tokens, D), lambda t, core: (0, 0)),
            scratch_shapes=[pltpu.VMEM((steps, tokens, width), f32), pltpu.VMEM((tokens, HEAD), f32)],
        ),
        out_shape=jax.ShapeDtypeStruct((tokens, D), bf16),
        compiler_params=pltpu.CompilerParams(vmem_limit_bytes=56 * 1024 * 1024),
        cost_estimate=pl.CostEstimate(
            flops=2 * tokens * KV * D, bytes_accessed=12 * 1024 * 1024, transcendentals=0
        ),
    )(core, keys, own, other, x, scale, gain)


def weights_of_core(key_weight):
    rows, columns = key_weight.shape
    halves = key_weight.reshape(rows, 2, columns // 2).transpose(1, 0, 2)
    send = jnp.broadcast_to(halves, (4, *halves.shape)).reshape(N_GROUP, rows, columns // 2)
    pieces = exchange(send, GROUP).reshape(N_GROUP * rows, columns // 2)
    whole = lax.all_gather(pieces, ("yh", "yl", "z"), axis=0, tiled=True)
    return whole.reshape(2, 4, 8, *pieces.shape)


def body(norm_input, key_grad, positions, norm_gain, key_weight, first_moment, second_moment):
    gain = norm_gain.astype(f32)[None, :]
    core = lax.axis_index("c").astype(jnp.int32).reshape(1)
    own = weights_of_core(key_weight)
    cosine, sine = rotation(positions)
    send, keys, scale = prepare(norm_input, key_grad, cosine, sine, gain)
    received = exchange(send, GROUP)
    partial = product(received).reshape(N_PLANE, 16, 512)
    pieces = exchange(partial, PLANE)
    piece = jnp.sum(pieces.astype(f32), axis=0)
    own, _ = lax.optimization_barrier((own, piece))
    other = lax.ppermute(own, "c", [(0, 1), (1, 0)])

    swap = [(i * 8 + k, k * 8 + i) for i in range(8) for k in range(8)]
    grad_shard = lax.ppermute(piece, ("x", "c", "z"), swap)
    square = jnp.broadcast_to(jnp.sum(piece * piece), (8, 128))
    square = sum_over(square, GROUP, 8)
    square = sum_over(square, ("yh", "yl"), 8)
    square = sum_over(square, "z", 8)
    total_square = square[0, 0]

    clip_limit = math.sqrt(KV * D)
    clip_factor = jnp.minimum(1.0, clip_limit / (jnp.sqrt(total_square) + 1e-06))
    clipped = grad_shard * clip_factor
    new_first = beta_one * first_moment + (1.0 - beta_one) * clipped
    new_second = beta_two * second_moment + (1.0 - beta_two) * clipped * clipped
    own_rows = key_weight.astype(f32)
    updated = (
        own_rows * (1.0 - learn_rate * decay_rate)
        - learn_rate * new_first / (jnp.sqrt(new_second) + eps_adam)
    ).astype(bf16)
    new_weight = exchange(copies_for(updated, 32), DP).reshape(KV, 512)

    input_grad = backward(core, keys, own, other, norm_input, scale, gain)
    return (input_grad, new_weight, new_first, new_second)


def solution(mesh):
    split = Mesh(mesh.devices.reshape(4, 4, 2, 8, 2), ("yl", "x", "c", "z", "yh"))
    placed = (
        P(DP_TENSOR, None),
        P(DP_TENSOR, None),
        P(DP_TENSOR),
        P(),
        P(DP, TENSOR),
        P(DP, TENSOR),
        P(DP, TENSOR),
    )
    return jax.shard_map(
        body,
        mesh=split,
        in_specs=placed,
        out_specs=(P(DP_TENSOR, None), P(None, TENSOR), P(DP, TENSOR), P(DP, TENSOR)),
        check_vma=False,
    )
```

time: 383 us -> 215 us (0.56)
  the two profiles are of different devices: /device:TPU:25 before, /device:TPU:1 now
where the time goes in v1:
time: 215 us; the launch traced here: 214 us
  blocking collectives  128 us (60%)
  starting transfers between devices  23.1 us (11%)
  Pallas kernels  21.5 us (10%)
  waiting for transfers between devices  17.6 us (8%)
  between operations  14.9 us (7%)
  other arithmetic  4.52 us (2%)
  local copies, waits for them, and re-layouts  4.2 us (2%)
    all_to_all x5, blocking collectives, exchange(): return lax.all_to_all(x, axes, split_axis=0, concat_axis=0, tiled=True)  128 us
    all_to_all x2, waiting for transfers between devices, exchange(): return lax.all_to_all(x, axes, split_axis=0, concat_axis=0, tiled=True)  17.3 us
    pallas_call x1, Pallas kernels, backward(): pl.pallas_call(backward_kernel, grid_spec=pltpu.PrefetchScalarGridSpec(nu...  14.9 us
    all_to_all x2, starting transfers between devices, exchange(): return lax.all_to_all(x, axes, split_axis=0, concat_axis=0, tiled=True)  12.8 us
    ppermute x1, starting transfers between devices, body(): grad_shard = lax.ppermute(piece, ('x', 'c', 'z'), swap)  5.97 us
    pallas_call x1, Pallas kernels, prepare(): pl.pallas_call(prepare_kernel, grid=(tokens // tile,), in_specs=[pl.Block...  4.78 us
  transfers between devices with their start and end apart: 5, of which 3 were waited for; matrix products, arithmetic and copies ran while one was open for 3% of the time, Pallas kernels for 3%

profile of v1, /device:TPU:1, one launch (start us, length us, event | category | flops | bytes accessed | tf_op | source)
XLA Modules:
  0.0 214.1 jit_solution(5280954186288958229)
XLA Ops:
  7.2 0.7 reshape.45
  8.0 14.8 %all_to_all.35 = bf16[8,16,256]{2,1,0:T(8,128)(2,1)} all-to-all(bf16[8,16,256]{2,1,0:T(8,128)(2,1)S(1)} %bitcast.15), channel_id=1, replica_groups=mesh['yl'=4,'x'=4,'c'=2,'z'=8,'yh'=2] {'x','c'}, dimensions={0} | all-to-all | bytes 131072 | tf_op jit(solution)/shard_map/all_to_all | solution.py:37
  22.8 0.7 convert_element_type.13
  23.4 1.3 broadcast_in_dim.25
  25.1 0.8 pad_maximum_fusion
  25.8 4.8 %shard_map.102 = (bf16[8,128,1536]{2,1,0:T(8,128)(2,1)}, bf16[128,512]{1,0:T(8,128)(2,1)}, f32[128,128]{1,0:T(8,128)}) custom-call(bf16[128,8192]{1,0:T(8,128)(2,1)} %x_ref.3, bf16[128,512]{1,0:T(8,128)(2,1)} %key_ref.1, f32[128,128]{1,0:T(8,128)} %get-tuple-element.18.cos_ref, f32[128,128]{1,0:T(8,128)} %get-tuple-element.19.sin_ref, f32[1,8192]{1,0:T(1,128)} %bitcast.13), custom_call_target="tpu_custom_call" | custom-call | flops 8388608 | bytes 6291456 | tf_op jit(solution)/shard_map/pallas_call | solution.py:76
  30.6 42.2 %all_to_all.36.key_ref.normed_ref = bf16[8,128,1536]{2,1,0:T(8,128)(2,1)S(1)} all-to-all(bf16[8,128,1536]{2,1,0:T(8,128)(2,1)} %get-tuple-element.9), channel_id=1, replica_groups=mesh['yl'=4,'x'=4,'c'=2,'z'=8,'yh'=2] {'x','c'}, dimensions={0} | all-to-all | bytes 6291456 | tf_op jit(solution)/shard_map/all_to_all | solution.py:37
  72.8 1.8 shard_map.103
  74.6 50.4 %all_to_all.37 = bf16[64,16,512]{2,1,0:T(8,128)(2,1)S(1)} all-to-all(bf16[64,16,512]{2,1,0:T(8,128)(2,1)S(1)} %bitcast.9), channel_id=1, replica_groups=mesh['yl'=4,'x'=4,'c'=2,'z'=8,'yh'=2] {'yl','z','yh'}, dimensions={0} | all-to-all | bytes 2097152 | tf_op jit(solution)/shard_map/all_to_all | solution.py:37
  125.5 4.2 %collective-permute-start = (bf16[2,4,8,128,256]{4,3,2,1,0:T(8,128)(2,1)}, bf16[2,4,8,128,256]{4,3,2,1,0:T(8,128)(2,1)}, u32[]{:S(2)}, u32[]{:S(2)}) collective-permute-start(bf16[2,4,8,128,256]{4,3,2,1,0:T(8,128)(2,1)} %bitcast.10), channel_id=1, source_target_pairs={{0,16},{16,0},{1,17},{17,1},{2,18},{18,2},{3,19},{19,3},{4,20},{20... | collective-permute-start | bytes 12582920 | tf_op jit(solution)/shard_map/ppermute | solution.py:208
  129.7 0.6 multiply_reduce_fusion
  130.3 0.6 broadcast_in_dim_broadcast_in_dim.3
  131.0 8.5 %all_to_all.38 = f32[8,8,128]{2,1,0:T(8,128)S(1)} all-to-all(f32[8,8,128]{2,1,0:T(8,128)S(1)} %broadcast_in_dim_broadcast_in_dim.3), channel_id=1, replica_groups=mesh['yl'=4,'x'=4,'c'=2,'z'=8,'yh'=2] {'x','c'}, dimensions={0} | all-to-all | bytes 65536 | tf_op jit(solution)/shard_map/all_to_all | solution.py:37
  139.5 12.4 %all_to_all.39 = f32[8,8,128]{2,1,0:T(8,128)S(1)} all-to-all(f32[8,8,128]{2,1,0:T(8,128)S(1)} %broadcast_in_dim.22), channel_id=1, replica_groups=mesh['yl'=4,'x'=4,'c'=2,'z'=8,'yh'=2] {'yh','yl'}, dimensions={0} | all-to-all | bytes 65536 | tf_op jit(solution)/shard_map/all_to_all | solution.py:37
  152.0 0.6 broadcast_in_dim.23
  152.6 4.0 %all-to-all-start.5 = ((f32[8,8,128]{2,1,0:T(8,128)}), f32[8,8,128]{2,1,0:T(8,128)S(1)}, u32[]{:S(2)}, u32[]{:S(2)}) async-start(f32[8,8,128]{2,1,0:T(8,128)} %broadcast_in_dim.23), calls=%async_computation.5 | async-start | bytes 65536 | tf_op jit(solution)/shard_map/all_to_all | solution.py:37
  156.5 6.0 %collective-permute-start.1 = (f32[16,512]{1,0:T(8,128)S(1)}, f32[16,512]{1,0:T(8,128)S(1)}, u32[]{:S(2)}, u32[]{:S(2)}) collective-permute-start(f32[16,512]{1,0:T(8,128)S(1)} %convert_reduce_fusion), channel_id=1, source_target_pairs={{0,0},{2,16},{4,32},{6,48},{8,64},{10,80},{12,96},{14,112},{16,2},... | collective-permute-start | bytes 98312 | tf_op jit(solution)/shard_map/ppermute | solution.py:211
  162.5 0.9 all-to-all-done.5
  164.7 0.6 subtract_convert_fusion
  165.4 0.9 broadcast_in_dim.24
  166.2 8.9 %all-to-all-start.6 = ((bf16[32,16,512]{2,1,0:T(8,128)(2,1)}), bf16[32,16,512]{2,1,0:T(8,128)(2,1)S(1)}, u32[]{:S(2)}, u32[]{:S(2)}) async-start(bf16[32,16,512]{2,1,0:T(8,128)(2,1)} %broadcast_in_dim.24), calls=%async_computation.6 | async-start | bytes 1048576 | tf_op jit(solution)/shard_map/all_to_all | solution.py:37
  175.1 16.4 %all-to-all-done.6 = bf16[32,16,512]{2,1,0:T(8,128)(2,1)S(1)} async-done(((bf16[32,16,512]{2,1,0:T(8,128)(2,1)}), bf16[32,16,512]{2,1,0:T(8,128)(2,1)S(1)}, u32[]{:S(2)}, u32[]{:S(2)}) %all-to-all-start.6) | async-done | bytes 524320 | tf_op jit(solution)/shard_map/all_to_all | solution.py:37
  191.5 14.9 %shard_map.104 = bf16[128,8192]{1,0:T(8,128)(2,1)} custom-call(s32[1]{0:T(128)} %bitcast.core_ref, bf16[128,512]{1,0:T(8,128)(2,1)} %get-tuple-element.8.key_ref, bf16[2,4,8,128,256]{4,3,2,1,0:T(8,128)(2,1)} %bitcast.11, bf16[2,4,8,128,256]{4,3,2,1,0:T(8,128)(2,1)} %collective-permute-done.other_ref, bf16[128,8192]{1,0:T(8,128)(2,1)} %x_ref.3, ...), custom_call_target="tpu_custom_call" | custom-call | flops 1073741824 | bytes 12582912 | tf_op jit(solution)/shard_map/pallas_call | solution.py:164
  206.5 0.8 copy.14
  (21 shorter events, 1.4 us)
Async XLA Ops:
  7.2 118.3 %all-gather.2.cloned.1.call-start = ((), (), s32[]{:S(2)}) async-start(), calls=%async_computation.7 | async-start | bytes 4259840 | tf_op jit(solution)/shard_map/all_gather | solution.py:193
  74.6 90.1 %copy-start = (bf16[16,512]{1,0:T(8,128)(2,1)S(1)}, bf16[16,512]{1,0:T(8,128)(2,1)}, u32[]{:S(2)}) copy-start(bf16[16,512]{1,0:T(8,128)(2,1)} %param.11) | copy-start | bytes 49156
  74.6 90.1 %copy-start.1 = (f32[16,512]{1,0:T(8,128)S(1)}, f32[16,512]{1,0:T(8,128)}, u32[]{:S(2)}) copy-start(f32[16,512]{1,0:T(8,128)} %param.12) | copy-start | bytes 98308
  74.6 90.1 %copy-start.2 = (f32[16,512]{1,0:T(8,128)S(1)}, f32[16,512]{1,0:T(8,128)}, u32[]{:S(2)}) copy-start(f32[16,512]{1,0:T(8,128)} %param.13) | copy-start | bytes 98308
  125.5 66.0 %collective-permute-start = (bf16[2,4,8,128,256]{4,3,2,1,0:T(8,128)(2,1)}, bf16[2,4,8,128,256]{4,3,2,1,0:T(8,128)(2,1)}, u32[]{:S(2)}, u32[]{:S(2)}) collective-permute-start(bf16[2,4,8,128,256]{4,3,2,1,0:T(8,128)(2,1)} %bitcast.10), channel_id=1, source_target_pairs={{0,16},{16,0},{1,17},{17,1},{2,18},{18,2},{3,19},{19,3},{4,20},{20... | collective-permute-start | bytes 12582920 | tf_op jit(solution)/shard_map/ppermute | solution.py:208
  152.6 10.9 %all-to-all-start.5 = ((f32[8,8,128]{2,1,0:T(8,128)}), f32[8,8,128]{2,1,0:T(8,128)S(1)}, u32[]{:S(2)}, u32[]{:S(2)}) async-start(f32[8,8,128]{2,1,0:T(8,128)} %broadcast_in_dim.23), calls=%async_computation.5 | async-start | bytes 65536 | tf_op jit(solution)/shard_map/all_to_all | solution.py:37
  156.5 8.2 %collective-permute-start.1 = (f32[16,512]{1,0:T(8,128)S(1)}, f32[16,512]{1,0:T(8,128)S(1)}, u32[]{:S(2)}, u32[]{:S(2)}) collective-permute-start(f32[16,512]{1,0:T(8,128)S(1)} %convert_reduce_fusion), channel_id=1, source_target_pairs={{0,0},{2,16},{4,32},{6,48},{8,64},{10,80},{12,96},{14,112},{16,2},... | collective-permute-start | bytes 98312 | tf_op jit(solution)/shard_map/ppermute | solution.py:211
  166.2 25.3 %all-to-all-start.6 = ((bf16[32,16,512]{2,1,0:T(8,128)(2,1)}), bf16[32,16,512]{2,1,0:T(8,128)(2,1)S(1)}, u32[]{:S(2)}, u32[]{:S(2)}) async-start(bf16[32,16,512]{2,1,0:T(8,128)(2,1)} %broadcast_in_dim.24), calls=%async_computation.6 | async-start | bytes 1048576 | tf_op jit(solution)/shard_map/all_to_all | solution.py:37
Sparse Core Ops, SparseCore 0:
  22.9 102.5 all-gather.1

commit v2 on v1

--- a/solution.py
+++ b/solution.py
@@ -41,10 +41,6 @@
     return jnp.broadcast_to(x, (count, *x.shape))
 
 
-def sum_over(x, axes, count):
-    return jnp.sum(exchange(copies_for(x, count), axes), axis=0)
-
-
 def rotation(positions):
     half_width = HEAD // 2
     frequency = 500000.0 ** (-(2.0 * jnp.arange(half_width, dtype=f32)) / HEAD)
@@ -58,7 +54,7 @@
     x = x_ref[...].astype(f32)
     scale = lax.rsqrt(jnp.sum(x * x, axis=1, keepdims=True) / D + eps_norm)
     scale_ref[...] = jnp.broadcast_to(scale, scale_ref.shape)
-    normed = (x * scale * gain_ref[...]).astype(bf16)
+    normed = (x * scale * gain_ref[...].astype(f32)).astype(bf16)
     for j in range(N_GROUP):
         send_ref[j, :, :WIDE] = normed[:, j * WIDE : (j + 1) * WIDE]
     for h in range(KV_HEADS):
@@ -130,36 +126,45 @@
     core = core_ref[0]
     tokens = key_ref.shape[0]
     half = own_ref.shape[4]
+    width = 2 * half
+    first = step * own_ref.shape[2] * 2
 
     @pl.when(step == 0)
     def _():
         cross[...] = jnp.zeros_like(cross)
 
-    for side, ref in ((core, own_ref), (1 - core, other_ref)):
-        inside = pl.ds(pl.multiple_of(side * half, half), half)
-        columns = pl.ds(pl.multiple_of(step * 2 * half + side * half, half), half)
-        up = jnp.dot(key_ref[...], ref[...].reshape(KV, half), preferred_element_type=f32)
-        weighted = up * gain_ref[:, inside]
-        held[step, :, inside] = weighted
-        term = jnp.sum(weighted * x_ref[:, columns].astype(f32), axis=1, keepdims=True)
-        cross[...] += jnp.broadcast_to(term, (tokens, HEAD))
+    total = jnp.zeros(cross.shape, f32)
+    for z in range(own_ref.shape[2]):
+        for yh in range(2):
+            block = z * 2 + yh
+            for side, ref in ((core, own_ref), (1 - core, other_ref)):
+                inside = pl.ds(pl.multiple_of(side * half, half), half)
+                columns = pl.ds(pl.multiple_of((first + block) * width + side * half, half), half)
+                local = pl.ds(pl.multiple_of(block * width + side * half, half), half)
+                up = jnp.dot(key_ref[...], ref[yh, :, z].reshape(KV, half), preferred_element_type=f32)
+                weighted = up * gain_ref[:, local].astype(f32)
+                held[first + block, :, inside] = weighted
+                term = weighted * x_ref[:, columns].astype(f32)
+                for k in range(half // HEAD):
+                    total += term[:, k * HEAD : (k + 1) * HEAD]
+    cross[...] += total
 
     @pl.when(step == pl.num_programs(0) - 1)
     def _():
         scale = scale_ref[:, :1]
-        inner = scale * (cross[:, :1] / D)
-        width = 2 * half
+        inner = scale * scale * (jnp.sum(cross[...], axis=1, keepdims=True) / D)
         for t in range(D // width):
             part = slice(t * width, (t + 1) * width)
-            xhat = x_ref[:, part].astype(f32) * scale
-            out_ref[:, part] = (scale * (held[t] - xhat * inner)).astype(bf16)
+            x = x_ref[:, part].astype(f32)
+            out_ref[:, part] = (scale * (held[t] - x * inner)).astype(bf16)
 
 
 def backward(core, keys, own, other, x, scale, gain):
     tokens = x.shape[0]
     width = 512
-    steps = D // width
-    weights = pl.BlockSpec((1, 4, 1, 128, width // 2), lambda t, core: (t % 2, 0, t // 2, 0, 0))
+    deep = 2
+    steps = 8 // deep
+    weights = pl.BlockSpec((2, 4, deep, 128, width // 2), lambda t, core: (0, 0, t, 0, 0))
     whole = lambda a: pl.BlockSpec(a.shape, lambda t, core: (0, 0))
     return pl.pallas_call(
         backward_kernel,
@@ -172,10 +177,10 @@
                 weights,
                 whole(x),
                 whole(scale),
-                pl.BlockSpec((1, width), lambda t, core: (0, t)),
+                pl.BlockSpec((1, 2 * deep * width), lambda t, core: (0, t)),
             ],
             out_specs=pl.BlockSpec((tokens, D), lambda t, core: (0, 0)),
-            scratch_shapes=[pltpu.VMEM((steps, tokens, width), f32), pltpu.VMEM((tokens, HEAD), f32)],
+            scratch_shapes=[pltpu.VMEM((D // width, tokens, width), f32), pltpu.VMEM((tokens, HEAD), f32)],
         ),
         out_shape=jax.ShapeDtypeStruct((tokens, D), bf16),
         compiler_params=pltpu.CompilerParams(vmem_limit_bytes=56 * 1024 * 1024),
@@ -185,49 +190,113 @@
     )(core, keys, own, other, x, scale, gain)
 
 
-def weights_of_core(key_weight):
-    rows, columns = key_weight.shape
-    halves = key_weight.reshape(rows, 2, columns // 2).transpose(1, 0, 2)
-    send = jnp.broadcast_to(halves, (4, *halves.shape)).reshape(N_GROUP, rows, columns // 2)
-    pieces = exchange(send, GROUP).reshape(N_GROUP * rows, columns // 2)
-    whole = lax.all_gather(pieces, ("yh", "yl", "z"), axis=0, tiled=True)
-    return whole.reshape(2, 4, 8, *pieces.shape)
+def local_call(kernel, outs, *args):
+    return pl.pallas_call(
+        kernel,
+        out_shape=[jax.ShapeDtypeStruct(shape, kind) for shape, kind in outs],
+        compiler_params=pltpu.CompilerParams(vmem_limit_bytes=32 * 1024 * 1024),
+    )(*args)
+
+
+def add_pieces_kernel(pieces_ref, piece_ref, square_ref):
+    piece = jnp.sum(pieces_ref[...].astype(f32), axis=0)
+    piece_ref[...] = piece
+    square = jnp.sum(jnp.sum(piece * piece, axis=0, keepdims=True), axis=1, keepdims=True)
+    square_ref[...] = jnp.broadcast_to(square, square_ref.shape)
+
+
+def add_pieces(pieces):
+    return local_call(add_pieces_kernel, [(pieces.shape[1:], f32), ((8, 128), f32)], pieces)
+
+
+def add_pair_kernel(one_ref, two_ref, out_ref):
+    out_ref[...] = jnp.broadcast_to(one_ref[...] + two_ref[...], out_ref.shape)
+
+
+def add_pair(one, two):
+    return local_call(add_pair_kernel, [((8, 8, 128), f32)], one, two)[0]
+
+
+def late_kernel(squares_ref, shard_ref, out_ref):
+    out_ref[:, :, :512] = jnp.broadcast_to(shard_ref[...].astype(bf16), (32, 16, 512))
+    rest = jnp.sum(squares_ref[...], axis=0)
+    lane = lax.broadcasted_iota(jnp.int32, (8, 128), 1)
+    beside = jnp.zeros((8, 128), f32)
+    for k in range(3):
+        term = rest.astype(bf16).astype(f32)
+        rest = rest - term
+        beside = jnp.where(lane == k, term, beside)
+    beside = jnp.concatenate([beside, beside], axis=0).astype(bf16)
+    out_ref[:, :, 512:] = jnp.broadcast_to(beside, (32, 16, 128))
+
+
+def late_rows(squares, shard):
+    return local_call(late_kernel, [((32, 16, 640), bf16)], squares, shard)[0]
+
+
+def update_kernel(gathered_ref, state_ref, shard_ref, first_ref, second_ref, weight_out, first_out, second_out):
+    terms = jnp.sum(gathered_ref[:, :, 512:].astype(f32), axis=0)
+    total_square = jnp.sum(terms[:1], axis=1, keepdims=True)
+    clip_limit = math.sqrt(KV * D)
+    clip_factor = jnp.minimum(1.0, clip_limit / (jnp.sqrt(total_square) + 1e-06))
+
+    def moments(gradient, first, second):
+        clipped = gradient * clip_factor
+        return (
+            beta_one * first + (1.0 - beta_one) * clipped,
+            beta_two * second + (1.0 - beta_two) * clipped * clipped,
+        )
+
+    new_first, new_second = moments(shard_ref[...], first_ref[...], second_ref[...])
+    first_out[...] = new_first
+    second_out[...] = new_second
+    for r in range(32):
+        rows = slice(r * 16, (r + 1) * 16)
+        state = state_ref[rows].astype(f32)
+        new_first, new_second = moments(gathered_ref[r, :, :512].astype(f32), state[:, 512:1024], state[:, 1024:])
+        weight_out[rows] = (
+            state[:, :512] * (1.0 - learn_rate * decay_rate)
+            - learn_rate * new_first / (jnp.sqrt(new_second) + eps_adam)
+        ).astype(bf16)
+
+
+def update(gathered, state, shard, first, second):
+    outs = [((KV, 512), bf16), (first.shape, f32), (second.shape, f32)]
+    return local_call(update_kernel, outs, gathered, state, shard, first, second)
 
 
 def body(norm_input, key_grad, positions, norm_gain, key_weight, first_moment, second_moment):
-    gain = norm_gain.astype(f32)[None, :]
-    core = lax.axis_index("c").astype(jnp.int32).reshape(1)
-    own = weights_of_core(key_weight)
+    gain = norm_gain[None, :]
+    core = lax.axis_index("c")
     cosine, sine = rotation(positions)
     send, keys, scale = prepare(norm_input, key_grad, cosine, sine, gain)
+
+    state = jnp.concatenate([key_weight, first_moment.astype(bf16), second_moment.astype(bf16)], axis=1)
+    state = exchange(copies_for(state, N_GROUP), GROUP).reshape(N_GROUP * 16, 3 * 512)
+    send, state = lax.optimization_barrier((send, state))
+
+    half = lax.dynamic_slice_in_dim(state, core * 256, 256, 1)
+    own = lax.all_gather(half, ("yh", "yl", "z"), axis=0, tiled=True).reshape(2, 4, 8, 128, 256)
+
     received = exchange(send, GROUP)
+    state, received = lax.optimization_barrier((state, received))
+    state = lax.all_gather(state, "yl", axis=0, tiled=True)
+
     partial = product(received).reshape(N_PLANE, 16, 512)
     pieces = exchange(partial, PLANE)
-    piece = jnp.sum(pieces.astype(f32), axis=0)
+    piece, square = add_pieces(pieces)
     own, _ = lax.optimization_barrier((own, piece))
     other = lax.ppermute(own, "c", [(0, 1), (1, 0)])
 
     swap = [(i * 8 + k, k * 8 + i) for i in range(8) for k in range(8)]
     grad_shard = lax.ppermute(piece, ("x", "c", "z"), swap)
-    square = jnp.broadcast_to(jnp.sum(piece * piece), (8, 128))
-    square = sum_over(square, GROUP, 8)
-    square = sum_over(square, ("yh", "yl"), 8)
-    square = sum_over(square, "z", 8)
-    total_square = square[0, 0]
-
-    clip_limit = math.sqrt(KV * D)
-    clip_factor = jnp.minimum(1.0, clip_limit / (jnp.sqrt(total_square) + 1e-06))
-    clipped = grad_shard * clip_factor
-    new_first = beta_one * first_moment + (1.0 - beta_one) * clipped
-    new_second = beta_two * second_moment + (1.0 - beta_two) * clipped * clipped
-    own_rows = key_weight.astype(f32)
-    updated = (
-        own_rows * (1.0 - learn_rate * decay_rate)
-        - learn_rate * new_first / (jnp.sqrt(new_second) + eps_adam)
-    ).astype(bf16)
-    new_weight = exchange(copies_for(updated, 32), DP).reshape(KV, 512)
-
-    input_grad = backward(core, keys, own, other, norm_input, scale, gain)
+    square = add_pair(square, lax.ppermute(square, "yh", [(0, 1), (1, 0)]))
+    late = late_rows(exchange(square, "z"), grad_shard)
+    late, other, own = lax.optimization_barrier((late, other, own))
+    gathered = exchange(late, DP)
+    input_grad = backward(core.astype(jnp.int32).reshape(1), keys, own, other, norm_input, scale, gain)
+    state, input_grad = lax.optimization_barrier((state, input_grad))
+    new_weight, new_first, new_second = update(gathered, state, grad_shard, first_moment, second_moment)
     return (input_grad, new_weight, new_first, new_second)
 
 

time: 215 us -> 206 us (0.958)
  blocking collectives: 128 us -> 91.4 us
  starting transfers between devices: 23.1 us -> 43 us
  waiting for transfers between devices: 17.6 us -> 28.6 us
  Pallas kernels: 21.5 us -> 18.2 us
    all_to_all x5 -> x2, blocking collectives: 128 us -> 91.4 us  [exchange(): return lax.all_to_all(x, axes, split_axis=0, concat_axis=0, tiled=True)]
    all_to_all x2 -> x3, starting transfers between devices: 12.8 us -> 27.7 us  [exchange(): return lax.all_to_all(x, axes, split_axis=0, concat_axis=0, tiled=True)]
    all_gather x1 -> x2, waiting for transfers between devices: 0.25 us -> 10.6 us  [the longest x1 10.6 us: body(): lax.all_gather(half, ('yh', 'yl', 'z'), axis=0, tiled=True)]
    pallas_call x1, Pallas kernels: 14.9 us -> 7.92 us  [backward(): pl.pallas_call(backward_kernel, grid_spec=pltpu.PrefetchScalarGridSpec(nu...]
    ppermute x0 -> x1, starting transfers between devices: none -> 5.81 us  [body(): square = add_pair(square, lax.ppermute(square, 'yh', [(0, 1), (1, 0)]))]
    all_to_all x2 -> x3, waiting for transfers between devices: 17.3 us -> 13.4 us  [exchange(): return lax.all_to_all(x, axes, split_axis=0, concat_axis=0, tiled=True)]
    pallas_call x0 -> x4, Pallas kernels: none -> 3.62 us  [local_call(): pl.pallas_call(kernel, out_shape=[jax.ShapeDtypeStruct(shape, kind) for s...]
    ppermute x0 -> x1, waiting for transfers between devices: none -> 2.48 us  [body(): square = add_pair(square, lax.ppermute(square, 'yh', [(0, 1), (1, 0)]))]
  transfers between devices with their start and end apart: 5 -> 8, of which waited for: 3 -> 5; matrix products, arithmetic and copies ran while one was open for 3% -> 2% of each run, Pallas kernels for 3% -> 8%
where the time goes in v2:
time: 206 us; the launch traced here: 205 us
  blocking collectives  91.4 us (44%)
  starting transfers between devices  43 us (21%)
  waiting for transfers between devices  28.6 us (14%)
  Pallas kernels  18.2 us (9%)
  between operations  15.5 us (8%)
  local copies, waits for them, and re-layouts  4.22 us (2%)
  other arithmetic  3.97 us (2%)
    all_to_all x2, blocking collectives, exchange(): return lax.all_to_all(x, axes, split_axis=0, concat_axis=0, tiled=True)  91.4 us
    all_to_all x3, starting transfers between devices, exchange(): return lax.all_to_all(x, axes, split_axis=0, concat_axis=0, tiled=True)  27.7 us
    all_to_all x3, waiting for transfers between devices, exchange(): return lax.all_to_all(x, axes, split_axis=0, concat_axis=0, tiled=True)  13.4 us
    all_gather x1, waiting for transfers between devices, body(): lax.all_gather(half, ('yh', 'yl', 'z'), axis=0, tiled=True)  10.6 us
    pallas_call x1, Pallas kernels, backward(): pl.pallas_call(backward_kernel, grid_spec=pltpu.PrefetchScalarGridSpec(nu...  7.92 us
    ppermute x1, starting transfers between devices, body(): square = add_pair(square, lax.ppermute(square, 'yh', [(0, 1), (1, 0)]))  5.81 us
    ppermute x1, starting transfers between devices, body(): grad_shard = lax.ppermute(piece, ('x', 'c', 'z'), swap)  4.95 us
    pallas_call x1, Pallas kernels, prepare(): pl.pallas_call(prepare_kernel, grid=(tokens // tile,), in_specs=[pl.Block...  4.84 us
  transfers between devices with their start and end apart: 8, of which 5 were waited for; matrix products, arithmetic and copies ran while one was open for 2% of the time, Pallas kernels for 8%

profile of v2, /device:TPU:1, one launch (start us, length us, event | category | flops | bytes accessed | tf_op | source)
XLA Modules:
  0.0 204.8 jit_solution(11631951790223947665)
XLA Ops:
  8.0 0.8 convert_element_type.10
  8.8 0.8 convert_element_type.11
  9.5 0.7 pad_maximum_fusion.2
  10.2 0.8 broadcast_in_dim.9
  11.0 10.2 %all-to-all-start = ((bf16[8,16,1536]{2,1,0:T(8,128)(2,1)}), bf16[8,16,1536]{2,1,0:T(8,128)(2,1)S(1)}, u32[]{:S(2)}, u32[]{:S(2)}) async-start(bf16[8,16,1536]{2,1,0:T(8,128)(2,1)} %broadcast_in_dim.9), calls=%async_computation | async-start | bytes 786432 | tf_op jit(solution)/shard_map/all_to_all | solution.py:37
  21.9 1.3 broadcast_in_dim.8.gain_ref
  23.6 0.7 pad_maximum_fusion
  24.3 4.8 %shard_map.102 = (bf16[8,128,1536]{2,1,0:T(8,128)(2,1)}, bf16[128,512]{1,0:T(8,128)(2,1)}, f32[128,128]{1,0:T(8,128)}) custom-call(bf16[128,8192]{1,0:T(8,128)(2,1)} %x_ref.3, bf16[128,512]{1,0:T(8,128)(2,1)} %key_ref.1, f32[128,128]{1,0:T(8,128)} %get-tuple-element.43.cos_ref, f32[128,128]{1,0:T(8,128)} %get-tuple-element.44.sin_ref, ...), custom_call_target="tpu_custom_call" | custom-call | flops 8388608 | bytes 6291456 | tf_op jit(solution)/shard_map/pallas_call | solution.py:72
  30.1 42.6 %all_to_all.25.key_ref.normed_ref = bf16[8,128,1536]{2,1,0:T(8,128)(2,1)S(1)} all-to-all(bf16[8,128,1536]{2,1,0:T(8,128)(2,1)} %get-tuple-element.24), channel_id=1, replica_groups=mesh['yl'=4,'x'=4,'c'=2,'z'=8,'yh'=2] {'x','c'}, dimensions={0} | all-to-all | bytes 6291456 | tf_op jit(solution)/shard_map/all_to_all | solution.py:37
  72.7 1.8 shard_map.103
  74.5 48.8 %all_to_all.26.pieces_ref = bf16[64,16,512]{2,1,0:T(8,128)(2,1)S(1)} all-to-all(bf16[64,16,512]{2,1,0:T(8,128)(2,1)S(1)} %bitcast.4), channel_id=1, replica_groups=mesh['yl'=4,'x'=4,'c'=2,'z'=8,'yh'=2] {'yl','z','yh'}, dimensions={0} | all-to-all | bytes 2097152 | tf_op jit(solution)/shard_map/all_to_all | solution.py:37
  123.5 10.6 %all-gather.5.cloned.1.call-done = bf16[8192,256]{1,0:T(8,128)(2,1)} async-done(((bf16[128,256]{1,0:T(8,128)(2,1)}), bf16[8192,256]{1,0:T(8,128)(2,1)}) %all-gather.5.cloned.1.call-update) | async-done | bytes 4194320 | tf_op jit(solution)/shard_map/all_gather | solution.py:279
  134.1 4.5 %collective-permute-start.2 = (bf16[2,4,8,128,256]{4,3,2,1,0:T(8,128)(2,1)}, bf16[2,4,8,128,256]{4,3,2,1,0:T(8,128)(2,1)}, u32[]{:S(2)}, u32[]{:S(2)}) collective-permute-start(bf16[2,4,8,128,256]{4,3,2,1,0:T(8,128)(2,1)} %bitcast.5), channel_id=1, source_target_pairs={{0,16},{16,0},{1,17},{17,1},{2,18},{18,2},{3,19},{19,3},{4,20},{20... | collective-permute-start | bytes 12582920 | tf_op jit(solution)/shard_map/ppermute | solution.py:289
  138.7 5.8 %collective-permute-start = (f32[8,128]{1,0:T(8,128)S(1)}, f32[8,128]{1,0:T(8,128)S(1)}, u32[]{:S(2)}, u32[]{:S(2)}) collective-permute-start(f32[8,128]{1,0:T(8,128)S(1)} %get-tuple-element.28.one_ref), channel_id=1, source_target_pairs={{0,1},{1,0},{2,3},{3,2},{4,5},{5,4},{6,7},{7,6},{8,9},{9,8},{10,11... | collective-permute-start | bytes 12296 | tf_op jit(solution)/shard_map/ppermute | solution.py:293
  144.5 2.5 %collective-permute-done.two_ref = f32[8,128]{1,0:T(8,128)S(1)} collective-permute-done((f32[8,128]{1,0:T(8,128)S(1)}, f32[8,128]{1,0:T(8,128)S(1)}, u32[]{:S(2)}, u32[]{:S(2)}) %collective-permute-start) | collective-permute-done | bytes 4128 | tf_op jit(solution)/shard_map/ppermute | solution.py:293
  147.6 5.2 %all-to-all-start.3 = ((f32[8,8,128]{2,1,0:T(8,128)}), f32[8,8,128]{2,1,0:T(8,128)S(1)}, u32[]{:S(2)}, u32[]{:S(2)}) async-start(f32[8,8,128]{2,1,0:T(8,128)} %shard_map.105), calls=%async_computation.3 | async-start | bytes 65536 | tf_op jit(solution)/shard_map/all_to_all | solution.py:37
  152.8 5.0 %collective-permute-start.1 = (f32[16,512]{1,0:T(8,128)S(1)}, f32[16,512]{1,0:T(8,128)S(1)}, u32[]{:S(2)}, u32[]{:S(2)}) collective-permute-start(f32[16,512]{1,0:T(8,128)S(1)} %get-tuple-element.29), channel_id=1, source_target_pairs={{0,0},{2,16},{4,32},{6,48},{8,64},{10,80},{12,96},{14,112},{16,2},... | collective-permute-start | bytes 98312 | tf_op jit(solution)/shard_map/ppermute | solution.py:292
  157.7 2.1 %collective-permute-done.1.shard_ref = f32[16,512]{1,0:T(8,128)S(1)} collective-permute-done((f32[16,512]{1,0:T(8,128)S(1)}, f32[16,512]{1,0:T(8,128)S(1)}, u32[]{:S(2)}, u32[]{:S(2)}) %collective-permute-start.1) | collective-permute-done | bytes 32800 | tf_op jit(solution)/shard_map/ppermute | solution.py:292
  159.8 0.9 shard_map.106
  160.8 12.3 %all-to-all-start.4 = ((bf16[32,16,640]{2,1,0:T(8,128)(2,1)}), bf16[32,16,640]{2,1,0:T(8,128)(2,1)S(1)}, u32[]{:S(2)}, u32[]{:S(2)}) async-start(bf16[32,16,640]{2,1,0:T(8,128)(2,1)} %shard_map.106), calls=%async_computation.4 | async-start | bytes 1310720 | tf_op jit(solution)/shard_map/all_to_all | solution.py:37
  173.0 7.9 %shard_map.107 = bf16[128,8192]{1,0:T(8,128)(2,1)} custom-call(s32[1]{0:T(128)} %bitcast.1.core_ref, bf16[128,512]{1,0:T(8,128)(2,1)} %get-tuple-element.26.key_ref, bf16[2,4,8,128,256]{4,3,2,1,0:T(8,128)(2,1)} %bitcast.6, bf16[2,4,8,128,256]{4,3,2,1,0:T(8,128)(2,1)} %collective-permute-done.2.other_ref, bf16[128,8192]{1,0:T(8,128)(2,1)} %x_ref.3, ...), custom_call_target="tpu_custom_call" | custom-call | flops 1073741824 | bytes 12582912 | tf_op jit(solution)/shard_map/pallas_call | solution.py:169
  181.0 13.2 %all-to-all-done.4.gathered_ref = bf16[32,16,640]{2,1,0:T(8,128)(2,1)S(1)} async-done(((bf16[32,16,640]{2,1,0:T(8,128)(2,1)}), bf16[32,16,640]{2,1,0:T(8,128)(2,1)S(1)}, u32[]{:S(2)}, u32[]{:S(2)}) %all-to-all-start.4) | async-done | bytes 655392 | tf_op jit(solution)/shard_map/all_to_all | solution.py:37
  194.2 1.4 copy-done
  195.6 1.8 shard_map.108
  (21 shorter events, 2.8 us)
Async XLA Ops:
  11.0 18.3 %all-to-all-start = ((bf16[8,16,1536]{2,1,0:T(8,128)(2,1)}), bf16[8,16,1536]{2,1,0:T(8,128)(2,1)S(1)}, u32[]{:S(2)}, u32[]{:S(2)}) async-start(bf16[8,16,1536]{2,1,0:T(8,128)(2,1)} %broadcast_in_dim.9), calls=%async_computation | async-start | bytes 786432 | tf_op jit(solution)/shard_map/all_to_all | solution.py:37
  21.2 112.8 %all-gather.5.cloned.1.call-start = ((), (), s32[]{:S(2)}) async-start(), calls=%async_computation.6 | async-start | bytes 4259840 | tf_op jit(solution)/shard_map/all_gather | solution.py:279
  29.3 43.4 %copy-start.3 = (bf16[8,16,1536]{2,1,0:T(8,128)(2,1)}, bf16[8,16,1536]{2,1,0:T(8,128)(2,1)S(1)}, u32[]{:S(2)}) copy-start(bf16[8,16,1536]{2,1,0:T(8,128)(2,1)S(1)} %all-to-all-done) | copy-start | bytes 1179652
  30.0 150.9 %all-gather.3.cloned.1.call-start = ((), (), s32[]{:S(2)}) async-start(), calls=%async_computation.5 | async-start | bytes 1966080 | tf_op jit(solution)/shard_map/all_gather | solution.py:283
  134.1 26.7 %collective-permute-start.2 = (bf16[2,4,8,128,256]{4,3,2,1,0:T(8,128)(2,1)}, bf16[2,4,8,128,256]{4,3,2,1,0:T(8,128)(2,1)}, u32[]{:S(2)}, u32[]{:S(2)}) collective-permute-start(bf16[2,4,8,128,256]{4,3,2,1,0:T(8,128)(2,1)} %bitcast.5), channel_id=1, source_target_pairs={{0,16},{16,0},{1,17},{17,1},{2,18},{18,2},{3,19},{19,3},{4,20},{20... | collective-permute-start | bytes 12582920 | tf_op jit(solution)/shard_map/ppermute | solution.py:289
  138.7 8.3 %collective-permute-start = (f32[8,128]{1,0:T(8,128)S(1)}, f32[8,128]{1,0:T(8,128)S(1)}, u32[]{:S(2)}, u32[]{:S(2)}) collective-permute-start(f32[8,128]{1,0:T(8,128)S(1)} %get-tuple-element.28.one_ref), channel_id=1, source_target_pairs={{0,1},{1,0},{2,3},{3,2},{4,5},{5,4},{6,7},{7,6},{8,9},{9,8},{10,11... | collective-permute-start | bytes 12296 | tf_op jit(solution)/shard_map/ppermute | solution.py:293
  147.6 12.2 %all-to-all-start.3 = ((f32[8,8,128]{2,1,0:T(8,128)}), f32[8,8,128]{2,1,0:T(8,128)S(1)}, u32[]{:S(2)}, u32[]{:S(2)}) async-start(f32[8,8,128]{2,1,0:T(8,128)} %shard_map.105), calls=%async_computation.3 | async-start | bytes 65536 | tf_op jit(solution)/shard_map/all_to_all | solution.py:37
  152.8 7.0 %collective-permute-start.1 = (f32[16,512]{1,0:T(8,128)S(1)}, f32[16,512]{1,0:T(8,128)S(1)}, u32[]{:S(2)}, u32[]{:S(2)}) collective-permute-start(f32[16,512]{1,0:T(8,128)S(1)} %get-tuple-element.29), channel_id=1, source_target_pairs={{0,0},{2,16},{4,32},{6,48},{8,64},{10,80},{12,96},{14,112},{16,2},... | collective-permute-start | bytes 98312 | tf_op jit(solution)/shard_map/ppermute | solution.py:292
  160.8 33.5 %all-to-all-start.4 = ((bf16[32,16,640]{2,1,0:T(8,128)(2,1)}), bf16[32,16,640]{2,1,0:T(8,128)(2,1)S(1)}, u32[]{:S(2)}, u32[]{:S(2)}) async-start(bf16[32,16,640]{2,1,0:T(8,128)(2,1)} %shard_map.106), calls=%async_computation.4 | async-start | bytes 1310720 | tf_op jit(solution)/shard_map/all_to_all | solution.py:37
  173.0 21.2 %copy-start.1 = (f32[16,512]{1,0:T(8,128)S(1)}, f32[16,512]{1,0:T(8,128)}, u32[]{:S(2)}) copy-start(f32[16,512]{1,0:T(8,128)} %second_ref.1) | copy-start | bytes 98308
  173.0 21.2 %copy-start.2 = (f32[16,512]{1,0:T(8,128)S(1)}, f32[16,512]{1,0:T(8,128)}, u32[]{:S(2)}) copy-start(f32[16,512]{1,0:T(8,128)} %first_ref.1) | copy-start | bytes 98308
  194.2 1.4 copy-start
Sparse Core Ops, SparseCore 0:
  30.2 103.8 all-gather.4
Sparse Core Ops, SparseCore 1:
  138.7 41.0 all-gather.2

commit v3 on v2

--- a/solution.py
+++ b/solution.py
@@ -47,19 +47,24 @@
     angles = positions.astype(f32)[:, None] * frequency[None, :]
     cosine = jnp.cos(angles)
     sine = jnp.sin(angles)
-    return jnp.concatenate([cosine, cosine], axis=1), jnp.concatenate([sine, -sine], axis=1)
-
-
-def prepare_kernel(x_ref, key_ref, cos_ref, sin_ref, gain_ref, send_ref, key_out_ref, scale_ref):
+    return cosine, sine
+
+
+def prepare_kernel(x_ref, key_ref, cos_ref, sin_ref, gain_ref, send_ref, key_out_ref, scale_ref, gain_out_ref):
     x = x_ref[...].astype(f32)
     scale = lax.rsqrt(jnp.sum(x * x, axis=1, keepdims=True) / D + eps_norm)
     scale_ref[...] = jnp.broadcast_to(scale, scale_ref.shape)
-    normed = (x * scale * gain_ref[...].astype(f32)).astype(bf16)
-    for j in range(N_GROUP):
-        send_ref[j, :, :WIDE] = normed[:, j * WIDE : (j + 1) * WIDE]
+    gain = gain_ref[...].astype(f32)
+    gain_out_ref[...] = gain
+    for k in range(D // HEAD):
+        j, at = divmod(k * HEAD, WIDE)
+        part = x_ref[:, k * HEAD : (k + 1) * HEAD].astype(f32)
+        send_ref[j, :, at : at + HEAD] = (part * scale * gain[k : k + 1]).astype(bf16)
+    cosine = jnp.concatenate([cos_ref[...], cos_ref[...]], axis=1)
+    sine = jnp.concatenate([sin_ref[...], -sin_ref[...]], axis=1)
     for h in range(KV_HEADS):
         part = key_ref[:, h * HEAD : (h + 1) * HEAD].astype(f32)
-        turned = part * cos_ref[...] + pltpu.roll(part, HEAD // 2, 1) * sin_ref[...]
+        turned = part * cosine + pltpu.roll(part, HEAD // 2, 1) * sine
         turned = turned.astype(bf16)
         key_out_ref[:, h * HEAD : (h + 1) * HEAD] = turned
         for j in range(N_GROUP):
@@ -75,19 +80,21 @@
         in_specs=[
             pl.BlockSpec((tile, D), lambda i: (i, 0)),
             pl.BlockSpec((tile, KV), lambda i: (i, 0)),
-            pl.BlockSpec((tile, HEAD), lambda i: (i, 0)),
-            pl.BlockSpec((tile, HEAD), lambda i: (i, 0)),
-            pl.BlockSpec((1, D), lambda i: (0, 0)),
+            pl.BlockSpec((tile, HEAD // 2), lambda i: (i, 0)),
+            pl.BlockSpec((tile, HEAD // 2), lambda i: (i, 0)),
+            pl.BlockSpec(gain.shape, lambda i: (0, 0)),
         ],
         out_specs=[
             pl.BlockSpec((N_GROUP, tile, COLS), lambda i: (0, i, 0)),
             pl.BlockSpec((tile, KV), lambda i: (i, 0)),
             pl.BlockSpec((tile, HEAD), lambda i: (i, 0)),
+            pl.BlockSpec(gain.shape, lambda i: (0, 0)),
         ],
         out_shape=[
             jax.ShapeDtypeStruct((N_GROUP, tokens, COLS), bf16),
             jax.ShapeDtypeStruct((tokens, KV), bf16),
             jax.ShapeDtypeStruct((tokens, HEAD), f32),
+            jax.ShapeDtypeStruct(gain.shape, f32),
         ],
         compiler_params=pltpu.CompilerParams(vmem_limit_bytes=56 * 1024 * 1024),
         cost_estimate=pl.CostEstimate(flops=8 * tokens * D, bytes_accessed=6 * 1024 * 1024, transcendentals=0),
@@ -121,10 +128,11 @@
     )(received, received)
 
 
-def backward_kernel(core_ref, key_ref, own_ref, other_ref, x_ref, scale_ref, gain_ref, out_ref, held, cross):
+def backward_kernel(
+    core_ref, key_ref, own_ref, other_ref, x_ref, scale_ref, gain_ref, out_ref, held, cross
+):
     step = pl.program_id(0)
     core = core_ref[0]
-    tokens = key_ref.shape[0]
     half = own_ref.shape[4]
     width = 2 * half
     first = step * own_ref.shape[2] * 2
@@ -136,17 +144,16 @@
     total = jnp.zeros(cross.shape, f32)
     for z in range(own_ref.shape[2]):
         for yh in range(2):
-            block = z * 2 + yh
+            block = first + z * 2 + yh
             for side, ref in ((core, own_ref), (1 - core, other_ref)):
-                inside = pl.ds(pl.multiple_of(side * half, half), half)
-                columns = pl.ds(pl.multiple_of((first + block) * width + side * half, half), half)
-                local = pl.ds(pl.multiple_of(block * width + side * half, half), half)
                 up = jnp.dot(key_ref[...], ref[yh, :, z].reshape(KV, half), preferred_element_type=f32)
-                weighted = up * gain_ref[:, local].astype(f32)
-                held[first + block, :, inside] = weighted
-                term = weighted * x_ref[:, columns].astype(f32)
                 for k in range(half // HEAD):
-                    total += term[:, k * HEAD : (k + 1) * HEAD]
+                    group = block * (width // HEAD) + side * (half // HEAD) + k
+                    columns = pl.ds(pl.multiple_of(group * HEAD, HEAD), HEAD)
+                    inside = pl.ds(pl.multiple_of(side * half + k * HEAD, HEAD), HEAD)
+                    weighted = up[:, k * HEAD : (k + 1) * HEAD] * gain_ref[pl.ds(group, 1), :]
+                    held[block, :, inside] = weighted
+                    total += weighted * x_ref[:, columns].astype(f32)
     cross[...] += total
 
     @pl.when(step == pl.num_programs(0) - 1)
@@ -171,14 +178,7 @@
         grid_spec=pltpu.PrefetchScalarGridSpec(
             num_scalar_prefetch=1,
             grid=(steps,),
-            in_specs=[
-                whole(keys),
-                weights,
-                weights,
-                whole(x),
-                whole(scale),
-                pl.BlockSpec((1, 2 * deep * width), lambda t, core: (0, t)),
-            ],
+            in_specs=[whole(keys), weights, weights, whole(x), whole(scale), whole(gain)],
             out_specs=pl.BlockSpec((tokens, D), lambda t, core: (0, 0)),
             scratch_shapes=[pltpu.VMEM((D // width, tokens, width), f32), pltpu.VMEM((tokens, HEAD), f32)],
         ),
@@ -234,7 +234,10 @@
     return local_call(late_kernel, [((32, 16, 640), bf16)], squares, shard)[0]
 
 
-def update_kernel(gathered_ref, state_ref, shard_ref, first_ref, second_ref, weight_out, first_out, second_out):
+def update_kernel(
+    place_ref, gathered_ref, own_ref, other_ref, m0_ref, m1_ref, m2_ref, m3_ref, shard_ref, first_ref, second_ref,
+    weight_out, first_out, second_out,
+):
     terms = jnp.sum(gathered_ref[:, :, 512:].astype(f32), axis=0)
     total_square = jnp.sum(terms[:1], axis=1, keepdims=True)
     clip_limit = math.sqrt(KV * D)
@@ -250,53 +253,76 @@
     new_first, new_second = moments(shard_ref[...], first_ref[...], second_ref[...])
     first_out[...] = new_first
     second_out[...] = new_second
-    for r in range(32):
-        rows = slice(r * 16, (r + 1) * 16)
-        state = state_ref[rows].astype(f32)
-        new_first, new_second = moments(gathered_ref[r, :, :512].astype(f32), state[:, 512:1024], state[:, 1024:])
-        weight_out[rows] = (
-            state[:, :512] * (1.0 - learn_rate * decay_rate)
-            - learn_rate * new_first / (jnp.sqrt(new_second) + eps_adam)
-        ).astype(bf16)
-
-
-def update(gathered, state, shard, first, second):
-    outs = [((KV, 512), bf16), (first.shape, f32), (second.shape, f32)]
-    return local_call(update_kernel, outs, gathered, state, shard, first, second)
+    core, yl = place_ref[0], place_ref[1]
+    half = own_ref.shape[1]
+    for k, ref in enumerate((m0_ref, m1_ref, m2_ref, m3_ref)):
+        block = yl ^ k
+        for r in range(8):
+            part = slice(r * 16, (r + 1) * 16)
+            rows = pl.ds(pl.multiple_of(block * 128 + r * 16, 16), 16)
+            gradient = gathered_ref[block * 8 + r, :, :512].astype(f32)
+            new_first, new_second = moments(gradient, ref[part, :512].astype(f32), ref[part, 512:].astype(f32))
+            step = learn_rate * new_first / (jnp.sqrt(new_second) + eps_adam)
+            own = own_ref[rows, :].astype(f32)
+            other = other_ref[rows, :].astype(f32)
+            for side in range(2):
+                inside = slice(side * half, (side + 1) * half)
+                weight = jnp.where(core == side, own, other)
+                weight_out[rows, inside] = (weight * (1.0 - learn_rate * decay_rate) - step[:, inside]).astype(bf16)
+
+
+def update(place, *args):
+    shard = args[-1]
+    return pl.pallas_call(
+        update_kernel,
+        in_specs=[pl.BlockSpec(memory_space=pltpu.SMEM)] + [pl.BlockSpec(memory_space=pltpu.VMEM)] * len(args),
+        out_specs=[pl.BlockSpec(memory_space=pltpu.VMEM)] * 3,
+        out_shape=[jax.ShapeDtypeStruct(s, k) for s, k in (((KV, 512), bf16), (shard.shape, f32), (shard.shape, f32))],
+        compiler_params=pltpu.CompilerParams(vmem_limit_bytes=32 * 1024 * 1024),
+    )(place, *args)
+
+
+def state_kernel(weight_ref, first_ref, second_ref, out_ref):
+    out_ref[:, :, :512] = jnp.broadcast_to(weight_ref[...], (N_GROUP, 16, 512))
+    out_ref[:, :, 512:1024] = jnp.broadcast_to(first_ref[...].astype(bf16), (N_GROUP, 16, 512))
+    out_ref[:, :, 1024:] = jnp.broadcast_to(second_ref[...].astype(bf16), (N_GROUP, 16, 512))
 
 
 def body(norm_input, key_grad, positions, norm_gain, key_weight, first_moment, second_moment):
-    gain = norm_gain[None, :]
     core = lax.axis_index("c")
+    state = local_call(state_kernel, [((N_GROUP, 16, 1536), bf16)], key_weight, first_moment, second_moment)[0]
+    state = exchange(state, GROUP).reshape(N_GROUP * 16, 1536)
     cosine, sine = rotation(positions)
-    send, keys, scale = prepare(norm_input, key_grad, cosine, sine, gain)
-
-    state = jnp.concatenate([key_weight, first_moment.astype(bf16), second_moment.astype(bf16)], axis=1)
-    state = exchange(copies_for(state, N_GROUP), GROUP).reshape(N_GROUP * 16, 3 * 512)
+    send, keys, scale, gain = prepare(norm_input, key_grad, cosine, sine, norm_gain.reshape(D // HEAD, HEAD))
     send, state = lax.optimization_barrier((send, state))
 
     half = lax.dynamic_slice_in_dim(state, core * 256, 256, 1)
     own = lax.all_gather(half, ("yh", "yl", "z"), axis=0, tiled=True).reshape(2, 4, 8, 128, 256)
 
     received = exchange(send, GROUP)
-    state, received = lax.optimization_barrier((state, received))
-    state = lax.all_gather(state, "yl", axis=0, tiled=True)
-
+    moments = [state[:, 512:]]
+    moments += [lax.ppermute(moments[0], "yl", [(i, i ^ k) for i in range(4)]) for k in (1, 2, 3)]
+    received, *moments = lax.optimization_barrier((received, *moments))
     partial = product(received).reshape(N_PLANE, 16, 512)
     pieces = exchange(partial, PLANE)
     piece, square = add_pieces(pieces)
-    own, _ = lax.optimization_barrier((own, piece))
-    other = lax.ppermute(own, "c", [(0, 1), (1, 0)])
 
     swap = [(i * 8 + k, k * 8 + i) for i in range(8) for k in range(8)]
     grad_shard = lax.ppermute(piece, ("x", "c", "z"), swap)
     square = add_pair(square, lax.ppermute(square, "yh", [(0, 1), (1, 0)]))
+    own, _ = lax.optimization_barrier((own, square))
+    other = lax.ppermute(own, "c", [(0, 1), (1, 0)])
     late = late_rows(exchange(square, "z"), grad_shard)
-    late, other, own = lax.optimization_barrier((late, other, own))
+    late, own, other = lax.optimization_barrier((late, own, other))
     gathered = exchange(late, DP)
     input_grad = backward(core.astype(jnp.int32).reshape(1), keys, own, other, norm_input, scale, gain)
-    state, input_grad = lax.optimization_barrier((state, input_grad))
-    new_weight, new_first, new_second = update(gathered, state, grad_shard, first_moment, second_moment)
+    own, other, input_grad = lax.optimization_barrier((own, other, input_grad))
+    z, yh = lax.axis_index("z"), lax.axis_index("yh")
+    weights = [lax.dynamic_slice(w, (yh, 0, z, 0, 0), (1, 4, 1, 128, 256)).reshape(KV, 256) for w in (own, other)]
+    place = jnp.stack([core, lax.axis_index("yl")]).astype(jnp.int32)
+    new_weight, new_first, new_second = update(
+        place, gathered, *weights, *moments, grad_shard, first_moment, second_moment
+    )
     return (input_grad, new_weight, new_first, new_second)
 
 

time: 206 us -> 192 us (0.932)
  blocking collectives: 91.4 us -> 47 us
  waiting for transfers between devices: 28.6 us -> 46.9 us
  starting transfers between devices: 43 us -> 54.2 us
  local copies, waits for them, and re-layouts: 4.22 us -> 7.12 us
  other arithmetic: 3.97 us -> 1.71 us
    all_to_all x2 -> x1, blocking collectives: 91.4 us -> 47 us  [exchange(): return lax.all_to_all(x, axes, split_axis=0, concat_axis=0, tiled=True)]
    ppermute x0 -> x3, waiting for transfers between devices: none -> 14.4 us  [body(): lax.ppermute(moments[0], 'yl', [(i, i ^ k) for i in range(4)])]
    all_to_all x3 -> x4, waiting for transfers between devices: 13.4 us -> 23.3 us  [exchange(): return lax.all_to_all(x, axes, split_axis=0, concat_axis=0, tiled=True)]
    ppermute x0 -> x3, starting transfers between devices: none -> 9.3 us  [body(): lax.ppermute(moments[0], 'yl', [(i, i ^ k) for i in range(4)])]
    all_gather x1, waiting for transfers between devices: 10.6 us -> 4.84 us  [body(): lax.all_gather(half, ('yh', 'yl', 'z'), axis=0, tiled=True)]
    unnamed x8 -> x24, local copies, waits for them, and re-layouts: 1.43 us -> 4.42 us
    all_to_all x3 -> x4, starting transfers between devices: 27.7 us -> 30.5 us  [exchange(): return lax.all_to_all(x, axes, split_axis=0, concat_axis=0, tiled=True)]
    pallas_call x0 -> x1, Pallas kernels: none -> 2.35 us  [update(): pl.pallas_call(update_kernel, in_specs=[pl.BlockSpec(memory_space=pltpu.S...]
  transfers between devices with their start and end apart: 8 -> 11, of which waited for: 5 -> 9; matrix products, arithmetic and copies ran while one was open for 2% -> 2% of each run, Pallas kernels for 8% -> 9%
where the time goes in v3:
time: 192 us; the launch traced here: 191 us
  starting transfers between devices  54.2 us (28%)
  blocking collectives  47 us (24%)
  waiting for transfers between devices  46.9 us (24%)
  Pallas kernels  19.5 us (10%)
  between operations  14.2 us (7%)
  local copies, waits for them, and re-layouts  7.12 us (4%)
    all_to_all x1, blocking collectives, exchange(): return lax.all_to_all(x, axes, split_axis=0, concat_axis=0, tiled=True)  47 us
    all_to_all x4, starting transfers between devices, exchange(): return lax.all_to_all(x, axes, split_axis=0, concat_axis=0, tiled=True)  30.5 us
    all_to_all x4, waiting for transfers between devices, exchange(): return lax.all_to_all(x, axes, split_axis=0, concat_axis=0, tiled=True)  23.3 us
    ppermute x3, waiting for transfers between devices, body(): lax.ppermute(moments[0], 'yl', [(i, i ^ k) for i in range(4)])  14.4 us
    ppermute x3, starting transfers between devices, body(): lax.ppermute(moments[0], 'yl', [(i, i ^ k) for i in range(4)])  9.3 us
    pallas_call x1, Pallas kernels, backward(): pl.pallas_call(backward_kernel, grid_spec=pltpu.PrefetchScalarGridSpec(nu...  8.04 us
    ppermute x1, starting transfers between devices, body(): square = add_pair(square, lax.ppermute(square, 'yh', [(0, 1), (1, 0)]))  5.93 us
    all_gather x1, waiting for transfers between devices, body(): lax.all_gather(half, ('yh', 'yl', 'z'), axis=0, tiled=True)  4.84 us
  transfers between devices with their start and end apart: 11, of which 9 were waited for; matrix products, arithmetic and copies ran while one was open for 2% of the time, Pallas kernels for 9%

profile of v3, /device:TPU:1, one launch (start us, length us, event | category | flops | bytes accessed | tf_op | source)
XLA Modules:
  0.0 190.6 jit_solution(1749070732071615007)
XLA Ops:
  10.2 10.2 %all-to-all-start = ((bf16[8,16,1536]{2,1,0:T(8,128)(2,1)}), bf16[8,16,1536]{2,1,0:T(8,128)(2,1)S(1)}, u32[]{:S(2)}, u32[]{:S(2)}) async-start(bf16[8,16,1536]{2,1,0:T(8,128)(2,1)} %shard_map.103), calls=%async_computation | async-start | bytes 786432 | tf_op jit(solution)/shard_map/all_to_all | solution.py:37
  22.1 4.7 %shard_map.102 = (bf16[8,128,1536]{2,1,0:T(8,128)(2,1)}, bf16[128,512]{1,0:T(8,128)(2,1)}, f32[128,128]{1,0:T(8,128)}, f32[64,128]{1,0:T(8,128)}) custom-call(bf16[128,8192]{1,0:T(8,128)(2,1)} %x_ref.3, bf16[128,512]{1,0:T(8,128)(2,1)} %key_ref.1, f32[128,64]{1,0:T(8,128)} %get-tuple-element.51.cos_ref, f32[128,64]{1,0:T(8,128)} %get-tuple-element.50.sin_ref, ...), custom_call_target="tpu_custom_call" | custom-call | flops 8388608 | bytes 6291456 | tf_op jit(solution)/shard_map/pallas_call | solution.py:77
  26.8 1.7 all-to-all-done
  29.3 4.4 %all-to-all-start.1 = ((bf16[8,128,1536]{2,1,0:T(8,128)(2,1)}), bf16[8,128,1536]{2,1,0:T(8,128)(2,1)S(1)}, u32[]{:S(2)}, u32[]{:S(2)}) async-start(bf16[8,128,1536]{2,1,0:T(8,128)(2,1)} %get-tuple-element.28), calls=%async_computation.1 | async-start | bytes 6291456 | tf_op jit(solution)/shard_map/all_to_all | solution.py:37
  34.7 1.9 %collective-permute-start.2 = (bf16[128,1024]{1,0:T(8,128)(2,1)S(1)}, bf16[128,1024]{1,0:T(8,128)(2,1)S(1)}, u32[]{:S(2)}, u32[]{:S(2)}) collective-permute-start(bf16[128,1024]{1,0:T(8,128)(2,1)S(1)} %slice.3.m0_ref), channel_id=1, source_target_pairs={{0,384},{128,256},{256,128},{384,0},{1,385},{129,257},{257,129},{3... | collective-permute-start | bytes 786440 | tf_op jit(solution)/shard_map/ppermute | solution.py:304
  36.6 1.9 %collective-permute-start.1 = (bf16[128,1024]{1,0:T(8,128)(2,1)S(1)}, bf16[128,1024]{1,0:T(8,128)(2,1)S(1)}, u32[]{:S(2)}, u32[]{:S(2)}) collective-permute-start(bf16[128,1024]{1,0:T(8,128)(2,1)S(1)} %slice.3.m0_ref), channel_id=1, source_target_pairs={{0,256},{128,384},{256,0},{384,128},{1,257},{129,385},{257,1},{385... | collective-permute-start | bytes 786440 | tf_op jit(solution)/shard_map/ppermute | solution.py:304
  38.5 5.5 %collective-permute-start = (bf16[128,1024]{1,0:T(8,128)(2,1)S(1)}, bf16[128,1024]{1,0:T(8,128)(2,1)S(1)}, u32[]{:S(2)}, u32[]{:S(2)}) collective-permute-start(bf16[128,1024]{1,0:T(8,128)(2,1)S(1)} %slice.3.m0_ref), channel_id=1, source_target_pairs={{0,128},{128,0},{256,384},{384,256},{1,129},{129,1},{257,385},{385... | collective-permute-start | bytes 786440 | tf_op jit(solution)/shard_map/ppermute | solution.py:304
  44.0 2.3 %collective-permute-done.2.m3_ref = bf16[128,1024]{1,0:T(8,128)(2,1)S(1)} collective-permute-done((bf16[128,1024]{1,0:T(8,128)(2,1)S(1)}, bf16[128,1024]{1,0:T(8,128)(2,1)S(1)}, u32[]{:S(2)}, u32[]{:S(2)}) %collective-permute-start.2) | collective-permute-done | bytes 262176 | tf_op jit(solution)/shard_map/ppermute | solution.py:304
  47.0 12.1 %collective-permute-done.1.m2_ref = bf16[128,1024]{1,0:T(8,128)(2,1)S(1)} collective-permute-done((bf16[128,1024]{1,0:T(8,128)(2,1)S(1)}, bf16[128,1024]{1,0:T(8,128)(2,1)S(1)}, u32[]{:S(2)}, u32[]{:S(2)}) %collective-permute-start.1) | collective-permute-done | bytes 262176 | tf_op jit(solution)/shard_map/ppermute | solution.py:304
  60.5 10.8 %all-to-all-done.1.key_ref.normed_ref = bf16[8,128,1536]{2,1,0:T(8,128)(2,1)S(1)} async-done(((bf16[8,128,1536]{2,1,0:T(8,128)(2,1)}), bf16[8,128,1536]{2,1,0:T(8,128)(2,1)S(1)}, u32[]{:S(2)}, u32[]{:S(2)}) %all-to-all-start.1) | async-done | bytes 3145760 | tf_op jit(solution)/shard_map/all_to_all | solution.py:37
  71.3 1.8 shard_map.104
  73.1 47.0 %all_to_all.25.pieces_ref = bf16[64,16,512]{2,1,0:T(8,128)(2,1)S(1)} all-to-all(bf16[64,16,512]{2,1,0:T(8,128)(2,1)S(1)} %bitcast.8), channel_id=1, replica_groups=mesh['yl'=4,'x'=4,'c'=2,'z'=8,'yh'=2] {'yl','z','yh'}, dimensions={0} | all-to-all | bytes 2097152 | tf_op jit(solution)/shard_map/all_to_all | solution.py:37
  120.3 5.9 %collective-permute-start.3 = (f32[8,128]{1,0:T(8,128)S(1)}, f32[8,128]{1,0:T(8,128)S(1)}, u32[]{:S(2)}, u32[]{:S(2)}) collective-permute-start(f32[8,128]{1,0:T(8,128)S(1)} %get-tuple-element.31.one_ref), channel_id=1, source_target_pairs={{0,1},{1,0},{2,3},{3,2},{4,5},{5,4},{6,7},{7,6},{8,9},{9,8},{10,11... | collective-permute-start | bytes 12296 | tf_op jit(solution)/shard_map/ppermute | solution.py:312
  126.3 2.3 %collective-permute-done.3.two_ref = f32[8,128]{1,0:T(8,128)S(1)} collective-permute-done((f32[8,128]{1,0:T(8,128)S(1)}, f32[8,128]{1,0:T(8,128)S(1)}, u32[]{:S(2)}, u32[]{:S(2)}) %collective-permute-start.3) | collective-permute-done | bytes 4128 | tf_op jit(solution)/shard_map/ppermute | solution.py:312
  129.2 4.8 %all-gather.2.cloned.1.call-done = bf16[8192,256]{1,0:T(8,128)(2,1)} async-done(((bf16[128,256]{1,0:T(8,128)(2,1)}), bf16[8192,256]{1,0:T(8,128)(2,1)}) %all-gather.2.cloned.1.call-update) | async-done | bytes 4194320 | tf_op jit(solution)/shard_map/all_gather | solution.py:300
  134.0 4.7 %collective-permute-start.5 = (bf16[2,4,8,128,256]{4,3,2,1,0:T(8,128)(2,1)}, bf16[2,4,8,128,256]{4,3,2,1,0:T(8,128)(2,1)}, u32[]{:S(2)}, u32[]{:S(2)}) collective-permute-start(bf16[2,4,8,128,256]{4,3,2,1,0:T(8,128)(2,1)} %bitcast.11), channel_id=1, source_target_pairs={{0,16},{16,0},{1,17},{17,1},{2,18},{18,2},{3,19},{19,3},{4,20},{20... | collective-permute-start | bytes 12582920 | tf_op jit(solution)/shard_map/ppermute | solution.py:314
  138.7 4.7 %all-to-all-start.3 = ((f32[8,8,128]{2,1,0:T(8,128)}), f32[8,8,128]{2,1,0:T(8,128)S(1)}, u32[]{:S(2)}, u32[]{:S(2)}) async-start(f32[8,8,128]{2,1,0:T(8,128)} %shard_map.106), calls=%async_computation.3 | async-start | bytes 65536 | tf_op jit(solution)/shard_map/all_to_all | solution.py:37
  143.4 3.8 %collective-permute-start.4 = (f32[16,512]{1,0:T(8,128)S(1)}, f32[16,512]{1,0:T(8,128)S(1)}, u32[]{:S(2)}, u32[]{:S(2)}) collective-permute-start(f32[16,512]{1,0:T(8,128)S(1)} %get-tuple-element.32), channel_id=1, source_target_pairs={{0,0},{2,16},{4,32},{6,48},{8,64},{10,80},{12,96},{14,112},{16,2},... | collective-permute-start | bytes 98312 | tf_op jit(solution)/shard_map/ppermute | solution.py:311
  147.2 2.0 %collective-permute-done.4.shard_ref = f32[16,512]{1,0:T(8,128)S(1)} collective-permute-done((f32[16,512]{1,0:T(8,128)S(1)}, f32[16,512]{1,0:T(8,128)S(1)}, u32[]{:S(2)}, u32[]{:S(2)}) %collective-permute-start.4) | collective-permute-done | bytes 32800 | tf_op jit(solution)/shard_map/ppermute | solution.py:311
  149.2 1.1 all-to-all-done.3.squares_ref
  151.2 11.1 %all-to-all-start.4 = ((bf16[32,16,640]{2,1,0:T(8,128)(2,1)}), bf16[32,16,640]{2,1,0:T(8,128)(2,1)S(1)}, u32[]{:S(2)}, u32[]{:S(2)}) async-start(bf16[32,16,640]{2,1,0:T(8,128)(2,1)} %shard_map.107), calls=%async_computation.4 | async-start | bytes 1310720 | tf_op jit(solution)/shard_map/all_to_all | solution.py:37
  162.5 8.0 %shard_map.108 = bf16[128,8192]{1,0:T(8,128)(2,1)} custom-call(s32[1]{0:T(128)} %bitcast.4.core_ref, bf16[128,512]{1,0:T(8,128)(2,1)} %get-tuple-element.36.key_ref, bf16[2,4,8,128,256]{4,3,2,1,0:T(8,128)(2,1)} %bitcast.12, bf16[2,4,8,128,256]{4,3,2,1,0:T(8,128)(2,1)} %collective-permute-done.5.other_ref, bf16[128,8192]{1,0:T(8,128)(2,1)} %x_ref.3, ...), custom_call_target="tpu_custom_call" | custom-call | flops 1073741824 | bytes 12582912 | tf_op jit(solution)/shard_map/pallas_call | solution.py:176
  171.6 9.7 %all-to-all-done.4.gathered_ref = bf16[32,16,640]{2,1,0:T(8,128)(2,1)S(1)} async-done(((bf16[32,16,640]{2,1,0:T(8,128)(2,1)}), bf16[32,16,640]{2,1,0:T(8,128)(2,1)S(1)}, u32[]{:S(2)}, u32[]{:S(2)}) %all-to-all-start.4) | async-done | bytes 655392 | tf_op jit(solution)/shard_map/all_to_all | solution.py:37
  181.4 2.4 %shard_map.109 = (bf16[512,512]{1,0:T(8,128)(2,1)}, f32[16,512]{1,0:T(8,128)}, f32[16,512]{1,0:T(8,128)}) custom-call(s32[2]{0:T(128)S(1)} %pad_add_fusion.place_ref, bf16[32,16,640]{2,1,0:T(8,128)(2,1)S(1)} %all-to-all-done.4.gathered_ref, bf16[512,256]{1,0:T(8,128)(2,1)S(1)} %bitcast.10, bf16[512,256]{1,0:T(8,128)(2,1)S(1)} %bitcast.9, ...), custom_call_target="tpu_custom_call" | custom-call | tf_op jit(solution)/shard_map/pallas_call | solution.py:276
  (39 shorter events, 11.5 us)
Async XLA Ops:
  7.2 0.8 copy-start.6
  7.9 0.8 copy-start.8
  8.7 0.7 copy-start.10
  10.2 18.3 %all-to-all-start = ((bf16[8,16,1536]{2,1,0:T(8,128)(2,1)}), bf16[8,16,1536]{2,1,0:T(8,128)(2,1)S(1)}, u32[]{:S(2)}, u32[]{:S(2)}) async-start(bf16[8,16,1536]{2,1,0:T(8,128)(2,1)} %shard_map.103), calls=%async_computation | async-start | bytes 786432 | tf_op jit(solution)/shard_map/all_to_all | solution.py:37
  20.4 113.6 %all-gather.2.cloned.1.call-start = ((), (), s32[]{:S(2)}) async-start(), calls=%async_computation.5 | async-start | bytes 4259840 | tf_op jit(solution)/shard_map/all_gather | solution.py:300
  28.5 0.8 copy-start.11
  29.3 42.0 %all-to-all-start.1 = ((bf16[8,128,1536]{2,1,0:T(8,128)(2,1)}), bf16[8,128,1536]{2,1,0:T(8,128)(2,1)S(1)}, u32[]{:S(2)}, u32[]{:S(2)}) async-start(bf16[8,128,1536]{2,1,0:T(8,128)(2,1)} %get-tuple-element.28), calls=%async_computation.1 | async-start | bytes 6291456 | tf_op jit(solution)/shard_map/all_to_all | solution.py:37
  34.7 11.6 %collective-permute-start.2 = (bf16[128,1024]{1,0:T(8,128)(2,1)S(1)}, bf16[128,1024]{1,0:T(8,128)(2,1)S(1)}, u32[]{:S(2)}, u32[]{:S(2)}) collective-permute-start(bf16[128,1024]{1,0:T(8,128)(2,1)S(1)} %slice.3.m0_ref), channel_id=1, source_target_pairs={{0,384},{128,256},{256,128},{384,0},{1,385},{129,257},{257,129},{3... | collective-permute-start | bytes 786440 | tf_op jit(solution)/shard_map/ppermute | solution.py:304
  36.6 22.5 %collective-permute-start.1 = (bf16[128,1024]{1,0:T(8,128)(2,1)S(1)}, bf16[128,1024]{1,0:T(8,128)(2,1)S(1)}, u32[]{:S(2)}, u32[]{:S(2)}) collective-permute-start(bf16[128,1024]{1,0:T(8,128)(2,1)S(1)} %slice.3.m0_ref), channel_id=1, source_target_pairs={{0,256},{128,384},{256,0},{384,128},{1,257},{129,385},{257,1},{385... | collective-permute-start | bytes 786440 | tf_op jit(solution)/shard_map/ppermute | solution.py:304
  38.5 21.3 %collective-permute-start = (bf16[128,1024]{1,0:T(8,128)(2,1)S(1)}, bf16[128,1024]{1,0:T(8,128)(2,1)S(1)}, u32[]{:S(2)}, u32[]{:S(2)}) collective-permute-start(bf16[128,1024]{1,0:T(8,128)(2,1)S(1)} %slice.3.m0_ref), channel_id=1, source_target_pairs={{0,128},{128,0},{256,384},{384,256},{1,129},{129,1},{257,385},{385... | collective-permute-start | bytes 786440 | tf_op jit(solution)/shard_map/ppermute | solution.py:304
  46.3 0.7 copy-start
  59.1 0.7 copy-start.2
  59.8 0.7 copy-start.4
  120.3 8.3 %collective-permute-start.3 = (f32[8,128]{1,0:T(8,128)S(1)}, f32[8,128]{1,0:T(8,128)S(1)}, u32[]{:S(2)}, u32[]{:S(2)}) collective-permute-start(f32[8,128]{1,0:T(8,128)S(1)} %get-tuple-element.31.one_ref), channel_id=1, source_target_pairs={{0,1},{1,0},{2,3},{3,2},{4,5},{5,4},{6,7},{7,6},{8,9},{9,8},{10,11... | collective-permute-start | bytes 12296 | tf_op jit(solution)/shard_map/ppermute | solution.py:312
  134.0 17.2 %collective-permute-start.5 = (bf16[2,4,8,128,256]{4,3,2,1,0:T(8,128)(2,1)}, bf16[2,4,8,128,256]{4,3,2,1,0:T(8,128)(2,1)}, u32[]{:S(2)}, u32[]{:S(2)}) collective-permute-start(bf16[2,4,8,128,256]{4,3,2,1,0:T(8,128)(2,1)} %bitcast.11), channel_id=1, source_target_pairs={{0,16},{16,0},{1,17},{17,1},{2,18},{18,2},{3,19},{19,3},{4,20},{20... | collective-permute-start | bytes 12582920 | tf_op jit(solution)/shard_map/ppermute | solution.py:314
  138.7 11.5 %all-to-all-start.3 = ((f32[8,8,128]{2,1,0:T(8,128)}), f32[8,8,128]{2,1,0:T(8,128)S(1)}, u32[]{:S(2)}, u32[]{:S(2)}) async-start(f32[8,8,128]{2,1,0:T(8,128)} %shard_map.106), calls=%async_computation.3 | async-start | bytes 65536 | tf_op jit(solution)/shard_map/all_to_all | solution.py:37
  143.4 5.8 %collective-permute-start.4 = (f32[16,512]{1,0:T(8,128)S(1)}, f32[16,512]{1,0:T(8,128)S(1)}, u32[]{:S(2)}, u32[]{:S(2)}) collective-permute-start(f32[16,512]{1,0:T(8,128)S(1)} %get-tuple-element.32), channel_id=1, source_target_pairs={{0,0},{2,16},{4,32},{6,48},{8,64},{10,80},{12,96},{14,112},{16,2},... | collective-permute-start | bytes 98312 | tf_op jit(solution)/shard_map/ppermute | solution.py:311
  151.2 30.1 %all-to-all-start.4 = ((bf16[32,16,640]{2,1,0:T(8,128)(2,1)}), bf16[32,16,640]{2,1,0:T(8,128)(2,1)S(1)}, u32[]{:S(2)}, u32[]{:S(2)}) async-start(bf16[32,16,640]{2,1,0:T(8,128)(2,1)} %shard_map.107), calls=%async_computation.4 | async-start | bytes 1310720 | tf_op jit(solution)/shard_map/all_to_all | solution.py:37
  162.5 18.9 %copy-start.1 = (bf16[128,1024]{1,0:T(8,128)(2,1)S(1)}, bf16[128,1024]{1,0:T(8,128)(2,1)}, u32[]{:S(2)}) copy-start(bf16[128,1024]{1,0:T(8,128)(2,1)} %copy-done) | copy-start | bytes 786436
  162.5 18.9 %copy-start.3 = (bf16[128,1024]{1,0:T(8,128)(2,1)S(1)}, bf16[128,1024]{1,0:T(8,128)(2,1)}, u32[]{:S(2)}) copy-start(bf16[128,1024]{1,0:T(8,128)(2,1)} %copy-done.2) | copy-start | bytes 786436
  162.5 18.9 %copy-start.5 = (bf16[128,1024]{1,0:T(8,128)(2,1)S(1)}, bf16[128,1024]{1,0:T(8,128)(2,1)}, u32[]{:S(2)}) copy-start(bf16[128,1024]{1,0:T(8,128)(2,1)} %copy-done.4) | copy-start | bytes 786436
  162.5 18.9 %copy-start.7 = (f32[16,512]{1,0:T(8,128)S(1)}, f32[16,512]{1,0:T(8,128)}, u32[]{:S(2)}) copy-start(f32[16,512]{1,0:T(8,128)} %first_ref.3) | copy-start | bytes 98308
  162.5 18.9 %copy-start.9 = (f32[16,512]{1,0:T(8,128)S(1)}, f32[16,512]{1,0:T(8,128)}, u32[]{:S(2)}) copy-start(f32[16,512]{1,0:T(8,128)} %second_ref.3) | copy-start | bytes 98308
Sparse Core Ops, SparseCore 0:
  29.3 104.6 all-gather.1

commit v4 on v3

--- a/solution.py
+++ b/solution.py
@@ -128,25 +128,30 @@
     )(received, received)
 
 
-def backward_kernel(
-    core_ref, key_ref, own_ref, other_ref, x_ref, scale_ref, gain_ref, out_ref, held, cross
-):
+def backward_kernel(place_ref, key_ref, *refs):
+    own, other = refs[:4], refs[4:8]
+    x_ref, scale_ref, gain_ref, out_ref, held, cross, sorted_keys = refs[8:]
     step = pl.program_id(0)
-    core = core_ref[0]
-    half = own_ref.shape[4]
+    core, yl, x, z, yh = (place_ref[i] for i in range(5))
+    deep, half = own[0].shape[0], own[0].shape[4]
     width = 2 * half
-    first = step * own_ref.shape[2] * 2
 
     @pl.when(step == 0)
     def _():
         cross[...] = jnp.zeros_like(cross)
+        row = lax.broadcasted_iota(jnp.int32, (KV, KV), 0)
+        at = lax.broadcasted_iota(jnp.int32, (KV, KV), 1)
+        source = ((((at >> 5) & 3) ^ yl) * 4 + ((at >> 7) ^ x)) * 32 + (at & 31)
+        order = jnp.where(row == source, 1.0, 0.0).astype(bf16)
+        sorted_keys[...] = jnp.dot(key_ref[...], order, preferred_element_type=f32).astype(bf16)
 
     total = jnp.zeros(cross.shape, f32)
-    for z in range(own_ref.shape[2]):
-        for yh in range(2):
-            block = first + z * 2 + yh
-            for side, ref in ((core, own_ref), (1 - core, other_ref)):
-                up = jnp.dot(key_ref[...], ref[yh, :, z].reshape(KV, half), preferred_element_type=f32)
+    for kz in range(deep):
+        for kyh in range(2):
+            block = (z ^ (step * deep + kz)) * 2 + (yh ^ kyh)
+            for side, pieces in ((core, own), (1 - core, other)):
+                weight = jnp.concatenate([p[kz, kyh].reshape(KV // 4, half) for p in pieces], axis=0)
+                up = jnp.dot(sorted_keys[...], weight, preferred_element_type=f32)
                 for k in range(half // HEAD):
                     group = block * (width // HEAD) + side * (half // HEAD) + k
                     columns = pl.ds(pl.multiple_of(group * HEAD, HEAD), HEAD)
@@ -162,40 +167,58 @@
         inner = scale * scale * (jnp.sum(cross[...], axis=1, keepdims=True) / D)
         for t in range(D // width):
             part = slice(t * width, (t + 1) * width)
-            x = x_ref[:, part].astype(f32)
-            out_ref[:, part] = (scale * (held[t] - x * inner)).astype(bf16)
-
-
-def backward(core, keys, own, other, x, scale, gain):
+            x_part = x_ref[:, part].astype(f32)
+            out_ref[:, part] = (scale * (held[t] - x_part * inner)).astype(bf16)
+
+
+def backward(place, keys, own, other, x, scale, gain):
     tokens = x.shape[0]
     width = 512
     deep = 2
     steps = 8 // deep
-    weights = pl.BlockSpec((2, 4, deep, 128, width // 2), lambda t, core: (0, 0, t, 0, 0))
-    whole = lambda a: pl.BlockSpec(a.shape, lambda t, core: (0, 0))
+    weights = pl.BlockSpec((deep, *own[0].shape[1:]), lambda t, place: (t, 0, 0, 0, 0))
+    whole = lambda a: pl.BlockSpec(a.shape, lambda t, place: (0, 0))
     return pl.pallas_call(
         backward_kernel,
         grid_spec=pltpu.PrefetchScalarGridSpec(
             num_scalar_prefetch=1,
             grid=(steps,),
-            in_specs=[whole(keys), weights, weights, whole(x), whole(scale), whole(gain)],
-            out_specs=pl.BlockSpec((tokens, D), lambda t, core: (0, 0)),
-            scratch_shapes=[pltpu.VMEM((D // width, tokens, width), f32), pltpu.VMEM((tokens, HEAD), f32)],
+            in_specs=[whole(keys)] + [weights] * 8 + [whole(x), whole(scale), whole(gain)],
+            out_specs=pl.BlockSpec((tokens, D), lambda t, place: (0, 0)),
+            scratch_shapes=[
+                pltpu.VMEM((D // width, tokens, width), f32),
+                pltpu.VMEM((tokens, HEAD), f32),
+                pltpu.VMEM((tokens, KV), bf16),
+            ],
         ),
         out_shape=jax.ShapeDtypeStruct((tokens, D), bf16),
         compiler_params=pltpu.CompilerParams(vmem_limit_bytes=56 * 1024 * 1024),
         cost_estimate=pl.CostEstimate(
             flops=2 * tokens * KV * D, bytes_accessed=12 * 1024 * 1024, transcendentals=0
         ),
-    )(core, keys, own, other, x, scale, gain)
-
-
-def local_call(kernel, outs, *args):
+    )(place, keys, *own, *other, x, scale, gain)
+
+
+def local_call(kernel, outs, *args, vmem=32):
     return pl.pallas_call(
         kernel,
         out_shape=[jax.ShapeDtypeStruct(shape, kind) for shape, kind in outs],
-        compiler_params=pltpu.CompilerParams(vmem_limit_bytes=32 * 1024 * 1024),
+        compiler_params=pltpu.CompilerParams(vmem_limit_bytes=vmem * 1024 * 1024),
     )(*args)
+
+
+def stack_kernel(*refs):
+    for k, ref in enumerate(refs[:-1]):
+        refs[-1][k] = ref[...]
+
+
+def from_others(x, axis):
+    return [lax.ppermute(x, axis, [(i, i ^ k) for i in range(lax.axis_size(axis))]) for k in range(1, lax.axis_size(axis))]
+
+
+def stacked(x, axis):
+    parts = [x, *from_others(x, axis)]
+    return local_call(stack_kernel, [((len(parts), *x.shape), x.dtype)], *parts)[0]
 
 
 def add_pieces_kernel(pieces_ref, piece_ref, square_ref):
@@ -235,7 +258,7 @@
 
 
 def update_kernel(
-    place_ref, gathered_ref, own_ref, other_ref, m0_ref, m1_ref, m2_ref, m3_ref, shard_ref, first_ref, second_ref,
+    place_ref, gathered_ref, s0_ref, s1_ref, s2_ref, s3_ref, shard_ref, first_ref, second_ref,
     weight_out, first_out, second_out,
 ):
     terms = jnp.sum(gathered_ref[:, :, 512:].astype(f32), axis=0)
@@ -253,22 +276,17 @@
     new_first, new_second = moments(shard_ref[...], first_ref[...], second_ref[...])
     first_out[...] = new_first
     second_out[...] = new_second
-    core, yl = place_ref[0], place_ref[1]
-    half = own_ref.shape[1]
-    for k, ref in enumerate((m0_ref, m1_ref, m2_ref, m3_ref)):
-        block = yl ^ k
+    for k, ref in enumerate((s0_ref, s1_ref, s2_ref, s3_ref)):
+        block = place_ref[1] ^ k
         for r in range(8):
-            part = slice(r * 16, (r + 1) * 16)
             rows = pl.ds(pl.multiple_of(block * 128 + r * 16, 16), 16)
             gradient = gathered_ref[block * 8 + r, :, :512].astype(f32)
-            new_first, new_second = moments(gradient, ref[part, :512].astype(f32), ref[part, 512:].astype(f32))
-            step = learn_rate * new_first / (jnp.sqrt(new_second) + eps_adam)
-            own = own_ref[rows, :].astype(f32)
-            other = other_ref[rows, :].astype(f32)
-            for side in range(2):
-                inside = slice(side * half, (side + 1) * half)
-                weight = jnp.where(core == side, own, other)
-                weight_out[rows, inside] = (weight * (1.0 - learn_rate * decay_rate) - step[:, inside]).astype(bf16)
+            state = ref[r * 16 : (r + 1) * 16, :].astype(f32)
+            new_first, new_second = moments(gradient, state[:, 512:1024], state[:, 1024:])
+            weight_out[rows, :] = (
+                state[:, :512] * (1.0 - learn_rate * decay_rate)
+                - learn_rate * new_first / (jnp.sqrt(new_second) + eps_adam)
+            ).astype(bf16)
 
 
 def update(place, *args):
@@ -289,39 +307,40 @@
 
 
 def body(norm_input, key_grad, positions, norm_gain, key_weight, first_moment, second_moment):
-    core = lax.axis_index("c")
-    state = local_call(state_kernel, [((N_GROUP, 16, 1536), bf16)], key_weight, first_moment, second_moment)[0]
-    state = exchange(state, GROUP).reshape(N_GROUP * 16, 1536)
+    place = jnp.stack([lax.axis_index(name) for name in ("c", "yl", "x", "z", "yh")]).astype(jnp.int32)
+    state = local_call(
+        state_kernel, [((N_GROUP, 16, 1536), bf16)], key_weight, first_moment, second_moment, vmem=56
+    )[0]
+    state = exchange(state, GROUP)
     cosine, sine = rotation(positions)
     send, keys, scale, gain = prepare(norm_input, key_grad, cosine, sine, norm_gain.reshape(D // HEAD, HEAD))
     send, state = lax.optimization_barrier((send, state))
 
-    half = lax.dynamic_slice_in_dim(state, core * 256, 256, 1)
-    own = lax.all_gather(half, ("yh", "yl", "z"), axis=0, tiled=True).reshape(2, 4, 8, 128, 256)
-
     received = exchange(send, GROUP)
-    moments = [state[:, 512:]]
-    moments += [lax.ppermute(moments[0], "yl", [(i, i ^ k) for i in range(4)]) for k in (1, 2, 3)]
-    received, *moments = lax.optimization_barrier((received, *moments))
+    own = lax.dynamic_slice(state, (2 * place[2], 0, 256 * place[0]), (2, 16, 256)).reshape(32, 256)
+    own = stacked(stacked(stacked(own, "yl"), "yh"), "z")
+    state = state.reshape(N_GROUP * 16, 1536)
+    states = [state, *from_others(state, "yl")]
+    received, own, *states = lax.optimization_barrier((received, own, *states))
+
     partial = product(received).reshape(N_PLANE, 16, 512)
+    own, partial = lax.optimization_barrier((own, partial))
     pieces = exchange(partial, PLANE)
+    own = [own, *from_others(own, "x")]
+    pieces, *own = lax.optimization_barrier((pieces, *own))
     piece, square = add_pieces(pieces)
 
     swap = [(i * 8 + k, k * 8 + i) for i in range(8) for k in range(8)]
     grad_shard = lax.ppermute(piece, ("x", "c", "z"), swap)
     square = add_pair(square, lax.ppermute(square, "yh", [(0, 1), (1, 0)]))
-    own, _ = lax.optimization_barrier((own, square))
-    other = lax.ppermute(own, "c", [(0, 1), (1, 0)])
+    *own, _ = lax.optimization_barrier((*own, square))
+    other = [lax.ppermute(part, "c", [(0, 1), (1, 0)]) for part in own]
     late = late_rows(exchange(square, "z"), grad_shard)
-    late, own, other = lax.optimization_barrier((late, own, other))
+    late, *halves = lax.optimization_barrier((late, *own, *other))
     gathered = exchange(late, DP)
-    input_grad = backward(core.astype(jnp.int32).reshape(1), keys, own, other, norm_input, scale, gain)
-    own, other, input_grad = lax.optimization_barrier((own, other, input_grad))
-    z, yh = lax.axis_index("z"), lax.axis_index("yh")
-    weights = [lax.dynamic_slice(w, (yh, 0, z, 0, 0), (1, 4, 1, 128, 256)).reshape(KV, 256) for w in (own, other)]
-    place = jnp.stack([core, lax.axis_index("yl")]).astype(jnp.int32)
+    input_grad = backward(place, keys, halves[:4], halves[4:], norm_input, scale, gain)
     new_weight, new_first, new_second = update(
-        place, gathered, *weights, *moments, grad_shard, first_moment, second_moment
+        place, gathered, *states, grad_shard, first_moment, second_moment
     )
     return (input_grad, new_weight, new_first, new_second)
 

time: 192 us -> 234 us (1.22)
  starting transfers between devices: 54.2 us -> 138 us
  blocking collectives: 47 us -> 0 us
  waiting for transfers between devices: 46.9 us -> 64.4 us
  between operations: 14.2 us -> 1.01 us
    ppermute x4 -> x21, starting transfers between devices: 14 us -> 83.5 us  [the longest x17 58.9 us: from_others(): lax.ppermute(x, axis, [(i, i ^ k) for i in range(lax.axis_size(axis))])]
    all_to_all x1 -> x0, blocking collectives: 47 us -> none  [exchange(): return lax.all_to_all(x, axes, split_axis=0, concat_axis=0, tiled=True)]
    ppermute x4 -> x21, waiting for transfers between devices: 14.4 us -> 49.2 us  [the longest x17 49.2 us: from_others(): lax.ppermute(x, axis, [(i, i ^ k) for i in range(lax.axis_size(axis))])]
    all_to_all x4 -> x5, starting transfers between devices: 30.5 us -> 44 us  [exchange(): return lax.all_to_all(x, axes, split_axis=0, concat_axis=0, tiled=True)]
    all_to_all x4 -> x5, waiting for transfers between devices: 23.3 us -> 11.5 us  [exchange(): return lax.all_to_all(x, axes, split_axis=0, concat_axis=0, tiled=True)]
    all_gather x1 -> x0, waiting for transfers between devices: 4.84 us -> none  [body(): lax.all_gather(half, ('yh', 'yl', 'z'), axis=0, tiled=True)]
    unnamed x24 -> x30, local copies, waits for them, and re-layouts: 4.42 us -> 5.22 us
  transfers between devices with their start and end apart: 11 -> 28, of which waited for: 9 -> 12; matrix products, arithmetic and copies ran while one was open for 2% -> 1% of each run, Pallas kernels for 9% -> 6%
where the time goes in v4:
time: 234 us; the launch traced here: 233 us
  starting transfers between devices  138 us (59%)
  waiting for transfers between devices  64.4 us (28%)
  Pallas kernels  21.5 us (9%)
  local copies, waits for them, and re-layouts  5.83 us (2%)
    ppermute x17, starting transfers between devices, from_others(): lax.ppermute(x, axis, [(i, i ^ k) for i in range(lax.axis_size(axis))])  58.9 us
    ppermute x17, waiting for transfers between devices, from_others(): lax.ppermute(x, axis, [(i, i ^ k) for i in range(lax.axis_size(axis))])  49.2 us
    all_to_all x5, starting transfers between devices, exchange(): return lax.all_to_all(x, axes, split_axis=0, concat_axis=0, tiled=True)  44 us
    ppermute x4, starting transfers between devices, body(): other = [lax.ppermute(part, 'c', [(0, 1), (1, 0)]) for part in own]  24.5 us
    all_to_all x5, waiting for transfers between devices, exchange(): return lax.all_to_all(x, axes, split_axis=0, concat_axis=0, tiled=True)  11.5 us
    pallas_call x1, Pallas kernels, backward(): pl.pallas_call(backward_kernel, grid_spec=pltpu.PrefetchScalarGridSpec(nu...  9.15 us
    ppermute x1, starting transfers between devices, body(): square = add_pair(square, lax.ppermute(square, 'yh', [(0, 1), (1, 0)]))  6.54 us
    unnamed x30, local copies, waits for them, and re-layouts  5.22 us
  transfers between devices with their start and end apart: 28, of which 12 were waited for; matrix products, arithmetic and copies ran while one was open for 1% of the time, Pallas kernels for 6%

profile of v4, /device:TPU:1, one launch (start us, length us, event | category | flops | bytes accessed | tf_op | source)
XLA Modules:
  0.0 232.6 jit_solution(12167557220351665578)
XLA Ops:
  2.2 10.2 %all-to-all-start = ((bf16[8,16,1536]{2,1,0:T(8,128)(2,1)}), bf16[8,16,1536]{2,1,0:T(8,128)(2,1)S(1)}, u32[]{:S(2)}, u32[]{:S(2)}) async-start(bf16[8,16,1536]{2,1,0:T(8,128)(2,1)} %shard_map.103), calls=%async_computation | async-start | bytes 786432 | tf_op jit(solution)/shard_map/all_to_all | solution.py:37
  14.1 4.8 %shard_map.102 = (bf16[8,128,1536]{2,1,0:T(8,128)(2,1)}, bf16[128,512]{1,0:T(8,128)(2,1)}, f32[128,128]{1,0:T(8,128)}, f32[64,128]{1,0:T(8,128)}) custom-call(bf16[128,8192]{1,0:T(8,128)(2,1)} %refs_8_.1, bf16[128,512]{1,0:T(8,128)(2,1)} %key_ref.1, f32[128,64]{1,0:T(8,128)} %get-tuple-element.79.cos_ref, f32[128,64]{1,0:T(8,128)} %get-tuple-element.78.sin_ref, ...), custom_call_target="tpu_custom_call" | custom-call | flops 8388608 | bytes 6291456 | tf_op jit(solution)/shard_map/pallas_call | solution.py:77
  20.5 4.4 %all-to-all-start.1 = ((bf16[8,128,1536]{2,1,0:T(8,128)(2,1)}), bf16[8,128,1536]{2,1,0:T(8,128)(2,1)S(1)}, u32[]{:S(2)}, u32[]{:S(2)}) async-start(bf16[8,128,1536]{2,1,0:T(8,128)(2,1)} %get-tuple-element.43), calls=%async_computation.1 | async-start | bytes 6291456 | tf_op jit(solution)/shard_map/all_to_all | solution.py:37
  28.8 5.4 %collective-permute-start.2 = (bf16[32,256]{1,0:T(8,128)(2,1)S(1)}, bf16[32,256]{1,0:T(8,128)(2,1)S(1)}, u32[]{:S(2)}, u32[]{:S(2)}) collective-permute-start(bf16[32,256]{1,0:T(8,128)(2,1)S(1)} %bitcast.16), channel_id=1, source_target_pairs={{0,384},{128,256},{256,128},{384,0},{1,385},{129,257},{257,129},{3... | collective-permute-start | bytes 49160 | tf_op jit(solution)/shard_map/ppermute | solution.py:216
  35.7 3.6 %collective-permute-start.3 = (bf16[4,32,256]{2,1,0:T(8,128)(2,1)S(1)}, bf16[4,32,256]{2,1,0:T(8,128)(2,1)S(1)}, u32[]{:S(2)}, u32[]{:S(2)}) collective-permute-start(bf16[4,32,256]{2,1,0:T(8,128)(2,1)S(1)} %shard_map.104.refs_0_), channel_id=1, source_target_pairs={{0,1},{1,0},{2,3},{3,2},{4,5},{5,4},{6,7},{7,6},{8,9},{9,8},{10,11... | collective-permute-start | bytes 196616 | tf_op jit(solution)/shard_map/ppermute | solution.py:216
  39.3 5.5 %collective-permute-done.3.refs_1_ = bf16[4,32,256]{2,1,0:T(8,128)(2,1)S(1)} collective-permute-done((bf16[4,32,256]{2,1,0:T(8,128)(2,1)S(1)}, bf16[4,32,256]{2,1,0:T(8,128)(2,1)S(1)}, u32[]{:S(2)}, u32[]{:S(2)}) %collective-permute-start.3) | collective-permute-done | bytes 65568 | tf_op jit(solution)/shard_map/ppermute | solution.py:216
  44.8 9.0 %collective-permute-start.10 = (bf16[2,4,32,256]{3,2,1,0:T(8,128)(2,1)S(1)}, bf16[2,4,32,256]{3,2,1,0:T(8,128)(2,1)S(1)}, u32[]{:S(2)}, u32[]{:S(2)}) collective-permute-start(bf16[2,4,32,256]{3,2,1,0:T(8,128)(2,1)S(1)} %shard_map.105.refs_0_), channel_id=1, source_target_pairs={{0,14},{2,12},{4,10},{6,8},{8,6},{10,4},{12,2},{14,0},{1,15},{3,13... | collective-permute-start | bytes 393224 | tf_op jit(solution)/shard_map/ppermute | solution.py:216
  53.8 3.1 %collective-permute-start.4 = (bf16[2,4,32,256]{3,2,1,0:T(8,128)(2,1)S(1)}, bf16[2,4,32,256]{3,2,1,0:T(8,128)(2,1)S(1)}, u32[]{:S(2)}, u32[]{:S(2)}) collective-permute-start(bf16[2,4,32,256]{3,2,1,0:T(8,128)(2,1)S(1)} %shard_map.105.refs_0_), channel_id=1, source_target_pairs={{0,2},{2,0},{4,6},{6,4},{8,10},{10,8},{12,14},{14,12},{1,3},{3,1},... | collective-permute-start | bytes 393224 | tf_op jit(solution)/shard_map/ppermute | solution.py:216
  63.3 4.8 %collective-permute-start.13 = (bf16[128,1536]{1,0:T(8,128)(2,1)S(1)}, bf16[128,1536]{1,0:T(8,128)(2,1)S(1)}, u32[]{:S(2)}, u32[]{:S(2)}) collective-permute-start(bf16[128,1536]{1,0:T(8,128)(2,1)S(1)} %bitcast.12), channel_id=1, source_target_pairs={{0,384},{128,256},{256,128},{384,0},{1,385},{129,257},{257,129},{3... | collective-permute-start | bytes 1179656 | tf_op jit(solution)/shard_map/ppermute | solution.py:216
  68.1 4.3 %collective-permute-start.6 = (bf16[2,4,32,256]{3,2,1,0:T(8,128)(2,1)S(1)}, bf16[2,4,32,256]{3,2,1,0:T(8,128)(2,1)S(1)}, u32[]{:S(2)}, u32[]{:S(2)}) collective-permute-start(bf16[2,4,32,256]{3,2,1,0:T(8,128)(2,1)S(1)} %shard_map.105.refs_0_), channel_id=1, source_target_pairs={{0,6},{2,4},{4,2},{6,0},{8,14},{10,12},{12,10},{14,8},{1,7},{3,5},... | collective-permute-start | bytes 393224 | tf_op jit(solution)/shard_map/ppermute | solution.py:216
  75.8 5.0 %collective-permute-start.8 = (bf16[2,4,32,256]{3,2,1,0:T(8,128)(2,1)S(1)}, bf16[2,4,32,256]{3,2,1,0:T(8,128)(2,1)S(1)}, u32[]{:S(2)}, u32[]{:S(2)}) collective-permute-start(bf16[2,4,32,256]{3,2,1,0:T(8,128)(2,1)S(1)} %shard_map.105.refs_0_), channel_id=1, source_target_pairs={{0,10},{2,8},{4,14},{6,12},{8,2},{10,0},{12,6},{14,4},{1,11},{3,9}... | collective-permute-start | bytes 393224 | tf_op jit(solution)/shard_map/ppermute | solution.py:216
  85.1 5.9 %collective-permute-done.9.refs_6_ = bf16[2,4,32,256]{3,2,1,0:T(8,128)(2,1)S(1)} collective-permute-done((bf16[2,4,32,256]{3,2,1,0:T(8,128)(2,1)S(1)}, bf16[2,4,32,256]{3,2,1,0:T(8,128)(2,1)S(1)}, u32[]{:S(2)}, u32[]{:S(2)}) %collective-permute-start.9) | collective-permute-done | bytes 131104 | tf_op jit(solution)/shard_map/ppermute | solution.py:216
  97.1 12.3 %all-to-all-start.2 = ((bf16[64,16,512]{2,1,0:T(8,128)(2,1)}), bf16[64,16,512]{2,1,0:T(8,128)(2,1)S(1)}, u32[]{:S(2)}, u32[]{:S(2)}) async-start(bf16[64,16,512]{2,1,0:T(8,128)(2,1)} %bitcast.9), calls=%async_computation.2 | async-start | bytes 2097152 | tf_op jit(solution)/shard_map/all_to_all | solution.py:37
  109.3 2.7 %collective-permute-start.14 = (bf16[8,2,4,32,256]{4,3,2,1,0:T(8,128)(2,1)}, bf16[8,2,4,32,256]{4,3,2,1,0:T(8,128)(2,1)S(1)}, u32[]{:S(2)}, u32[]{:S(2)}) collective-permute-start(bf16[8,2,4,32,256]{4,3,2,1,0:T(8,128)(2,1)} %copy-done), channel_id=1, source_target_pairs={{0,32},{32,0},{64,96},{96,64},{1,33},{33,1},{65,97},{97,65},{2,34}... | collective-permute-start | bytes 3145736 | tf_op jit(solution)/shard_map/ppermute | solution.py:216
  112.0 4.3 %collective-permute-start.15 = (bf16[8,2,4,32,256]{4,3,2,1,0:T(8,128)(2,1)}, bf16[8,2,4,32,256]{4,3,2,1,0:T(8,128)(2,1)S(1)}, u32[]{:S(2)}, u32[]{:S(2)}) collective-permute-start(bf16[8,2,4,32,256]{4,3,2,1,0:T(8,128)(2,1)} %copy-done), channel_id=1, source_target_pairs={{0,64},{32,96},{64,0},{96,32},{1,65},{33,97},{65,1},{97,33},{2,66}... | collective-permute-start | bytes 3145736 | tf_op jit(solution)/shard_map/ppermute | solution.py:216
  118.9 9.4 %collective-permute-done.14.refs_1_ = bf16[8,2,4,32,256]{4,3,2,1,0:T(8,128)(2,1)S(1)} collective-permute-done((bf16[8,2,4,32,256]{4,3,2,1,0:T(8,128)(2,1)}, bf16[8,2,4,32,256]{4,3,2,1,0:T(8,128)(2,1)S(1)}, u32[]{:S(2)}, u32[]{:S(2)}) %collective-permute-start.14) | collective-permute-done | bytes 1048608 | tf_op jit(solution)/shard_map/ppermute | solution.py:216
  128.3 23.3 %collective-permute-done.15.refs_2_ = bf16[8,2,4,32,256]{4,3,2,1,0:T(8,128)(2,1)S(1)} collective-permute-done((bf16[8,2,4,32,256]{4,3,2,1,0:T(8,128)(2,1)}, bf16[8,2,4,32,256]{4,3,2,1,0:T(8,128)(2,1)S(1)}, u32[]{:S(2)}, u32[]{:S(2)}) %collective-permute-start.15) | collective-permute-done | bytes 1048608 | tf_op jit(solution)/shard_map/ppermute | solution.py:216
  152.9 6.5 %collective-permute-start.17 = (f32[8,128]{1,0:T(8,128)S(1)}, f32[8,128]{1,0:T(8,128)S(1)}, u32[]{:S(2)}, u32[]{:S(2)}) collective-permute-start(f32[8,128]{1,0:T(8,128)S(1)} %get-tuple-element.50.one_ref), channel_id=1, source_target_pairs={{0,1},{1,0},{2,3},{3,2},{4,5},{5,4},{6,7},{7,6},{8,9},{9,8},{10,11... | collective-permute-start | bytes 12296 | tf_op jit(solution)/shard_map/ppermute | solution.py:335
  161.7 18.3 %collective-permute-start.19 = (bf16[8,2,4,32,256]{4,3,2,1,0:T(8,128)(2,1)S(1)}, bf16[8,2,4,32,256]{4,3,2,1,0:T(8,128)(2,1)S(1)}, u32[]{:S(2)}, u32[]{:S(2)}) collective-permute-start(bf16[8,2,4,32,256]{4,3,2,1,0:T(8,128)(2,1)S(1)} %copy-done.1), channel_id=1, source_target_pairs={{0,16},{16,0},{1,17},{17,1},{2,18},{18,2},{3,19},{19,3},{4,20},{20... | collective-permute-start | bytes 3145736 | tf_op jit(solution)/shard_map/ppermute | solution.py:337
  186.3 6.2 %all-to-all-start.3 = ((f32[8,8,128]{2,1,0:T(8,128)}), f32[8,8,128]{2,1,0:T(8,128)S(1)}, u32[]{:S(2)}, u32[]{:S(2)}) async-start(f32[8,8,128]{2,1,0:T(8,128)} %shard_map.109), calls=%async_computation.3 | async-start | bytes 65536 | tf_op jit(solution)/shard_map/all_to_all | solution.py:37
  192.5 4.3 %collective-permute-start.18 = (f32[16,512]{1,0:T(8,128)S(1)}, f32[16,512]{1,0:T(8,128)S(1)}, u32[]{:S(2)}, u32[]{:S(2)}) collective-permute-start(f32[16,512]{1,0:T(8,128)S(1)} %get-tuple-element.51), channel_id=1, source_target_pairs={{0,0},{2,16},{4,32},{6,48},{8,64},{10,80},{12,96},{14,112},{16,2},... | collective-permute-start | bytes 98312 | tf_op jit(solution)/shard_map/ppermute | solution.py:334
  200.4 10.9 %all-to-all-start.4 = ((bf16[32,16,640]{2,1,0:T(8,128)(2,1)}), bf16[32,16,640]{2,1,0:T(8,128)(2,1)S(1)}, u32[]{:S(2)}, u32[]{:S(2)}) async-start(bf16[32,16,640]{2,1,0:T(8,128)(2,1)} %shard_map.110), calls=%async_computation.4 | async-start | bytes 1310720 | tf_op jit(solution)/shard_map/all_to_all | solution.py:37
  212.0 9.2 %shard_map.111 = bf16[128,8192]{1,0:T(8,128)(2,1)} custom-call(s32[5]{0:T(128)} %stack.23.place_ref, bf16[128,512]{1,0:T(8,128)(2,1)} %get-tuple-element.41.key_ref, bf16[8,2,4,32,256]{4,3,2,1,0:T(8,128)(2,1)} %copy-done, bf16[8,2,4,32,256]{4,3,2,1,0:T(8,128)(2,1)} %copy-done.12, bf16[8,2,4,32,256]{4,3,2,1,0:T(8,128)(2,1)} %copy-done.13, ...), custom_call_target="tpu_custom_call" | custom-call | flops 1073741824 | bytes 12582912 | tf_op jit(solution)/shard_map/pallas_call | solution.py:181
  221.1 9.1 %all-to-all-done.4.gathered_ref = bf16[32,16,640]{2,1,0:T(8,128)(2,1)S(1)} async-done(((bf16[32,16,640]{2,1,0:T(8,128)(2,1)}), bf16[32,16,640]{2,1,0:T(8,128)(2,1)S(1)}, u32[]{:S(2)}, u32[]{:S(2)}) %all-to-all-start.4) | async-done | bytes 655392 | tf_op jit(solution)/shard_map/all_to_all | solution.py:37
  (78 shorter events, 49.2 us)
Async XLA Ops:
  2.2 18.3 %all-to-all-start = ((bf16[8,16,1536]{2,1,0:T(8,128)(2,1)}), bf16[8,16,1536]{2,1,0:T(8,128)(2,1)S(1)}, u32[]{:S(2)}, u32[]{:S(2)}) async-start(bf16[8,16,1536]{2,1,0:T(8,128)(2,1)} %shard_map.103), calls=%async_computation | async-start | bytes 786432 | tf_op jit(solution)/shard_map/all_to_all | solution.py:37
  20.5 73.8 %all-to-all-start.1 = ((bf16[8,128,1536]{2,1,0:T(8,128)(2,1)}), bf16[8,128,1536]{2,1,0:T(8,128)(2,1)S(1)}, u32[]{:S(2)}, u32[]{:S(2)}) async-start(bf16[8,128,1536]{2,1,0:T(8,128)(2,1)} %get-tuple-element.43), calls=%async_computation.1 | async-start | bytes 6291456 | tf_op jit(solution)/shard_map/all_to_all | solution.py:37
  25.0 9.3 %collective-permute-start = (bf16[32,256]{1,0:T(8,128)(2,1)S(1)}, bf16[32,256]{1,0:T(8,128)(2,1)S(1)}, u32[]{:S(2)}, u32[]{:S(2)}) collective-permute-start(bf16[32,256]{1,0:T(8,128)(2,1)S(1)} %bitcast.14), channel_id=1, source_target_pairs={{0,128},{128,0},{256,384},{384,256},{1,129},{129,1},{257,385},{385... | collective-permute-start | bytes 49160 | tf_op jit(solution)/shard_map/ppermute | solution.py:216
  35.7 9.1 %collective-permute-start.3 = (bf16[4,32,256]{2,1,0:T(8,128)(2,1)S(1)}, bf16[4,32,256]{2,1,0:T(8,128)(2,1)S(1)}, u32[]{:S(2)}, u32[]{:S(2)}) collective-permute-start(bf16[4,32,256]{2,1,0:T(8,128)(2,1)S(1)} %shard_map.104.refs_0_), channel_id=1, source_target_pairs={{0,1},{1,0},{2,3},{3,2},{4,5},{5,4},{6,7},{7,6},{8,9},{9,8},{10,11... | collective-permute-start | bytes 196616 | tf_op jit(solution)/shard_map/ppermute | solution.py:216
  44.8 18.5 %collective-permute-start.10 = (bf16[2,4,32,256]{3,2,1,0:T(8,128)(2,1)S(1)}, bf16[2,4,32,256]{3,2,1,0:T(8,128)(2,1)S(1)}, u32[]{:S(2)}, u32[]{:S(2)}) collective-permute-start(bf16[2,4,32,256]{3,2,1,0:T(8,128)(2,1)S(1)} %shard_map.105.refs_0_), channel_id=1, source_target_pairs={{0,14},{2,12},{4,10},{6,8},{8,6},{10,4},{12,2},{14,0},{1,15},{3,13... | collective-permute-start | bytes 393224 | tf_op jit(solution)/shard_map/ppermute | solution.py:216
  53.8 14.3 %collective-permute-start.4 = (bf16[2,4,32,256]{3,2,1,0:T(8,128)(2,1)S(1)}, bf16[2,4,32,256]{3,2,1,0:T(8,128)(2,1)S(1)}, u32[]{:S(2)}, u32[]{:S(2)}) collective-permute-start(bf16[2,4,32,256]{3,2,1,0:T(8,128)(2,1)S(1)} %shard_map.105.refs_0_), channel_id=1, source_target_pairs={{0,2},{2,0},{4,6},{6,4},{8,10},{10,8},{12,14},{14,12},{1,3},{3,1},... | collective-permute-start | bytes 393224 | tf_op jit(solution)/shard_map/ppermute | solution.py:216
  56.9 15.5 %collective-permute-start.5 = (bf16[2,4,32,256]{3,2,1,0:T(8,128)(2,1)S(1)}, bf16[2,4,32,256]{3,2,1,0:T(8,128)(2,1)S(1)}, u32[]{:S(2)}, u32[]{:S(2)}) collective-permute-start(bf16[2,4,32,256]{3,2,1,0:T(8,128)(2,1)S(1)} %shard_map.105.refs_0_), channel_id=1, source_target_pairs={{0,4},{2,6},{4,0},{6,2},{8,12},{10,14},{12,8},{14,10},{1,5},{3,7},... | collective-permute-start | bytes 393224 | tf_op jit(solution)/shard_map/ppermute | solution.py:216
  58.8 33.2 %collective-permute-start.11 = (bf16[128,1536]{1,0:T(8,128)(2,1)S(1)}, bf16[128,1536]{1,0:T(8,128)(2,1)S(1)}, u32[]{:S(2)}, u32[]{:S(2)}) collective-permute-start(bf16[128,1536]{1,0:T(8,128)(2,1)S(1)} %bitcast.10), channel_id=1, source_target_pairs={{0,128},{128,0},{256,384},{384,256},{1,129},{129,1},{257,385},{385... | collective-permute-start | bytes 1179656 | tf_op jit(solution)/shard_map/ppermute | solution.py:216
  60.8 32.0 %collective-permute-start.12 = (bf16[128,1536]{1,0:T(8,128)(2,1)S(1)}, bf16[128,1536]{1,0:T(8,128)(2,1)S(1)}, u32[]{:S(2)}, u32[]{:S(2)}) collective-permute-start(bf16[128,1536]{1,0:T(8,128)(2,1)S(1)} %bitcast.11), channel_id=1, source_target_pairs={{0,256},{128,384},{256,0},{384,128},{1,257},{129,385},{257,1},{385... | collective-permute-start | bytes 1179656 | tf_op jit(solution)/shard_map/ppermute | solution.py:216
  63.3 30.3 %collective-permute-start.13 = (bf16[128,1536]{1,0:T(8,128)(2,1)S(1)}, bf16[128,1536]{1,0:T(8,128)(2,1)S(1)}, u32[]{:S(2)}, u32[]{:S(2)}) collective-permute-start(bf16[128,1536]{1,0:T(8,128)(2,1)S(1)} %bitcast.12), channel_id=1, source_target_pairs={{0,384},{128,256},{256,128},{384,0},{1,385},{129,257},{257,129},{3... | collective-permute-start | bytes 1179656 | tf_op jit(solution)/shard_map/ppermute | solution.py:216
  72.4 10.6 %collective-permute-start.7 = (bf16[2,4,32,256]{3,2,1,0:T(8,128)(2,1)S(1)}, bf16[2,4,32,256]{3,2,1,0:T(8,128)(2,1)S(1)}, u32[]{:S(2)}, u32[]{:S(2)}) collective-permute-start(bf16[2,4,32,256]{3,2,1,0:T(8,128)(2,1)S(1)} %shard_map.105.refs_0_), channel_id=1, source_target_pairs={{0,8},{2,10},{4,12},{6,14},{8,0},{10,2},{12,4},{14,6},{1,9},{3,11}... | collective-permute-start | bytes 393224 | tf_op jit(solution)/shard_map/ppermute | solution.py:216
  75.8 9.3 %collective-permute-start.8 = (bf16[2,4,32,256]{3,2,1,0:T(8,128)(2,1)S(1)}, bf16[2,4,32,256]{3,2,1,0:T(8,128)(2,1)S(1)}, u32[]{:S(2)}, u32[]{:S(2)}) collective-permute-start(bf16[2,4,32,256]{3,2,1,0:T(8,128)(2,1)S(1)} %shard_map.105.refs_0_), channel_id=1, source_target_pairs={{0,10},{2,8},{4,14},{6,12},{8,2},{10,0},{12,6},{14,4},{1,11},{3,9}... | collective-permute-start | bytes 393224 | tf_op jit(solution)/shard_map/ppermute | solution.py:216
  83.1 7.9 %collective-permute-start.9 = (bf16[2,4,32,256]{3,2,1,0:T(8,128)(2,1)S(1)}, bf16[2,4,32,256]{3,2,1,0:T(8,128)(2,1)S(1)}, u32[]{:S(2)}, u32[]{:S(2)}) collective-permute-start(bf16[2,4,32,256]{3,2,1,0:T(8,128)(2,1)S(1)} %shard_map.105.refs_0_), channel_id=1, source_target_pairs={{0,12},{2,14},{4,8},{6,10},{8,4},{10,6},{12,0},{14,2},{1,13},{3,15... | collective-permute-start | bytes 393224 | tf_op jit(solution)/shard_map/ppermute | solution.py:216
  97.1 55.5 %all-to-all-start.2 = ((bf16[64,16,512]{2,1,0:T(8,128)(2,1)}), bf16[64,16,512]{2,1,0:T(8,128)(2,1)S(1)}, u32[]{:S(2)}, u32[]{:S(2)}) async-start(bf16[64,16,512]{2,1,0:T(8,128)(2,1)} %bitcast.9), calls=%async_computation.2 | async-start | bytes 2097152 | tf_op jit(solution)/shard_map/all_to_all | solution.py:37
  109.3 19.0 %collective-permute-start.14 = (bf16[8,2,4,32,256]{4,3,2,1,0:T(8,128)(2,1)}, bf16[8,2,4,32,256]{4,3,2,1,0:T(8,128)(2,1)S(1)}, u32[]{:S(2)}, u32[]{:S(2)}) collective-permute-start(bf16[8,2,4,32,256]{4,3,2,1,0:T(8,128)(2,1)} %copy-done), channel_id=1, source_target_pairs={{0,32},{32,0},{64,96},{96,64},{1,33},{33,1},{65,97},{97,65},{2,34}... | collective-permute-start | bytes 3145736 | tf_op jit(solution)/shard_map/ppermute | solution.py:216
  112.0 39.6 %collective-permute-start.15 = (bf16[8,2,4,32,256]{4,3,2,1,0:T(8,128)(2,1)}, bf16[8,2,4,32,256]{4,3,2,1,0:T(8,128)(2,1)S(1)}, u32[]{:S(2)}, u32[]{:S(2)}) collective-permute-start(bf16[8,2,4,32,256]{4,3,2,1,0:T(8,128)(2,1)} %copy-done), channel_id=1, source_target_pairs={{0,64},{32,96},{64,0},{96,32},{1,65},{33,97},{65,1},{97,33},{2,66}... | collective-permute-start | bytes 3145736 | tf_op jit(solution)/shard_map/ppermute | solution.py:216
  116.3 36.2 %collective-permute-start.16 = (bf16[8,2,4,32,256]{4,3,2,1,0:T(8,128)(2,1)}, bf16[8,2,4,32,256]{4,3,2,1,0:T(8,128)(2,1)}, u32[]{:S(2)}, u32[]{:S(2)}) collective-permute-start(bf16[8,2,4,32,256]{4,3,2,1,0:T(8,128)(2,1)} %copy-done), channel_id=1, source_target_pairs={{0,96},{32,64},{64,32},{96,0},{1,97},{33,65},{65,33},{97,1},{2,98}... | collective-permute-start | bytes 3145736 | tf_op jit(solution)/shard_map/ppermute | solution.py:216
  152.9 8.2 %collective-permute-start.17 = (f32[8,128]{1,0:T(8,128)S(1)}, f32[8,128]{1,0:T(8,128)S(1)}, u32[]{:S(2)}, u32[]{:S(2)}) collective-permute-start(f32[8,128]{1,0:T(8,128)S(1)} %get-tuple-element.50.one_ref), channel_id=1, source_target_pairs={{0,1},{1,0},{2,3},{3,2},{4,5},{5,4},{6,7},{7,6},{8,9},{9,8},{10,11... | collective-permute-start | bytes 12296 | tf_op jit(solution)/shard_map/ppermute | solution.py:335
  161.7 38.7 %collective-permute-start.19 = (bf16[8,2,4,32,256]{4,3,2,1,0:T(8,128)(2,1)S(1)}, bf16[8,2,4,32,256]{4,3,2,1,0:T(8,128)(2,1)S(1)}, u32[]{:S(2)}, u32[]{:S(2)}) collective-permute-start(bf16[8,2,4,32,256]{4,3,2,1,0:T(8,128)(2,1)S(1)} %copy-done.1), channel_id=1, source_target_pairs={{0,16},{16,0},{1,17},{17,1},{2,18},{18,2},{3,19},{19,3},{4,20},{20... | collective-permute-start | bytes 3145736 | tf_op jit(solution)/shard_map/ppermute | solution.py:337
  180.0 20.4 %collective-permute-start.20 = (bf16[8,2,4,32,256]{4,3,2,1,0:T(8,128)(2,1)}, bf16[8,2,4,32,256]{4,3,2,1,0:T(8,128)(2,1)}, u32[]{:S(2)}, u32[]{:S(2)}) collective-permute-start(bf16[8,2,4,32,256]{4,3,2,1,0:T(8,128)(2,1)} %copy-done.12), channel_id=1, source_target_pairs={{0,16},{16,0},{1,17},{17,1},{2,18},{18,2},{3,19},{19,3},{4,20},{20... | collective-permute-start | bytes 3145736 | tf_op jit(solution)/shard_map/ppermute | solution.py:337
  181.9 18.5 %collective-permute-start.21 = (bf16[8,2,4,32,256]{4,3,2,1,0:T(8,128)(2,1)}, bf16[8,2,4,32,256]{4,3,2,1,0:T(8,128)(2,1)}, u32[]{:S(2)}, u32[]{:S(2)}) collective-permute-start(bf16[8,2,4,32,256]{4,3,2,1,0:T(8,128)(2,1)} %copy-done.13), channel_id=1, source_target_pairs={{0,16},{16,0},{1,17},{17,1},{2,18},{18,2},{3,19},{19,3},{4,20},{20... | collective-permute-start | bytes 3145736 | tf_op jit(solution)/shard_map/ppermute | solution.py:337
  184.4 16.1 %collective-permute-start.22 = (bf16[8,2,4,32,256]{4,3,2,1,0:T(8,128)(2,1)}, bf16[8,2,4,32,256]{4,3,2,1,0:T(8,128)(2,1)}, u32[]{:S(2)}, u32[]{:S(2)}) collective-permute-start(bf16[8,2,4,32,256]{4,3,2,1,0:T(8,128)(2,1)} %collective-permute-done.16.refs_3_), channel_id=1, source_target_pairs={{0,16},{16,0},{1,17},{17,1},{2,18},{18,2},{3,19},{19,3},{4,20},{20... | collective-permute-start | bytes 3145736 | tf_op jit(solution)/shard_map/ppermute | solution.py:337
  186.3 13.2 %all-to-all-start.3 = ((f32[8,8,128]{2,1,0:T(8,128)}), f32[8,8,128]{2,1,0:T(8,128)S(1)}, u32[]{:S(2)}, u32[]{:S(2)}) async-start(f32[8,8,128]{2,1,0:T(8,128)} %shard_map.109), calls=%async_computation.3 | async-start | bytes 65536 | tf_op jit(solution)/shard_map/all_to_all | solution.py:37
  200.4 29.8 %all-to-all-start.4 = ((bf16[32,16,640]{2,1,0:T(8,128)(2,1)}), bf16[32,16,640]{2,1,0:T(8,128)(2,1)S(1)}, u32[]{:S(2)}, u32[]{:S(2)}) async-start(bf16[32,16,640]{2,1,0:T(8,128)(2,1)} %shard_map.110), calls=%async_computation.4 | async-start | bytes 1310720 | tf_op jit(solution)/shard_map/all_to_all | solution.py:37
  (19 other events, 242.8 us)

commit v5 on v3

--- a/solution.py
+++ b/solution.py
@@ -35,10 +35,6 @@
 
 def exchange(x, axes):
     return lax.all_to_all(x, axes, split_axis=0, concat_axis=0, tiled=True)
-
-
-def copies_for(x, count):
-    return jnp.broadcast_to(x, (count, *x.shape))
 
 
 def rotation(positions):
@@ -128,32 +124,26 @@
     )(received, received)
 
 
-def backward_kernel(
-    core_ref, key_ref, own_ref, other_ref, x_ref, scale_ref, gain_ref, out_ref, held, cross
-):
+def backward_kernel(key_ref, weight_ref, x_ref, scale_ref, gain_ref, out_ref, held, cross):
     step = pl.program_id(0)
-    core = core_ref[0]
-    half = own_ref.shape[4]
-    width = 2 * half
-    first = step * own_ref.shape[2] * 2
+    deep, width = weight_ref.shape[2], weight_ref.shape[4]
 
     @pl.when(step == 0)
     def _():
         cross[...] = jnp.zeros_like(cross)
 
     total = jnp.zeros(cross.shape, f32)
-    for z in range(own_ref.shape[2]):
+    for z in range(deep):
         for yh in range(2):
-            block = first + z * 2 + yh
-            for side, ref in ((core, own_ref), (1 - core, other_ref)):
-                up = jnp.dot(key_ref[...], ref[yh, :, z].reshape(KV, half), preferred_element_type=f32)
-                for k in range(half // HEAD):
-                    group = block * (width // HEAD) + side * (half // HEAD) + k
-                    columns = pl.ds(pl.multiple_of(group * HEAD, HEAD), HEAD)
-                    inside = pl.ds(pl.multiple_of(side * half + k * HEAD, HEAD), HEAD)
-                    weighted = up[:, k * HEAD : (k + 1) * HEAD] * gain_ref[pl.ds(group, 1), :]
-                    held[block, :, inside] = weighted
-                    total += weighted * x_ref[:, columns].astype(f32)
+            block = (step * deep + z) * 2 + yh
+            up = jnp.dot(key_ref[...], weight_ref[yh, :, z].reshape(KV, width), preferred_element_type=f32)
+            for k in range(width // HEAD):
+                group = block * (width // HEAD) + k
+                columns = pl.ds(pl.multiple_of(group * HEAD, HEAD), HEAD)
+                inside = slice(k * HEAD, (k + 1) * HEAD)
+                weighted = up[:, inside] * gain_ref[pl.ds(group, 1), :]
+                held[block, :, inside] = weighted
+                total += weighted * x_ref[:, columns].astype(f32)
     cross[...] += total
 
     @pl.when(step == pl.num_programs(0) - 1)
@@ -166,36 +156,43 @@
             out_ref[:, part] = (scale * (held[t] - x * inner)).astype(bf16)
 
 
-def backward(core, keys, own, other, x, scale, gain):
+def backward(keys, weights, x, scale, gain):
     tokens = x.shape[0]
     width = 512
     deep = 2
     steps = 8 // deep
-    weights = pl.BlockSpec((2, 4, deep, 128, width // 2), lambda t, core: (0, 0, t, 0, 0))
-    whole = lambda a: pl.BlockSpec(a.shape, lambda t, core: (0, 0))
+    whole = lambda a: pl.BlockSpec(a.shape, lambda t: (0, 0))
     return pl.pallas_call(
         backward_kernel,
-        grid_spec=pltpu.PrefetchScalarGridSpec(
-            num_scalar_prefetch=1,
-            grid=(steps,),
-            in_specs=[whole(keys), weights, weights, whole(x), whole(scale), whole(gain)],
-            out_specs=pl.BlockSpec((tokens, D), lambda t, core: (0, 0)),
-            scratch_shapes=[pltpu.VMEM((D // width, tokens, width), f32), pltpu.VMEM((tokens, HEAD), f32)],
-        ),
+        grid=(steps,),
+        in_specs=[
+            whole(keys),
+            pl.BlockSpec((2, 4, deep, 128, width), lambda t: (0, 0, t, 0, 0)),
+            whole(x),
+            whole(scale),
+            whole(gain),
+        ],
+        out_specs=pl.BlockSpec((tokens, D), lambda t: (0, 0)),
+        scratch_shapes=[pltpu.VMEM((D // width, tokens, width), f32), pltpu.VMEM((tokens, HEAD), f32)],
         out_shape=jax.ShapeDtypeStruct((tokens, D), bf16),
         compiler_params=pltpu.CompilerParams(vmem_limit_bytes=56 * 1024 * 1024),
         cost_estimate=pl.CostEstimate(
             flops=2 * tokens * KV * D, bytes_accessed=12 * 1024 * 1024, transcendentals=0
         ),
-    )(core, keys, own, other, x, scale, gain)
-
-
-def local_call(kernel, outs, *args):
+    )(keys, weights, x, scale, gain)
+
+
+def local_call(kernel, outs, *args, vmem=32):
     return pl.pallas_call(
         kernel,
         out_shape=[jax.ShapeDtypeStruct(shape, kind) for shape, kind in outs],
-        compiler_params=pltpu.CompilerParams(vmem_limit_bytes=32 * 1024 * 1024),
+        compiler_params=pltpu.CompilerParams(vmem_limit_bytes=vmem * 1024 * 1024),
     )(*args)
+
+
+def from_others(x, axis):
+    count = lax.axis_size(axis)
+    return [lax.ppermute(x, axis, [(i, i ^ k) for i in range(count)]) for k in range(1, count)]
 
 
 def add_pieces_kernel(pieces_ref, piece_ref, square_ref):
@@ -206,39 +203,32 @@
 
 
 def add_pieces(pieces):
-    return local_call(add_pieces_kernel, [(pieces.shape[1:], f32), ((8, 128), f32)], pieces)
-
-
-def add_pair_kernel(one_ref, two_ref, out_ref):
-    out_ref[...] = jnp.broadcast_to(one_ref[...] + two_ref[...], out_ref.shape)
-
-
-def add_pair(one, two):
-    return local_call(add_pair_kernel, [((8, 8, 128), f32)], one, two)[0]
-
-
-def late_kernel(squares_ref, shard_ref, out_ref):
-    out_ref[:, :, :512] = jnp.broadcast_to(shard_ref[...].astype(bf16), (32, 16, 512))
-    rest = jnp.sum(squares_ref[...], axis=0)
-    lane = lax.broadcasted_iota(jnp.int32, (8, 128), 1)
-    beside = jnp.zeros((8, 128), f32)
+    return local_call(add_pieces_kernel, [(pieces.shape[1:], f32), ((N_PLANE, 128), f32)], pieces)
+
+
+def late_kernel(squares_ref, s0_ref, s1_ref, s2_ref, s3_ref, out_ref):
+    for k, ref in enumerate((s0_ref, s1_ref, s2_ref, s3_ref)):
+        rows = slice(k * 16, (k + 1) * 16)
+        out_ref[:, rows, :512] = jnp.broadcast_to(ref[...].astype(bf16), (N_GROUP, 16, 512))
+    rest = jnp.broadcast_to(jnp.sum(squares_ref[...], axis=0, keepdims=True), (64, 128))
+    lane = lax.broadcasted_iota(jnp.int32, (64, 128), 1)
+    beside = jnp.zeros((64, 128), f32)
     for k in range(3):
         term = rest.astype(bf16).astype(f32)
         rest = rest - term
         beside = jnp.where(lane == k, term, beside)
-    beside = jnp.concatenate([beside, beside], axis=0).astype(bf16)
-    out_ref[:, :, 512:] = jnp.broadcast_to(beside, (32, 16, 128))
-
-
-def late_rows(squares, shard):
-    return local_call(late_kernel, [((32, 16, 640), bf16)], squares, shard)[0]
+    out_ref[:, :, 512:] = jnp.broadcast_to(beside.astype(bf16), (N_GROUP, 64, 128))
+
+
+def late_rows(squares, shards):
+    return local_call(late_kernel, [((N_GROUP, 64, 640), bf16)], squares, *shards)[0]
 
 
 def update_kernel(
-    place_ref, gathered_ref, own_ref, other_ref, m0_ref, m1_ref, m2_ref, m3_ref, shard_ref, first_ref, second_ref,
+    place_ref, gathered_ref, weight_ref, m0_ref, m1_ref, m2_ref, m3_ref, shard_ref, first_ref, second_ref,
     weight_out, first_out, second_out,
 ):
-    terms = jnp.sum(gathered_ref[:, :, 512:].astype(f32), axis=0)
+    terms = jnp.sum(gathered_ref[:, :16, 512:].astype(f32), axis=0)
     total_square = jnp.sum(terms[:1], axis=1, keepdims=True)
     clip_limit = math.sqrt(KV * D)
     clip_factor = jnp.minimum(1.0, clip_limit / (jnp.sqrt(total_square) + 1e-06))
@@ -253,22 +243,17 @@
     new_first, new_second = moments(shard_ref[...], first_ref[...], second_ref[...])
     first_out[...] = new_first
     second_out[...] = new_second
-    core, yl = place_ref[0], place_ref[1]
-    half = own_ref.shape[1]
     for k, ref in enumerate((m0_ref, m1_ref, m2_ref, m3_ref)):
-        block = yl ^ k
+        block = place_ref[0] ^ k
         for r in range(8):
             part = slice(r * 16, (r + 1) * 16)
             rows = pl.ds(pl.multiple_of(block * 128 + r * 16, 16), 16)
-            gradient = gathered_ref[block * 8 + r, :, :512].astype(f32)
+            gradient = gathered_ref[r, k * 16 : (k + 1) * 16, :512].astype(f32)
             new_first, new_second = moments(gradient, ref[part, :512].astype(f32), ref[part, 512:].astype(f32))
-            step = learn_rate * new_first / (jnp.sqrt(new_second) + eps_adam)
-            own = own_ref[rows, :].astype(f32)
-            other = other_ref[rows, :].astype(f32)
-            for side in range(2):
-                inside = slice(side * half, (side + 1) * half)
-                weight = jnp.where(core == side, own, other)
-                weight_out[rows, inside] = (weight * (1.0 - learn_rate * decay_rate) - step[:, inside]).astype(bf16)
+            weight_out[rows, :] = (
+                weight_ref[rows, :].astype(f32) * (1.0 - learn_rate * decay_rate)
+                - learn_rate * new_first / (jnp.sqrt(new_second) + eps_adam)
+            ).astype(bf16)
 
 
 def update(place, *args):
@@ -289,19 +274,19 @@
 
 
 def body(norm_input, key_grad, positions, norm_gain, key_weight, first_moment, second_moment):
-    core = lax.axis_index("c")
-    state = local_call(state_kernel, [((N_GROUP, 16, 1536), bf16)], key_weight, first_moment, second_moment)[0]
+    state = local_call(
+        state_kernel, [((N_GROUP, 16, 1536), bf16)], key_weight, first_moment, second_moment, vmem=56
+    )[0]
     state = exchange(state, GROUP).reshape(N_GROUP * 16, 1536)
     cosine, sine = rotation(positions)
     send, keys, scale, gain = prepare(norm_input, key_grad, cosine, sine, norm_gain.reshape(D // HEAD, HEAD))
     send, state = lax.optimization_barrier((send, state))
 
-    half = lax.dynamic_slice_in_dim(state, core * 256, 256, 1)
-    own = lax.all_gather(half, ("yh", "yl", "z"), axis=0, tiled=True).reshape(2, 4, 8, 128, 256)
+    weights = lax.all_gather(state[:, :512], ("yh", "yl", "z"), axis=0, tiled=True).reshape(2, 4, 8, 128, 512)
 
     received = exchange(send, GROUP)
-    moments = [state[:, 512:]]
-    moments += [lax.ppermute(moments[0], "yl", [(i, i ^ k) for i in range(4)]) for k in (1, 2, 3)]
+    moments = state[:, 512:]
+    moments = [moments, *from_others(moments, "yl")]
     received, *moments = lax.optimization_barrier((received, *moments))
     partial = product(received).reshape(N_PLANE, 16, 512)
     pieces = exchange(partial, PLANE)
@@ -309,19 +294,17 @@
 
     swap = [(i * 8 + k, k * 8 + i) for i in range(8) for k in range(8)]
     grad_shard = lax.ppermute(piece, ("x", "c", "z"), swap)
-    square = add_pair(square, lax.ppermute(square, "yh", [(0, 1), (1, 0)]))
-    own, _ = lax.optimization_barrier((own, square))
-    other = lax.ppermute(own, "c", [(0, 1), (1, 0)])
-    late = late_rows(exchange(square, "z"), grad_shard)
-    late, own, other = lax.optimization_barrier((late, own, other))
-    gathered = exchange(late, DP)
-    input_grad = backward(core.astype(jnp.int32).reshape(1), keys, own, other, norm_input, scale, gain)
-    own, other, input_grad = lax.optimization_barrier((own, other, input_grad))
-    z, yh = lax.axis_index("z"), lax.axis_index("yh")
-    weights = [lax.dynamic_slice(w, (yh, 0, z, 0, 0), (1, 4, 1, 128, 256)).reshape(KV, 256) for w in (own, other)]
-    place = jnp.stack([core, lax.axis_index("yl")]).astype(jnp.int32)
+    shards = [grad_shard, *from_others(grad_shard, "yl")]
+    late = late_rows(exchange(square, PLANE), shards)
+    late, weights = lax.optimization_barrier((late, weights))
+    gathered = exchange(late, GROUP)
+    input_grad = backward(keys, weights, norm_input, scale, gain)
+    weights, input_grad = lax.optimization_barrier((weights, input_grad))
+    at = (lax.axis_index("yh"), 0, lax.axis_index("z"), 0, 0)
+    weight = lax.dynamic_slice(weights, at, (1, 4, 1, 128, 512)).reshape(KV, 512)
+    place = lax.axis_index("yl").astype(jnp.int32).reshape(1)
     new_weight, new_first, new_second = update(
-        place, gathered, *weights, *moments, grad_shard, first_moment, second_moment
+        place, gathered, weight, *moments, grad_shard, first_moment, second_moment
     )
     return (input_grad, new_weight, new_first, new_second)
 

time: 192 us -> 178 us (0.927)
  waiting for transfers between devices: 46.9 us -> 36.3 us
  local copies, waits for them, and re-layouts: 7.12 us -> 4.96 us
    all_to_all x4, waiting for transfers between devices: 23.3 us -> 14.9 us  [exchange(): return lax.all_to_all(x, axes, split_axis=0, concat_axis=0, tiled=True)]
    ppermute x1, starting transfers between devices: 3.81 us -> 9.18 us  [body(): grad_shard = lax.ppermute(piece, ('x', 'c', 'z'), swap)]
    all_to_all x4, starting transfers between devices: 30.5 us -> 26.3 us  [exchange(): return lax.all_to_all(x, axes, split_axis=0, concat_axis=0, tiled=True)]
    all_gather x1, waiting for transfers between devices: 4.84 us -> 2.54 us  [body(): lax.all_gather(state[:, :512], ('yh', 'yl', 'z'), axis=0, tiled=True)]
    unnamed x24 -> x18, local copies, waits for them, and re-layouts: 4.42 us -> 2.19 us
    ppermute x5 -> x6, waiting for transfers between devices: 16.7 us -> 18.8 us  [from_others(): lax.ppermute(x, axis, [(i, i ^ k) for i in range(count)])]
    ppermute x1, waiting for transfers between devices: 1.97 us -> 0.01 us  [body(): grad_shard = lax.ppermute(piece, ('x', 'c', 'z'), swap)]
    ppermute x5 -> x6, starting transfers between devices: 19.9 us -> 18.6 us  [from_others(): lax.ppermute(x, axis, [(i, i ^ k) for i in range(count)])]
  transfers between devices with their start and end apart: 11 -> 12, of which waited for: 9 -> 8; matrix products, arithmetic and copies ran while one was open for 2% -> 2% of each run, Pallas kernels for 9% -> 9%
where the time goes in v5:
time: 178 us; the launch traced here: 177 us
  starting transfers between devices  54.1 us (30%)
  blocking collectives  46.2 us (26%)
  waiting for transfers between devices  36.3 us (20%)
  Pallas kernels  19.8 us (11%)
  between operations  14.2 us (8%)
  local copies, waits for them, and re-layouts  4.96 us (3%)
    all_to_all x1, blocking collectives, exchange(): return lax.all_to_all(x, axes, split_axis=0, concat_axis=0, tiled=True)  46.2 us
    all_to_all x4, starting transfers between devices, exchange(): return lax.all_to_all(x, axes, split_axis=0, concat_axis=0, tiled=True)  26.3 us
    ppermute x6, waiting for transfers between devices, from_others(): lax.ppermute(x, axis, [(i, i ^ k) for i in range(count)])  18.8 us
    ppermute x6, starting transfers between devices, from_others(): lax.ppermute(x, axis, [(i, i ^ k) for i in range(count)])  18.6 us
    all_to_all x4, waiting for transfers between devices, exchange(): return lax.all_to_all(x, axes, split_axis=0, concat_axis=0, tiled=True)  14.9 us
    ppermute x1, starting transfers between devices, body(): grad_shard = lax.ppermute(piece, ('x', 'c', 'z'), swap)  9.18 us
    pallas_call x1, Pallas kernels, backward(): pl.pallas_call(backward_kernel, grid=(steps,), in_specs=[whole(keys), pl....  8.05 us
    pallas_call x1, Pallas kernels, prepare(): pl.pallas_call(prepare_kernel, grid=(tokens // tile,), in_specs=[pl.Block...  4.75 us
  transfers between devices with their start and end apart: 12, of which 8 were waited for; matrix products, arithmetic and copies ran while one was open for 2% of the time, Pallas kernels for 9%

profile of v5, /device:TPU:1, one launch (start us, length us, event | category | flops | bytes accessed | tf_op | source)
XLA Modules:
  0.0 177.1 jit_solution(8853589518013263718)
XLA Ops:
  8.7 10.2 %all-to-all-start = ((bf16[8,16,1536]{2,1,0:T(8,128)(2,1)}), bf16[8,16,1536]{2,1,0:T(8,128)(2,1)S(1)}, u32[]{:S(2)}, u32[]{:S(2)}) async-start(bf16[8,16,1536]{2,1,0:T(8,128)(2,1)} %shard_map.103), calls=%async_computation | async-start | bytes 786432 | tf_op jit(solution)/shard_map/all_to_all | solution.py:37
  20.6 4.8 %shard_map.102 = (bf16[8,128,1536]{2,1,0:T(8,128)(2,1)}, bf16[128,512]{1,0:T(8,128)(2,1)}, f32[128,128]{1,0:T(8,128)}, f32[64,128]{1,0:T(8,128)}) custom-call(bf16[128,8192]{1,0:T(8,128)(2,1)} %x_ref.3, bf16[128,512]{1,0:T(8,128)(2,1)} %key_ref.1, f32[128,64]{1,0:T(8,128)} %get-tuple-element.45.cos_ref, f32[128,64]{1,0:T(8,128)} %get-tuple-element.44.sin_ref, ...), custom_call_target="tpu_custom_call" | custom-call | flops 8388608 | bytes 6291456 | tf_op jit(solution)/shard_map/pallas_call | solution.py:73
  25.4 1.7 all-to-all-done
  27.9 4.4 %all-to-all-start.1 = ((bf16[8,128,1536]{2,1,0:T(8,128)(2,1)}), bf16[8,128,1536]{2,1,0:T(8,128)(2,1)S(1)}, u32[]{:S(2)}, u32[]{:S(2)}) async-start(bf16[8,128,1536]{2,1,0:T(8,128)(2,1)} %get-tuple-element.25), calls=%async_computation.1 | async-start | bytes 6291456 | tf_op jit(solution)/shard_map/all_to_all | solution.py:37
  33.2 1.9 %collective-permute-start = (bf16[128,1024]{1,0:T(8,128)(2,1)S(1)}, bf16[128,1024]{1,0:T(8,128)(2,1)S(1)}, u32[]{:S(2)}, u32[]{:S(2)}) collective-permute-start(bf16[128,1024]{1,0:T(8,128)(2,1)S(1)} %slice.6.m0_ref), channel_id=1, source_target_pairs={{0,128},{128,0},{256,384},{384,256},{1,129},{129,1},{257,385},{385... | collective-permute-start | bytes 786440 | tf_op jit(solution)/shard_map/ppermute | solution.py:195
  35.2 1.9 %collective-permute-start.1 = (bf16[128,1024]{1,0:T(8,128)(2,1)S(1)}, bf16[128,1024]{1,0:T(8,128)(2,1)S(1)}, u32[]{:S(2)}, u32[]{:S(2)}) collective-permute-start(bf16[128,1024]{1,0:T(8,128)(2,1)S(1)} %slice.6.m0_ref), channel_id=1, source_target_pairs={{0,256},{128,384},{256,0},{384,128},{1,257},{129,385},{257,1},{385... | collective-permute-start | bytes 786440 | tf_op jit(solution)/shard_map/ppermute | solution.py:195
  37.1 5.5 %collective-permute-start.2 = (bf16[128,1024]{1,0:T(8,128)(2,1)S(1)}, bf16[128,1024]{1,0:T(8,128)(2,1)S(1)}, u32[]{:S(2)}, u32[]{:S(2)}) collective-permute-start(bf16[128,1024]{1,0:T(8,128)(2,1)S(1)} %slice.6.m0_ref), channel_id=1, source_target_pairs={{0,384},{128,256},{256,128},{384,0},{1,385},{129,257},{257,129},{3... | collective-permute-start | bytes 786440 | tf_op jit(solution)/shard_map/ppermute | solution.py:195
  42.6 1.7 collective-permute-done.m1_ref
  44.9 13.6 %collective-permute-done.1.m2_ref = bf16[128,1024]{1,0:T(8,128)(2,1)S(1)} collective-permute-done((bf16[128,1024]{1,0:T(8,128)(2,1)S(1)}, bf16[128,1024]{1,0:T(8,128)(2,1)S(1)}, u32[]{:S(2)}, u32[]{:S(2)}) %collective-permute-start.1) | collective-permute-done | bytes 262176 | tf_op jit(solution)/shard_map/ppermute | solution.py:195
  60.0 9.9 %all-to-all-done.1.key_ref.normed_ref = bf16[8,128,1536]{2,1,0:T(8,128)(2,1)S(1)} async-done(((bf16[8,128,1536]{2,1,0:T(8,128)(2,1)}), bf16[8,128,1536]{2,1,0:T(8,128)(2,1)S(1)}, u32[]{:S(2)}, u32[]{:S(2)}) %all-to-all-start.1) | async-done | bytes 3145760 | tf_op jit(solution)/shard_map/all_to_all | solution.py:37
  69.9 1.8 %shard_map.104 = bf16[32,2,16,512]{3,2,1,0:T(8,128)(2,1)S(1)} custom-call(bf16[8,128,1536]{2,1,0:T(8,128)(2,1)S(1)} %all-to-all-done.1.key_ref.normed_ref, bf16[8,128,1536]{2,1,0:T(8,128)(2,1)S(1)} %all-to-all-done.1.key_ref.normed_ref), custom_call_target="tpu_custom_call" | custom-call | flops 1073741824 | bytes 4194304 | tf_op jit(solution)/shard_map/pallas_call | solution.py:111
  71.6 46.2 %all_to_all.31.pieces_ref = bf16[64,16,512]{2,1,0:T(8,128)(2,1)S(1)} all-to-all(bf16[64,16,512]{2,1,0:T(8,128)(2,1)S(1)} %bitcast.10), channel_id=1, replica_groups=mesh['yl'=4,'x'=4,'c'=2,'z'=8,'yh'=2] {'yl','z','yh'}, dimensions={0} | all-to-all | bytes 2097152 | tf_op jit(solution)/shard_map/all_to_all | solution.py:37
  118.7 9.2 %collective-permute-start.3 = (f32[16,512]{1,0:T(8,128)S(1)}, f32[16,512]{1,0:T(8,128)S(1)}, u32[]{:S(2)}, u32[]{:S(2)}) collective-permute-start(f32[16,512]{1,0:T(8,128)S(1)} %get-tuple-element.29), channel_id=1, source_target_pairs={{0,0},{2,16},{4,32},{6,48},{8,64},{10,80},{12,96},{14,112},{16,2},... | collective-permute-start | bytes 98312 | tf_op jit(solution)/shard_map/ppermute | solution.py:296
  127.9 6.9 %all-to-all-start.3 = ((f32[64,1,128]{2,1,0:T(1,128)}), f32[64,1,128]{2,1,0:T(1,128)S(1)}, u32[]{:S(2)}, u32[]{:S(2)}) async-start(f32[64,1,128]{2,1,0:T(1,128)} %bitcast.4), calls=%async_computation.3 | async-start | bytes 65536 | tf_op jit(solution)/shard_map/all_to_all | solution.py:37
  134.8 2.9 %collective-permute-start.4 = (f32[16,512]{1,0:T(8,128)S(1)}, f32[16,512]{1,0:T(8,128)S(1)}, u32[]{:S(2)}, u32[]{:S(2)}) collective-permute-start(f32[16,512]{1,0:T(8,128)S(1)} %collective-permute-done.3.s0_ref.shard_ref), channel_id=1, source_target_pairs={{0,128},{128,0},{256,384},{384,256},{1,129},{129,1},{257,385},{385... | collective-permute-start | bytes 98312 | tf_op jit(solution)/shard_map/ppermute | solution.py:195
  137.8 4.2 %collective-permute-start.5 = (f32[16,512]{1,0:T(8,128)S(1)}, f32[16,512]{1,0:T(8,128)S(1)}, u32[]{:S(2)}, u32[]{:S(2)}) collective-permute-start(f32[16,512]{1,0:T(8,128)S(1)} %collective-permute-done.3.s0_ref.shard_ref), channel_id=1, source_target_pairs={{0,256},{128,384},{256,0},{384,128},{1,257},{129,385},{257,1},{385... | collective-permute-start | bytes 98312 | tf_op jit(solution)/shard_map/ppermute | solution.py:195
  142.0 2.2 %collective-permute-start.6 = (f32[16,512]{1,0:T(8,128)S(1)}, f32[16,512]{1,0:T(8,128)S(1)}, u32[]{:S(2)}, u32[]{:S(2)}) collective-permute-start(f32[16,512]{1,0:T(8,128)S(1)} %collective-permute-done.3.s0_ref.shard_ref), channel_id=1, source_target_pairs={{0,384},{128,256},{256,128},{384,0},{1,385},{129,257},{257,129},{3... | collective-permute-start | bytes 98312 | tf_op jit(solution)/shard_map/ppermute | solution.py:195
  144.1 1.6 all-to-all-done.3
  145.7 3.6 %collective-permute-done.6.s3_ref = f32[16,512]{1,0:T(8,128)S(1)} collective-permute-done((f32[16,512]{1,0:T(8,128)S(1)}, f32[16,512]{1,0:T(8,128)S(1)}, u32[]{:S(2)}, u32[]{:S(2)}) %collective-permute-start.6) | collective-permute-done | bytes 32800 | tf_op jit(solution)/shard_map/ppermute | solution.py:195
  150.3 2.5 %all-gather.2.cloned.1.call-done = bf16[8192,512]{1,0:T(8,128)(2,1)} async-done(((bf16[128,512]{1,0:T(8,128)(2,1)}), bf16[8192,512]{1,0:T(8,128)(2,1)}) %all-gather.2.cloned.1.call-update) | async-done | bytes 8388624 | tf_op jit(solution)/shard_map/all_gather | solution.py:285
  152.8 4.8 %all-to-all-start.4 = ((bf16[8,64,640]{2,1,0:T(8,128)(2,1)}), bf16[8,64,640]{2,1,0:T(8,128)(2,1)S(1)}, u32[]{:S(2)}, u32[]{:S(2)}) async-start(bf16[8,64,640]{2,1,0:T(8,128)(2,1)} %shard_map.106), calls=%async_computation.4 | async-start | bytes 1310720 | tf_op jit(solution)/shard_map/all_to_all | solution.py:37
  157.6 8.0 %shard_map.107 = bf16[128,8192]{1,0:T(8,128)(2,1)} custom-call(bf16[128,512]{1,0:T(8,128)(2,1)} %get-tuple-element.31.key_ref, bf16[2,4,8,128,512]{4,3,2,1,0:T(8,128)(2,1)} %bitcast.13, bf16[128,8192]{1,0:T(8,128)(2,1)} %x_ref.3, f32[128,128]{1,0:T(8,128)} %get-tuple-element.32.scale_ref, f32[64,128]{1,0:T(8,128)} %get-tuple-element.33.gain_ref), custom_call_target="tpu_custom_call" | custom-call | flops 1073741824 | bytes 12582912 | tf_op jit(solution)/shard_map/pallas_call | solution.py:165
  166.7 1.7 all-to-all-done.4.gathered_ref
  168.5 1.8 shard_map.108
  (33 shorter events, 10.1 us)
Async XLA Ops:
  8.7 18.3 %all-to-all-start = ((bf16[8,16,1536]{2,1,0:T(8,128)(2,1)}), bf16[8,16,1536]{2,1,0:T(8,128)(2,1)S(1)}, u32[]{:S(2)}, u32[]{:S(2)}) async-start(bf16[8,16,1536]{2,1,0:T(8,128)(2,1)} %shard_map.103), calls=%async_computation | async-start | bytes 786432 | tf_op jit(solution)/shard_map/all_to_all | solution.py:37
  19.0 133.8 %all-gather.2.cloned.1.call-start = ((), (), s32[]{:S(2)}) async-start(), calls=%async_computation.5 | async-start | bytes 8519680 | tf_op jit(solution)/shard_map/all_gather | solution.py:285
  27.1 0.8 copy-start.8
  27.9 42.0 %all-to-all-start.1 = ((bf16[8,128,1536]{2,1,0:T(8,128)(2,1)}), bf16[8,128,1536]{2,1,0:T(8,128)(2,1)S(1)}, u32[]{:S(2)}, u32[]{:S(2)}) async-start(bf16[8,128,1536]{2,1,0:T(8,128)(2,1)} %get-tuple-element.25), calls=%async_computation.1 | async-start | bytes 6291456 | tf_op jit(solution)/shard_map/all_to_all | solution.py:37
  33.2 11.0 %collective-permute-start = (bf16[128,1024]{1,0:T(8,128)(2,1)S(1)}, bf16[128,1024]{1,0:T(8,128)(2,1)S(1)}, u32[]{:S(2)}, u32[]{:S(2)}) collective-permute-start(bf16[128,1024]{1,0:T(8,128)(2,1)S(1)} %slice.6.m0_ref), channel_id=1, source_target_pairs={{0,128},{128,0},{256,384},{384,256},{1,129},{129,1},{257,385},{385... | collective-permute-start | bytes 786440 | tf_op jit(solution)/shard_map/ppermute | solution.py:195
  35.2 23.4 %collective-permute-start.1 = (bf16[128,1024]{1,0:T(8,128)(2,1)S(1)}, bf16[128,1024]{1,0:T(8,128)(2,1)S(1)}, u32[]{:S(2)}, u32[]{:S(2)}) collective-permute-start(bf16[128,1024]{1,0:T(8,128)(2,1)S(1)} %slice.6.m0_ref), channel_id=1, source_target_pairs={{0,256},{128,384},{256,0},{384,128},{1,257},{129,385},{257,1},{385... | collective-permute-start | bytes 786440 | tf_op jit(solution)/shard_map/ppermute | solution.py:195
  37.1 22.1 %collective-permute-start.2 = (bf16[128,1024]{1,0:T(8,128)(2,1)S(1)}, bf16[128,1024]{1,0:T(8,128)(2,1)S(1)}, u32[]{:S(2)}, u32[]{:S(2)}) collective-permute-start(bf16[128,1024]{1,0:T(8,128)(2,1)S(1)} %slice.6.m0_ref), channel_id=1, source_target_pairs={{0,384},{128,256},{256,128},{384,0},{1,385},{129,257},{257,129},{3... | collective-permute-start | bytes 786440 | tf_op jit(solution)/shard_map/ppermute | solution.py:195
  44.2 0.7 copy-start
  58.5 0.7 copy-start.2
  59.2 0.7 copy-start.4
  118.7 16.1 %collective-permute-start.3 = (f32[16,512]{1,0:T(8,128)S(1)}, f32[16,512]{1,0:T(8,128)S(1)}, u32[]{:S(2)}, u32[]{:S(2)}) collective-permute-start(f32[16,512]{1,0:T(8,128)S(1)} %get-tuple-element.29), channel_id=1, source_target_pairs={{0,0},{2,16},{4,32},{6,48},{8,64},{10,80},{12,96},{14,112},{16,2},... | collective-permute-start | bytes 98312 | tf_op jit(solution)/shard_map/ppermute | solution.py:296
  127.9 17.8 %all-to-all-start.3 = ((f32[64,1,128]{2,1,0:T(1,128)}), f32[64,1,128]{2,1,0:T(1,128)S(1)}, u32[]{:S(2)}, u32[]{:S(2)}) async-start(f32[64,1,128]{2,1,0:T(1,128)} %bitcast.4), calls=%async_computation.3 | async-start | bytes 65536 | tf_op jit(solution)/shard_map/all_to_all | solution.py:37
  134.8 10.9 %collective-permute-start.4 = (f32[16,512]{1,0:T(8,128)S(1)}, f32[16,512]{1,0:T(8,128)S(1)}, u32[]{:S(2)}, u32[]{:S(2)}) collective-permute-start(f32[16,512]{1,0:T(8,128)S(1)} %collective-permute-done.3.s0_ref.shard_ref), channel_id=1, source_target_pairs={{0,128},{128,0},{256,384},{384,256},{1,129},{129,1},{257,385},{385... | collective-permute-start | bytes 98312 | tf_op jit(solution)/shard_map/ppermute | solution.py:195
  137.8 7.9 %collective-permute-start.5 = (f32[16,512]{1,0:T(8,128)S(1)}, f32[16,512]{1,0:T(8,128)S(1)}, u32[]{:S(2)}, u32[]{:S(2)}) collective-permute-start(f32[16,512]{1,0:T(8,128)S(1)} %collective-permute-done.3.s0_ref.shard_ref), channel_id=1, source_target_pairs={{0,256},{128,384},{256,0},{384,128},{1,257},{129,385},{257,1},{385... | collective-permute-start | bytes 98312 | tf_op jit(solution)/shard_map/ppermute | solution.py:195
  142.0 7.3 %collective-permute-start.6 = (f32[16,512]{1,0:T(8,128)S(1)}, f32[16,512]{1,0:T(8,128)S(1)}, u32[]{:S(2)}, u32[]{:S(2)}) collective-permute-start(f32[16,512]{1,0:T(8,128)S(1)} %collective-permute-done.3.s0_ref.shard_ref), channel_id=1, source_target_pairs={{0,384},{128,256},{256,128},{384,0},{1,385},{129,257},{257,129},{3... | collective-permute-start | bytes 98312 | tf_op jit(solution)/shard_map/ppermute | solution.py:195
  152.8 15.7 %all-to-all-start.4 = ((bf16[8,64,640]{2,1,0:T(8,128)(2,1)}), bf16[8,64,640]{2,1,0:T(8,128)(2,1)S(1)}, u32[]{:S(2)}, u32[]{:S(2)}) async-start(bf16[8,64,640]{2,1,0:T(8,128)(2,1)} %shard_map.106), calls=%async_computation.4 | async-start | bytes 1310720 | tf_op jit(solution)/shard_map/all_to_all | solution.py:37
  157.6 10.9 %copy-start.1 = (bf16[128,1024]{1,0:T(8,128)(2,1)S(1)}, bf16[128,1024]{1,0:T(8,128)(2,1)}, u32[]{:S(2)}) copy-start(bf16[128,1024]{1,0:T(8,128)(2,1)} %copy-done) | copy-start | bytes 786436
  157.6 10.9 %copy-start.3 = (bf16[128,1024]{1,0:T(8,128)(2,1)S(1)}, bf16[128,1024]{1,0:T(8,128)(2,1)}, u32[]{:S(2)}) copy-start(bf16[128,1024]{1,0:T(8,128)(2,1)} %copy-done.2) | copy-start | bytes 786436
  157.6 10.9 %copy-start.5 = (bf16[128,1024]{1,0:T(8,128)(2,1)S(1)}, bf16[128,1024]{1,0:T(8,128)(2,1)}, u32[]{:S(2)}) copy-start(bf16[128,1024]{1,0:T(8,128)(2,1)} %copy-done.4) | copy-start | bytes 786436
  157.6 10.9 %copy-start.6 = (f32[16,512]{1,0:T(8,128)S(1)}, f32[16,512]{1,0:T(8,128)}, u32[]{:S(2)}) copy-start(f32[16,512]{1,0:T(8,128)} %first_ref.3) | copy-start | bytes 98308
  157.6 10.9 %copy-start.7 = (f32[16,512]{1,0:T(8,128)S(1)}, f32[16,512]{1,0:T(8,128)}, u32[]{:S(2)}) copy-start(f32[16,512]{1,0:T(8,128)} %second_ref.3) | copy-start | bytes 98308
Sparse Core Ops, SparseCore 0:
  27.9 124.8 all-gather.1

commit v6 on v5

--- a/solution.py
+++ b/solution.py
@@ -292,11 +292,17 @@
     pieces = exchange(partial, PLANE)
     piece, square = add_pieces(pieces)
 
-    swap = [(i * 8 + k, k * 8 + i) for i in range(8) for k in range(8)]
-    grad_shard = lax.ppermute(piece, ("x", "c", "z"), swap)
-    shards = [grad_shard, *from_others(grad_shard, "yl")]
+    shards = [
+        lax.ppermute(
+            piece,
+            ("yl", "x", "c", "z"),
+            [((y * 8 + i) * 8 + j, ((y ^ k) * 8 + j) * 8 + i) for y in range(4) for i in range(8) for j in range(8)],
+        )
+        for k in range(4)
+    ]
+    grad_shard = shards[0]
     late = late_rows(exchange(square, PLANE), shards)
-    late, weights = lax.optimization_barrier((late, weights))
+    weights, _ = lax.optimization_barrier((weights, late))
     gathered = exchange(late, GROUP)
     input_grad = backward(keys, weights, norm_input, scale, gain)
     weights, input_grad = lax.optimization_barrier((weights, input_grad))

time: 178 us -> 193 us (1.084)
  starting transfers between devices: 54.1 us -> 71.1 us
    all_to_all x4, starting transfers between devices: 26.3 us -> 45.9 us  [exchange(): return lax.all_to_all(x, axes, split_axis=0, concat_axis=0, tiled=True)]
    ppermute x6 -> x3, starting transfers between devices: 18.6 us -> 9.3 us  [from_others(): lax.ppermute(x, axis, [(i, i ^ k) for i in range(count)])]
    ppermute x1 -> x4, starting transfers between devices: 9.18 us -> 15.9 us  [body(): lax.ppermute(piece, ('yl', 'x', 'c', 'z'), [((y * 8 + i) * 8 + j, ((y ^ k...]
    ppermute x1 -> x4, waiting for transfers between devices: 0.01 us -> 6.12 us  [body(): lax.ppermute(piece, ('yl', 'x', 'c', 'z'), [((y * 8 + i) * 8 + j, ((y ^ k...]
    ppermute x6 -> x3, waiting for transfers between devices: 18.8 us -> 15.3 us  [from_others(): lax.ppermute(x, axis, [(i, i ^ k) for i in range(count)])]
    all_gather x1, waiting for transfers between devices: 2.54 us -> 0.01 us  [body(): lax.all_gather(state[:, :512], ('yh', 'yl', 'z'), axis=0, tiled=True)]
  transfers between devices with their start and end apart: 12 -> 12, of which waited for: 8 -> 7; matrix products, arithmetic and copies ran while one was open for 2% -> 2% of each run, Pallas kernels for 9% -> 9%
where the time goes in v6:
time: 193 us
  starting transfers between devices  71.1 us (37%)
  blocking collectives  46.2 us (24%)
  waiting for transfers between devices  34.7 us (18%)
  Pallas kernels  19.8 us (10%)
  between operations  14.2 us (7%)
  local copies, waits for them, and re-layouts  4.96 us (3%)
    all_to_all x1, blocking collectives, exchange(): return lax.all_to_all(x, axes, split_axis=0, concat_axis=0, tiled=True)  46.2 us
    all_to_all x4, starting transfers between devices, exchange(): return lax.all_to_all(x, axes, split_axis=0, concat_axis=0, tiled=True)  45.9 us
    ppermute x4, starting transfers between devices, body(): lax.ppermute(piece, ('yl', 'x', 'c', 'z'), [((y * 8 + i) * 8 + j, ((y ^ k...  15.9 us
    ppermute x3, waiting for transfers between devices, from_others(): lax.ppermute(x, axis, [(i, i ^ k) for i in range(count)])  15.3 us
    all_to_all x4, waiting for transfers between devices, exchange(): return lax.all_to_all(x, axes, split_axis=0, concat_axis=0, tiled=True)  13.3 us
    ppermute x3, starting transfers between devices, from_others(): lax.ppermute(x, axis, [(i, i ^ k) for i in range(count)])  9.3 us
    pallas_call x1, Pallas kernels, backward(): pl.pallas_call(backward_kernel, grid=(steps,), in_specs=[whole(keys), pl....  8.04 us
    ppermute x4, waiting for transfers between devices, body(): lax.ppermute(piece, ('yl', 'x', 'c', 'z'), [((y * 8 + i) * 8 + j, ((y ^ k...  6.12 us
  transfers between devices with their start and end apart: 12, of which 7 were waited for; matrix products, arithmetic and copies ran while one was open for 2% of the time, Pallas kernels for 9%

profile of v6, /device:TPU:1, one launch (start us, length us, event | category | flops | bytes accessed | tf_op | source)
XLA Modules:
  0.0 192.5 jit_solution(3862476547437745014)
XLA Ops:
  7.2 1.6 shard_map.103
  8.7 10.2 %all-to-all-start = ((bf16[8,16,1536]{2,1,0:T(8,128)(2,1)}), bf16[8,16,1536]{2,1,0:T(8,128)(2,1)S(1)}, u32[]{:S(2)}, u32[]{:S(2)}) async-start(bf16[8,16,1536]{2,1,0:T(8,128)(2,1)} %shard_map.103), calls=%async_computation | async-start | bytes 786432 | tf_op jit(solution)/shard_map/all_to_all | solution.py:37
  20.6 4.8 %shard_map.102 = (bf16[8,128,1536]{2,1,0:T(8,128)(2,1)}, bf16[128,512]{1,0:T(8,128)(2,1)}, f32[128,128]{1,0:T(8,128)}, f32[64,128]{1,0:T(8,128)}) custom-call(bf16[128,8192]{1,0:T(8,128)(2,1)} %x_ref.3, bf16[128,512]{1,0:T(8,128)(2,1)} %key_ref.1, f32[128,64]{1,0:T(8,128)} %get-tuple-element.43.cos_ref, f32[128,64]{1,0:T(8,128)} %get-tuple-element.42.sin_ref, ...), custom_call_target="tpu_custom_call" | custom-call | flops 8388608 | bytes 6291456 | tf_op jit(solution)/shard_map/pallas_call | solution.py:73
  25.4 1.7 all-to-all-done
  27.9 4.4 %all-to-all-start.1 = ((bf16[8,128,1536]{2,1,0:T(8,128)(2,1)}), bf16[8,128,1536]{2,1,0:T(8,128)(2,1)S(1)}, u32[]{:S(2)}, u32[]{:S(2)}) async-start(bf16[8,128,1536]{2,1,0:T(8,128)(2,1)} %get-tuple-element.25), calls=%async_computation.1 | async-start | bytes 6291456 | tf_op jit(solution)/shard_map/all_to_all | solution.py:37
  33.2 1.9 collective-permute-start
  35.2 1.9 collective-permute-start.1
  37.1 5.5 %collective-permute-start.2 = (bf16[128,1024]{1,0:T(8,128)(2,1)S(1)}, bf16[128,1024]{1,0:T(8,128)(2,1)S(1)}, u32[]{:S(2)}, u32[]{:S(2)}) collective-permute-start(bf16[128,1024]{1,0:T(8,128)(2,1)S(1)} %slice.7.m0_ref), channel_id=1, source_target_pairs={{0,384},{128,256},{256,128},{384,0},{1,385},{129,257},{257,129},{3... | collective-permute-start | bytes 786440 | tf_op jit(solution)/shard_map/ppermute | solution.py:195
  42.6 1.7 collective-permute-done.m1_ref
  44.9 13.6 %collective-permute-done.1.m2_ref = bf16[128,1024]{1,0:T(8,128)(2,1)S(1)} collective-permute-done((bf16[128,1024]{1,0:T(8,128)(2,1)S(1)}, bf16[128,1024]{1,0:T(8,128)(2,1)S(1)}, u32[]{:S(2)}, u32[]{:S(2)}) %collective-permute-start.1) | collective-permute-done | bytes 262176 | tf_op jit(solution)/shard_map/ppermute | solution.py:195
  60.0 9.9 %all-to-all-done.1.key_ref.normed_ref = bf16[8,128,1536]{2,1,0:T(8,128)(2,1)S(1)} async-done(((bf16[8,128,1536]{2,1,0:T(8,128)(2,1)}), bf16[8,128,1536]{2,1,0:T(8,128)(2,1)S(1)}, u32[]{:S(2)}, u32[]{:S(2)}) %all-to-all-start.1) | async-done | bytes 3145760 | tf_op jit(solution)/shard_map/all_to_all | solution.py:37
  69.9 1.8 shard_map.104
  71.6 46.2 %all_to_all.31.pieces_ref = bf16[64,16,512]{2,1,0:T(8,128)(2,1)S(1)} all-to-all(bf16[64,16,512]{2,1,0:T(8,128)(2,1)S(1)} %bitcast.10), channel_id=1, replica_groups=mesh['yl'=4,'x'=4,'c'=2,'z'=8,'yh'=2] {'yl','z','yh'}, dimensions={0} | all-to-all | bytes 2097152 | tf_op jit(solution)/shard_map/all_to_all | solution.py:37
  118.7 9.3 %all-to-all-start.3 = ((f32[64,1,128]{2,1,0:T(1,128)}), f32[64,1,128]{2,1,0:T(1,128)S(1)}, u32[]{:S(2)}, u32[]{:S(2)}) async-start(f32[64,1,128]{2,1,0:T(1,128)} %bitcast.5), calls=%async_computation.3 | async-start | bytes 65536 | tf_op jit(solution)/shard_map/all_to_all | solution.py:37
  128.0 5.5 %collective-permute-start.3 = (f32[16,512]{1,0:T(8,128)S(1)}, f32[16,512]{1,0:T(8,128)S(1)}, u32[]{:S(2)}, u32[]{:S(2)}) collective-permute-start(f32[16,512]{1,0:T(8,128)S(1)} %get-tuple-element.28), channel_id=1, source_target_pairs={{0,0},{2,16},{4,32},{6,48},{8,64},{10,80},{12,96},{14,112},{16,2},... | collective-permute-start | bytes 98312 | tf_op jit(solution)/shard_map/ppermute | solution.py:296
  133.5 2.8 %collective-permute-start.4 = (f32[16,512]{1,0:T(8,128)S(1)}, f32[16,512]{1,0:T(8,128)S(1)}, u32[]{:S(2)}, u32[]{:S(2)}) collective-permute-start(f32[16,512]{1,0:T(8,128)S(1)} %get-tuple-element.28), channel_id=1, source_target_pairs={{0,128},{2,144},{4,160},{6,176},{8,192},{10,208},{12,224},{14,240}... | collective-permute-start | bytes 98312 | tf_op jit(solution)/shard_map/ppermute | solution.py:296
  136.4 5.7 %collective-permute-start.5 = (f32[16,512]{1,0:T(8,128)S(1)}, f32[16,512]{1,0:T(8,128)S(1)}, u32[]{:S(2)}, u32[]{:S(2)}) collective-permute-start(f32[16,512]{1,0:T(8,128)S(1)} %get-tuple-element.28), channel_id=1, source_target_pairs={{0,256},{2,272},{4,288},{6,304},{8,320},{10,336},{12,352},{14,368}... | collective-permute-start | bytes 98312 | tf_op jit(solution)/shard_map/ppermute | solution.py:296
  142.0 1.9 collective-permute-start.6
  144.9 5.2 %collective-permute-done.6.s3_ref = f32[16,512]{1,0:T(8,128)S(1)} collective-permute-done((f32[16,512]{1,0:T(8,128)S(1)}, f32[16,512]{1,0:T(8,128)S(1)}, u32[]{:S(2)}, u32[]{:S(2)}) %collective-permute-start.6) | collective-permute-done | bytes 32800 | tf_op jit(solution)/shard_map/ppermute | solution.py:296
  151.1 21.9 %all-to-all-start.4 = ((bf16[8,64,640]{2,1,0:T(8,128)(2,1)}), bf16[8,64,640]{2,1,0:T(8,128)(2,1)S(1)}, u32[]{:S(2)}, u32[]{:S(2)}) async-start(bf16[8,64,640]{2,1,0:T(8,128)(2,1)} %shard_map.106), calls=%async_computation.4 | async-start | bytes 1310720 | tf_op jit(solution)/shard_map/all_to_all | solution.py:37
  173.1 8.0 %shard_map.107 = bf16[128,8192]{1,0:T(8,128)(2,1)} custom-call(bf16[128,512]{1,0:T(8,128)(2,1)} %get-tuple-element.30.key_ref, bf16[2,4,8,128,512]{4,3,2,1,0:T(8,128)(2,1)} %bitcast.13, bf16[128,8192]{1,0:T(8,128)(2,1)} %x_ref.3, f32[128,128]{1,0:T(8,128)} %get-tuple-element.31.scale_ref, f32[64,128]{1,0:T(8,128)} %get-tuple-element.32.gain_ref), custom_call_target="tpu_custom_call" | custom-call | flops 1073741824 | bytes 12582912 | tf_op jit(solution)/shard_map/pallas_call | solution.py:165
  181.1 1.1 constant_dynamic-slice_fusion
  182.2 1.7 all-to-all-done.4.gathered_ref
  183.9 1.8 shard_map.108
  (33 shorter events, 8.4 us)
Async XLA Ops:
  8.7 18.3 %all-to-all-start = ((bf16[8,16,1536]{2,1,0:T(8,128)(2,1)}), bf16[8,16,1536]{2,1,0:T(8,128)(2,1)S(1)}, u32[]{:S(2)}, u32[]{:S(2)}) async-start(bf16[8,16,1536]{2,1,0:T(8,128)(2,1)} %shard_map.103), calls=%async_computation | async-start | bytes 786432 | tf_op jit(solution)/shard_map/all_to_all | solution.py:37
  19.0 154.1 %all-gather.2.cloned.1.call-start = ((), (), s32[]{:S(2)}) async-start(), calls=%async_computation.5 | async-start | bytes 8519680 | tf_op jit(solution)/shard_map/all_gather | solution.py:285
  27.1 0.8 copy-start.8
  27.9 42.0 %all-to-all-start.1 = ((bf16[8,128,1536]{2,1,0:T(8,128)(2,1)}), bf16[8,128,1536]{2,1,0:T(8,128)(2,1)S(1)}, u32[]{:S(2)}, u32[]{:S(2)}) async-start(bf16[8,128,1536]{2,1,0:T(8,128)(2,1)} %get-tuple-element.25), calls=%async_computation.1 | async-start | bytes 6291456 | tf_op jit(solution)/shard_map/all_to_all | solution.py:37
  33.2 11.0 %collective-permute-start = (bf16[128,1024]{1,0:T(8,128)(2,1)S(1)}, bf16[128,1024]{1,0:T(8,128)(2,1)S(1)}, u32[]{:S(2)}, u32[]{:S(2)}) collective-permute-start(bf16[128,1024]{1,0:T(8,128)(2,1)S(1)} %slice.7.m0_ref), channel_id=1, source_target_pairs={{0,128},{128,0},{256,384},{384,256},{1,129},{129,1},{257,385},{385... | collective-permute-start | bytes 786440 | tf_op jit(solution)/shard_map/ppermute | solution.py:195
  35.2 23.4 %collective-permute-start.1 = (bf16[128,1024]{1,0:T(8,128)(2,1)S(1)}, bf16[128,1024]{1,0:T(8,128)(2,1)S(1)}, u32[]{:S(2)}, u32[]{:S(2)}) collective-permute-start(bf16[128,1024]{1,0:T(8,128)(2,1)S(1)} %slice.7.m0_ref), channel_id=1, source_target_pairs={{0,256},{128,384},{256,0},{384,128},{1,257},{129,385},{257,1},{385... | collective-permute-start | bytes 786440 | tf_op jit(solution)/shard_map/ppermute | solution.py:195
  37.1 22.1 %collective-permute-start.2 = (bf16[128,1024]{1,0:T(8,128)(2,1)S(1)}, bf16[128,1024]{1,0:T(8,128)(2,1)S(1)}, u32[]{:S(2)}, u32[]{:S(2)}) collective-permute-start(bf16[128,1024]{1,0:T(8,128)(2,1)S(1)} %slice.7.m0_ref), channel_id=1, source_target_pairs={{0,384},{128,256},{256,128},{384,0},{1,385},{129,257},{257,129},{3... | collective-permute-start | bytes 786440 | tf_op jit(solution)/shard_map/ppermute | solution.py:195
  44.2 0.7 copy-start
  58.5 0.7 copy-start.2
  59.2 0.7 copy-start.4
  118.7 31.4 %all-to-all-start.3 = ((f32[64,1,128]{2,1,0:T(1,128)}), f32[64,1,128]{2,1,0:T(1,128)S(1)}, u32[]{:S(2)}, u32[]{:S(2)}) async-start(f32[64,1,128]{2,1,0:T(1,128)} %bitcast.5), calls=%async_computation.3 | async-start | bytes 65536 | tf_op jit(solution)/shard_map/all_to_all | solution.py:37
  128.0 15.9 %collective-permute-start.3 = (f32[16,512]{1,0:T(8,128)S(1)}, f32[16,512]{1,0:T(8,128)S(1)}, u32[]{:S(2)}, u32[]{:S(2)}) collective-permute-start(f32[16,512]{1,0:T(8,128)S(1)} %get-tuple-element.28), channel_id=1, source_target_pairs={{0,0},{2,16},{4,32},{6,48},{8,64},{10,80},{12,96},{14,112},{16,2},... | collective-permute-start | bytes 98312 | tf_op jit(solution)/shard_map/ppermute | solution.py:296
  133.5 10.4 %collective-permute-start.4 = (f32[16,512]{1,0:T(8,128)S(1)}, f32[16,512]{1,0:T(8,128)S(1)}, u32[]{:S(2)}, u32[]{:S(2)}) collective-permute-start(f32[16,512]{1,0:T(8,128)S(1)} %get-tuple-element.28), channel_id=1, source_target_pairs={{0,128},{2,144},{4,160},{6,176},{8,192},{10,208},{12,224},{14,240}... | collective-permute-start | bytes 98312 | tf_op jit(solution)/shard_map/ppermute | solution.py:296
  136.4 8.5 %collective-permute-start.5 = (f32[16,512]{1,0:T(8,128)S(1)}, f32[16,512]{1,0:T(8,128)S(1)}, u32[]{:S(2)}, u32[]{:S(2)}) collective-permute-start(f32[16,512]{1,0:T(8,128)S(1)} %get-tuple-element.28), channel_id=1, source_target_pairs={{0,256},{2,272},{4,288},{6,304},{8,320},{10,336},{12,352},{14,368}... | collective-permute-start | bytes 98312 | tf_op jit(solution)/shard_map/ppermute | solution.py:296
  142.0 8.1 %collective-permute-start.6 = (f32[16,512]{1,0:T(8,128)S(1)}, f32[16,512]{1,0:T(8,128)S(1)}, u32[]{:S(2)}, u32[]{:S(2)}) collective-permute-start(f32[16,512]{1,0:T(8,128)S(1)} %get-tuple-element.28), channel_id=1, source_target_pairs={{0,384},{2,400},{4,416},{6,432},{8,448},{10,464},{12,480},{14,496}... | collective-permute-start | bytes 98312 | tf_op jit(solution)/shard_map/ppermute | solution.py:296
  151.1 32.8 %all-to-all-start.4 = ((bf16[8,64,640]{2,1,0:T(8,128)(2,1)}), bf16[8,64,640]{2,1,0:T(8,128)(2,1)S(1)}, u32[]{:S(2)}, u32[]{:S(2)}) async-start(bf16[8,64,640]{2,1,0:T(8,128)(2,1)} %shard_map.106), calls=%async_computation.4 | async-start | bytes 1310720 | tf_op jit(solution)/shard_map/all_to_all | solution.py:37
  173.0 10.9 %copy-start.1 = (bf16[128,1024]{1,0:T(8,128)(2,1)S(1)}, bf16[128,1024]{1,0:T(8,128)(2,1)}, u32[]{:S(2)}) copy-start(bf16[128,1024]{1,0:T(8,128)(2,1)} %copy-done) | copy-start | bytes 786436
  173.0 10.9 %copy-start.3 = (bf16[128,1024]{1,0:T(8,128)(2,1)S(1)}, bf16[128,1024]{1,0:T(8,128)(2,1)}, u32[]{:S(2)}) copy-start(bf16[128,1024]{1,0:T(8,128)(2,1)} %copy-done.2) | copy-start | bytes 786436
  173.0 10.9 %copy-start.5 = (bf16[128,1024]{1,0:T(8,128)(2,1)S(1)}, bf16[128,1024]{1,0:T(8,128)(2,1)}, u32[]{:S(2)}) copy-start(bf16[128,1024]{1,0:T(8,128)(2,1)} %copy-done.4) | copy-start | bytes 786436
  173.0 10.9 %copy-start.6 = (f32[16,512]{1,0:T(8,128)S(1)}, f32[16,512]{1,0:T(8,128)}, u32[]{:S(2)}) copy-start(f32[16,512]{1,0:T(8,128)} %first_ref.3) | copy-start | bytes 98308
  173.1 10.9 %copy-start.7 = (f32[16,512]{1,0:T(8,128)S(1)}, f32[16,512]{1,0:T(8,128)}, u32[]{:S(2)}) copy-start(f32[16,512]{1,0:T(8,128)} %second_ref.3) | copy-start | bytes 98308
Sparse Core Ops, SparseCore 0:
  27.9 128.9 all-gather.1

commit v7 on v5

--- a/solution.py
+++ b/solution.py
@@ -190,9 +190,9 @@
     )(*args)
 
 
-def from_others(x, axis):
-    count = lax.axis_size(axis)
-    return [lax.ppermute(x, axis, [(i, i ^ k) for i in range(count)]) for k in range(1, count)]
+def from_others(x, axes):
+    count = math.prod(lax.axis_size(axis) for axis in axes)
+    return [lax.ppermute(x, axes, [(i, i ^ k) for i in range(count)]) for k in range(1, count)]
 
 
 def add_pieces_kernel(pieces_ref, piece_ref, square_ref):
@@ -224,10 +224,9 @@
     return local_call(late_kernel, [((N_GROUP, 64, 640), bf16)], squares, *shards)[0]
 
 
-def update_kernel(
-    place_ref, gathered_ref, weight_ref, m0_ref, m1_ref, m2_ref, m3_ref, shard_ref, first_ref, second_ref,
-    weight_out, first_out, second_out,
-):
+def update_kernel(place_ref, gathered_ref, weight_ref, *refs):
+    moment_refs = refs[:N_GROUP]
+    shard_ref, first_ref, second_ref, weight_out, first_out, second_out = refs[N_GROUP:]
     terms = jnp.sum(gathered_ref[:, :16, 512:].astype(f32), axis=0)
     total_square = jnp.sum(terms[:1], axis=1, keepdims=True)
     clip_limit = math.sqrt(KV * D)
@@ -243,13 +242,12 @@
     new_first, new_second = moments(shard_ref[...], first_ref[...], second_ref[...])
     first_out[...] = new_first
     second_out[...] = new_second
-    for k, ref in enumerate((m0_ref, m1_ref, m2_ref, m3_ref)):
-        block = place_ref[0] ^ k
-        for r in range(8):
-            part = slice(r * 16, (r + 1) * 16)
-            rows = pl.ds(pl.multiple_of(block * 128 + r * 16, 16), 16)
-            gradient = gathered_ref[r, k * 16 : (k + 1) * 16, :512].astype(f32)
-            new_first, new_second = moments(gradient, ref[part, :512].astype(f32), ref[part, 512:].astype(f32))
+    for j, ref in enumerate(moment_refs):
+        group = place_ref[1] ^ j
+        for k in range(4):
+            rows = pl.ds(pl.multiple_of(((place_ref[0] ^ k) * N_GROUP + group) * 16, 16), 16)
+            gradient = gathered_ref[group, k * 16 : (k + 1) * 16, :512].astype(f32)
+            new_first, new_second = moments(gradient, ref[k, :, :512].astype(f32), ref[k, :, 512:].astype(f32))
             weight_out[rows, :] = (
                 weight_ref[rows, :].astype(f32) * (1.0 - learn_rate * decay_rate)
                 - learn_rate * new_first / (jnp.sqrt(new_second) + eps_adam)
@@ -267,42 +265,48 @@
     )(place, *args)
 
 
-def state_kernel(weight_ref, first_ref, second_ref, out_ref):
-    out_ref[:, :, :512] = jnp.broadcast_to(weight_ref[...], (N_GROUP, 16, 512))
-    out_ref[:, :, 512:1024] = jnp.broadcast_to(first_ref[...].astype(bf16), (N_GROUP, 16, 512))
-    out_ref[:, :, 1024:] = jnp.broadcast_to(second_ref[...].astype(bf16), (N_GROUP, 16, 512))
+def stack_kernel(*refs):
+    for k, ref in enumerate(refs[:-1]):
+        refs[-1][k] = ref[...]
+
+
+def round_kernel(first_ref, second_ref, out_ref):
+    out_ref[:, :512] = first_ref[...].astype(bf16)
+    out_ref[:, 512:] = second_ref[...].astype(bf16)
 
 
 def body(norm_input, key_grad, positions, norm_gain, key_weight, first_moment, second_moment):
-    state = local_call(
-        state_kernel, [((N_GROUP, 16, 1536), bf16)], key_weight, first_moment, second_moment, vmem=56
-    )[0]
-    state = exchange(state, GROUP).reshape(N_GROUP * 16, 1536)
+    weights = exchange(jnp.broadcast_to(key_weight, (N_GROUP, *key_weight.shape)), GROUP)
     cosine, sine = rotation(positions)
     send, keys, scale, gain = prepare(norm_input, key_grad, cosine, sine, norm_gain.reshape(D // HEAD, HEAD))
-    send, state = lax.optimization_barrier((send, state))
-
-    weights = lax.all_gather(state[:, :512], ("yh", "yl", "z"), axis=0, tiled=True).reshape(2, 4, 8, 128, 512)
+    send, weights = lax.optimization_barrier((send, weights))
+
+    weights = lax.all_gather(weights.reshape(128, 512), ("yh", "yl", "z"), axis=0, tiled=True)
+    weights = weights.reshape(2, 4, 8, 128, 512)
 
     received = exchange(send, GROUP)
-    moments = state[:, 512:]
-    moments = [moments, *from_others(moments, "yl")]
-    received, *moments = lax.optimization_barrier((received, *moments))
+    moments = local_call(round_kernel, [((16, 1024), bf16)], first_moment, second_moment, vmem=56)[0]
+    moments, _ = lax.optimization_barrier((moments, send))
+    moments = local_call(stack_kernel, [((4, 16, 1024), bf16)], moments, *from_others(moments, ("yl",)))[0]
+    received, moments = lax.optimization_barrier((received, moments))
     partial = product(received).reshape(N_PLANE, 16, 512)
+    partial, moments = lax.optimization_barrier((partial, moments))
     pieces = exchange(partial, PLANE)
+    moments = [moments, *from_others(moments, GROUP)]
+    pieces, *moments = lax.optimization_barrier((pieces, *moments))
     piece, square = add_pieces(pieces)
 
     swap = [(i * 8 + k, k * 8 + i) for i in range(8) for k in range(8)]
     grad_shard = lax.ppermute(piece, ("x", "c", "z"), swap)
-    shards = [grad_shard, *from_others(grad_shard, "yl")]
+    shards = [grad_shard, *from_others(grad_shard, ("yl",))]
     late = late_rows(exchange(square, PLANE), shards)
-    late, weights = lax.optimization_barrier((late, weights))
+    weights, _ = lax.optimization_barrier((weights, late))
     gathered = exchange(late, GROUP)
     input_grad = backward(keys, weights, norm_input, scale, gain)
     weights, input_grad = lax.optimization_barrier((weights, input_grad))
     at = (lax.axis_index("yh"), 0, lax.axis_index("z"), 0, 0)
     weight = lax.dynamic_slice(weights, at, (1, 4, 1, 128, 512)).reshape(KV, 512)
-    place = lax.axis_index("yl").astype(jnp.int32).reshape(1)
+    place = jnp.stack([lax.axis_index("yl"), lax.axis_index(GROUP)]).astype(jnp.int32)
     new_weight, new_first, new_second = update(
         place, gathered, weight, *moments, grad_shard, first_moment, second_moment
     )

time: 178 us -> 180 us (1.011)
  blocking collectives: 46.2 us -> 0 us
  starting transfers between devices: 54.1 us -> 87.5 us
  waiting for transfers between devices: 36.3 us -> 50.7 us
    all_to_all x1 -> x0, blocking collectives: 46.2 us -> none  [exchange(): return lax.all_to_all(x, axes, split_axis=0, concat_axis=0, tiled=True)]
    all_to_all x4 -> x5, waiting for transfers between devices: 14.9 us -> 40.8 us  [exchange(): return lax.all_to_all(x, axes, split_axis=0, concat_axis=0, tiled=True)]
    ppermute x6 -> x13, starting transfers between devices: 18.6 us -> 40.9 us  [from_others(): lax.ppermute(x, axes, [(i, i ^ k) for i in range(count)])]
    all_to_all x4 -> x5, starting transfers between devices: 26.3 us -> 40.1 us  [exchange(): return lax.all_to_all(x, axes, split_axis=0, concat_axis=0, tiled=True)]
    ppermute x6 -> x13, waiting for transfers between devices: 18.8 us -> 9.9 us  [from_others(): lax.ppermute(x, axes, [(i, i ^ k) for i in range(count)])]
    ppermute x1, starting transfers between devices: 9.18 us -> 6.5 us  [body(): grad_shard = lax.ppermute(piece, ('x', 'c', 'z'), swap)]
    all_gather x1, waiting for transfers between devices: 2.54 us -> 0.01 us  [body(): lax.all_gather(weights.reshape(128, 512), ('yh', 'yl', 'z'), axis=0, tile...]
  transfers between devices with their start and end apart: 12 -> 20, of which waited for: 8 -> 8; matrix products, arithmetic and copies ran while one was open for 2% -> 2% of each run, Pallas kernels for 9% -> 10%
where the time goes in v7:
time: 180 us; the launch traced here: 179 us
  starting transfers between devices  87.5 us (49%)
  waiting for transfers between devices  50.7 us (28%)
  Pallas kernels  20 us (11%)
  between operations  14.3 us (8%)
  local copies, waits for them, and re-layouts  4.83 us (3%)
    ppermute x13, starting transfers between devices, from_others(): lax.ppermute(x, axes, [(i, i ^ k) for i in range(count)])  40.9 us
    all_to_all x5, waiting for transfers between devices, exchange(): return lax.all_to_all(x, axes, split_axis=0, concat_axis=0, tiled=True)  40.8 us
    all_to_all x5, starting transfers between devices, exchange(): return lax.all_to_all(x, axes, split_axis=0, concat_axis=0, tiled=True)  40.1 us
    ppermute x13, waiting for transfers between devices, from_others(): lax.ppermute(x, axes, [(i, i ^ k) for i in range(count)])  9.9 us
    pallas_call x1, Pallas kernels, backward(): pl.pallas_call(backward_kernel, grid=(steps,), in_specs=[whole(keys), pl....  8.01 us
    ppermute x1, starting transfers between devices, body(): grad_shard = lax.ppermute(piece, ('x', 'c', 'z'), swap)  6.5 us
    pallas_call x1, Pallas kernels, prepare(): pl.pallas_call(prepare_kernel, grid=(tokens // tile,), in_specs=[pl.Block...  4.69 us
  transfers between devices with their start and end apart: 20, of which 8 were waited for; matrix products, arithmetic and copies ran while one was open for 2% of the time, Pallas kernels for 10%

profile of v7, /device:TPU:1, one launch (start us, length us, event | category | flops | bytes accessed | tf_op | source)
XLA Modules:
  0.0 179.0 jit_solution(829272148842323223)
XLA Ops:
  8.5 10.2 %all-to-all-start = ((bf16[8,16,512]{2,1,0:T(8,128)(2,1)}), bf16[8,16,512]{2,1,0:T(8,128)(2,1)S(1)}, u32[]{:S(2)}, u32[]{:S(2)}) async-start(bf16[8,16,512]{2,1,0:T(8,128)(2,1)} %broadcast_in_dim.2), calls=%async_computation | async-start | bytes 262144 | tf_op jit(solution)/shard_map/all_to_all | solution.py:37
  20.3 4.7 %shard_map.102 = (bf16[8,128,1536]{2,1,0:T(8,128)(2,1)}, bf16[128,512]{1,0:T(8,128)(2,1)}, f32[128,128]{1,0:T(8,128)}, f32[64,128]{1,0:T(8,128)}) custom-call(bf16[128,8192]{1,0:T(8,128)(2,1)} %x_ref.3, bf16[128,512]{1,0:T(8,128)(2,1)} %key_ref.1, f32[128,64]{1,0:T(8,128)} %get-tuple-element.61.cos_ref, f32[128,64]{1,0:T(8,128)} %get-tuple-element.60.sin_ref, ...), custom_call_target="tpu_custom_call" | custom-call | flops 8388608 | bytes 6291456 | tf_op jit(solution)/shard_map/pallas_call | solution.py:73
  25.7 4.9 %all-to-all-start.1 = ((bf16[8,128,1536]{2,1,0:T(8,128)(2,1)}), bf16[8,128,1536]{2,1,0:T(8,128)(2,1)S(1)}, u32[]{:S(2)}, u32[]{:S(2)}) async-start(bf16[8,128,1536]{2,1,0:T(8,128)(2,1)} %get-tuple-element.34), calls=%async_computation.1 | async-start | bytes 6291456 | tf_op jit(solution)/shard_map/all_to_all | solution.py:37
  35.8 5.4 %collective-permute-start.2 = (bf16[16,1024]{1,0:T(8,128)(2,1)}, bf16[16,1024]{1,0:T(8,128)(2,1)S(1)}, u32[]{:S(2)}, u32[]{:S(2)}) collective-permute-start(bf16[16,1024]{1,0:T(8,128)(2,1)} %shard_map.103.refs_0_), channel_id=1, source_target_pairs={{0,384},{128,256},{256,128},{384,0},{1,385},{129,257},{257,129},{3... | collective-permute-start | bytes 98312 | tf_op jit(solution)/shard_map/ppermute | solution.py:195
  43.6 24.5 %all-to-all-done.1.key_ref.normed_ref = bf16[8,128,1536]{2,1,0:T(8,128)(2,1)S(1)} async-done(((bf16[8,128,1536]{2,1,0:T(8,128)(2,1)}), bf16[8,128,1536]{2,1,0:T(8,128)(2,1)S(1)}, u32[]{:S(2)}, u32[]{:S(2)}) %all-to-all-start.1) | async-done | bytes 3145760 | tf_op jit(solution)/shard_map/all_to_all | solution.py:37
  70.9 11.9 %all-to-all-start.2 = ((bf16[64,16,512]{2,1,0:T(8,128)(2,1)}), bf16[64,16,512]{2,1,0:T(8,128)(2,1)S(1)}, u32[]{:S(2)}, u32[]{:S(2)}) async-start(bf16[64,16,512]{2,1,0:T(8,128)(2,1)} %bitcast.11), calls=%async_computation.2 | async-start | bytes 2097152 | tf_op jit(solution)/shard_map/all_to_all | solution.py:37
  82.8 3.1 %collective-permute-start.3 = (bf16[4,16,1024]{2,1,0:T(8,128)(2,1)S(1)}, bf16[4,16,1024]{2,1,0:T(8,128)(2,1)S(1)}, u32[]{:S(2)}, u32[]{:S(2)}) collective-permute-start(bf16[4,16,1024]{2,1,0:T(8,128)(2,1)S(1)} %shard_map.104.refs_0_), channel_id=1, source_target_pairs={{0,16},{16,0},{32,48},{48,32},{64,80},{80,64},{96,112},{112,96},{1... | collective-permute-start | bytes 393224 | tf_op jit(solution)/shard_map/ppermute | solution.py:195
  85.9 2.2 %collective-permute-start.4 = (bf16[4,16,1024]{2,1,0:T(8,128)(2,1)S(1)}, bf16[4,16,1024]{2,1,0:T(8,128)(2,1)S(1)}, u32[]{:S(2)}, u32[]{:S(2)}) collective-permute-start(bf16[4,16,1024]{2,1,0:T(8,128)(2,1)S(1)} %shard_map.104.refs_0_), channel_id=1, source_target_pairs={{0,32},{16,48},{32,0},{48,16},{64,96},{80,112},{96,64},{112,80},{1... | collective-permute-start | bytes 393224 | tf_op jit(solution)/shard_map/ppermute | solution.py:195
  88.1 3.3 %collective-permute-start.5 = (bf16[4,16,1024]{2,1,0:T(8,128)(2,1)S(1)}, bf16[4,16,1024]{2,1,0:T(8,128)(2,1)S(1)}, u32[]{:S(2)}, u32[]{:S(2)}) collective-permute-start(bf16[4,16,1024]{2,1,0:T(8,128)(2,1)S(1)} %shard_map.104.refs_0_), channel_id=1, source_target_pairs={{0,48},{16,32},{32,16},{48,0},{64,112},{80,96},{96,80},{112,64},{1... | collective-permute-start | bytes 393224 | tf_op jit(solution)/shard_map/ppermute | solution.py:195
  91.4 2.3 %collective-permute-start.6 = (bf16[4,16,1024]{2,1,0:T(8,128)(2,1)S(1)}, bf16[4,16,1024]{2,1,0:T(8,128)(2,1)S(1)}, u32[]{:S(2)}, u32[]{:S(2)}) collective-permute-start(bf16[4,16,1024]{2,1,0:T(8,128)(2,1)S(1)} %shard_map.104.refs_0_), channel_id=1, source_target_pairs={{0,64},{16,80},{32,96},{48,112},{64,0},{80,16},{96,32},{112,48},{1... | collective-permute-start | bytes 393224 | tf_op jit(solution)/shard_map/ppermute | solution.py:195
  93.7 4.8 %collective-permute-start.7 = (bf16[4,16,1024]{2,1,0:T(8,128)(2,1)S(1)}, bf16[4,16,1024]{2,1,0:T(8,128)(2,1)S(1)}, u32[]{:S(2)}, u32[]{:S(2)}) collective-permute-start(bf16[4,16,1024]{2,1,0:T(8,128)(2,1)S(1)} %shard_map.104.refs_0_), channel_id=1, source_target_pairs={{0,80},{16,64},{32,112},{48,96},{64,16},{80,0},{96,48},{112,32},{1... | collective-permute-start | bytes 393224 | tf_op jit(solution)/shard_map/ppermute | solution.py:195
  98.6 2.8 %collective-permute-start.8 = (bf16[4,16,1024]{2,1,0:T(8,128)(2,1)S(1)}, bf16[4,16,1024]{2,1,0:T(8,128)(2,1)S(1)}, u32[]{:S(2)}, u32[]{:S(2)}) collective-permute-start(bf16[4,16,1024]{2,1,0:T(8,128)(2,1)S(1)} %shard_map.104.refs_0_), channel_id=1, source_target_pairs={{0,96},{16,112},{32,64},{48,80},{64,32},{80,48},{96,0},{112,16},{1... | collective-permute-start | bytes 393224 | tf_op jit(solution)/shard_map/ppermute | solution.py:195
  101.4 3.9 %collective-permute-start.9 = (bf16[4,16,1024]{2,1,0:T(8,128)(2,1)S(1)}, bf16[4,16,1024]{2,1,0:T(8,128)(2,1)S(1)}, u32[]{:S(2)}, u32[]{:S(2)}) collective-permute-start(bf16[4,16,1024]{2,1,0:T(8,128)(2,1)S(1)} %shard_map.104.refs_0_), channel_id=1, source_target_pairs={{0,112},{16,96},{32,80},{48,64},{64,48},{80,32},{96,16},{112,0},{1... | collective-permute-start | bytes 393224 | tf_op jit(solution)/shard_map/ppermute | solution.py:195
  106.9 3.4 %collective-permute-done.9.refs_7_ = bf16[4,16,1024]{2,1,0:T(8,128)(2,1)S(1)} collective-permute-done((bf16[4,16,1024]{2,1,0:T(8,128)(2,1)S(1)}, bf16[4,16,1024]{2,1,0:T(8,128)(2,1)S(1)}, u32[]{:S(2)}, u32[]{:S(2)}) %collective-permute-start.9) | collective-permute-done | bytes 131104 | tf_op jit(solution)/shard_map/ppermute | solution.py:195
  110.3 12.9 %all-to-all-done.2.pieces_ref = bf16[64,16,512]{2,1,0:T(8,128)(2,1)S(1)} async-done(((bf16[64,16,512]{2,1,0:T(8,128)(2,1)}), bf16[64,16,512]{2,1,0:T(8,128)(2,1)S(1)}, u32[]{:S(2)}, u32[]{:S(2)}) %all-to-all-start.2) | async-done | bytes 1048608 | tf_op jit(solution)/shard_map/all_to_all | solution.py:37
  124.1 6.5 %collective-permute-start.10 = (f32[16,512]{1,0:T(8,128)S(1)}, f32[16,512]{1,0:T(8,128)S(1)}, u32[]{:S(2)}, u32[]{:S(2)}) collective-permute-start(f32[16,512]{1,0:T(8,128)S(1)} %get-tuple-element.42), channel_id=1, source_target_pairs={{0,0},{2,16},{4,32},{6,48},{8,64},{10,80},{12,96},{14,112},{16,2},... | collective-permute-start | bytes 98312 | tf_op jit(solution)/shard_map/ppermute | solution.py:300
  130.6 7.0 %all-to-all-start.3 = ((f32[64,1,128]{2,1,0:T(1,128)}), f32[64,1,128]{2,1,0:T(1,128)S(1)}, u32[]{:S(2)}, u32[]{:S(2)}) async-start(f32[64,1,128]{2,1,0:T(1,128)} %bitcast.5), calls=%async_computation.3 | async-start | bytes 65536 | tf_op jit(solution)/shard_map/all_to_all | solution.py:37
  137.6 2.9 %collective-permute-start.11 = (f32[16,512]{1,0:T(8,128)S(1)}, f32[16,512]{1,0:T(8,128)S(1)}, u32[]{:S(2)}, u32[]{:S(2)}) collective-permute-start(f32[16,512]{1,0:T(8,128)S(1)} %collective-permute-done.10.s0_ref.refs_8_), channel_id=1, source_target_pairs={{0,128},{128,0},{256,384},{384,256},{1,129},{129,1},{257,385},{385... | collective-permute-start | bytes 98312 | tf_op jit(solution)/shard_map/ppermute | solution.py:195
  140.5 4.2 %collective-permute-start.12 = (f32[16,512]{1,0:T(8,128)S(1)}, f32[16,512]{1,0:T(8,128)S(1)}, u32[]{:S(2)}, u32[]{:S(2)}) collective-permute-start(f32[16,512]{1,0:T(8,128)S(1)} %collective-permute-done.10.s0_ref.refs_8_), channel_id=1, source_target_pairs={{0,256},{128,384},{256,0},{384,128},{1,257},{129,385},{257,1},{385... | collective-permute-start | bytes 98312 | tf_op jit(solution)/shard_map/ppermute | solution.py:195
  144.7 2.2 %collective-permute-start.13 = (f32[16,512]{1,0:T(8,128)S(1)}, f32[16,512]{1,0:T(8,128)S(1)}, u32[]{:S(2)}, u32[]{:S(2)}) collective-permute-start(f32[16,512]{1,0:T(8,128)S(1)} %collective-permute-done.10.s0_ref.refs_8_), channel_id=1, source_target_pairs={{0,384},{128,256},{256,128},{384,0},{1,385},{129,257},{257,129},{3... | collective-permute-start | bytes 98312 | tf_op jit(solution)/shard_map/ppermute | solution.py:195
  148.5 3.3 %collective-permute-done.13.s3_ref = f32[16,512]{1,0:T(8,128)S(1)} collective-permute-done((f32[16,512]{1,0:T(8,128)S(1)}, f32[16,512]{1,0:T(8,128)S(1)}, u32[]{:S(2)}, u32[]{:S(2)}) %collective-permute-start.13) | collective-permute-done | bytes 32800 | tf_op jit(solution)/shard_map/ppermute | solution.py:195
  152.8 6.2 %all-to-all-start.4 = ((bf16[8,64,640]{2,1,0:T(8,128)(2,1)}), bf16[8,64,640]{2,1,0:T(8,128)(2,1)S(1)}, u32[]{:S(2)}, u32[]{:S(2)}) async-start(bf16[8,64,640]{2,1,0:T(8,128)(2,1)} %shard_map.107), calls=%async_computation.4 | async-start | bytes 1310720 | tf_op jit(solution)/shard_map/all_to_all | solution.py:37
  159.1 8.0 %shard_map.108 = bf16[128,8192]{1,0:T(8,128)(2,1)} custom-call(bf16[128,512]{1,0:T(8,128)(2,1)} %get-tuple-element.44.key_ref, bf16[2,4,8,128,512]{4,3,2,1,0:T(8,128)(2,1)} %bitcast.14, bf16[128,8192]{1,0:T(8,128)(2,1)} %x_ref.3, f32[128,128]{1,0:T(8,128)} %get-tuple-element.45.scale_ref, f32[64,128]{1,0:T(8,128)} %get-tuple-element.46.gain_ref), custom_call_target="tpu_custom_call" | custom-call | flops 1073741824 | bytes 12582912 | tf_op jit(solution)/shard_map/pallas_call | solution.py:165
  169.9 2.3 %shard_map.109 = (bf16[512,512]{1,0:T(8,128)(2,1)}, f32[16,512]{1,0:T(8,128)}, f32[16,512]{1,0:T(8,128)}) custom-call(s32[2]{0:T(128)S(1)} %pad_add_fusion.place_ref, bf16[8,64,640]{2,1,0:T(8,128)(2,1)S(1)} %all-to-all-done.4.gathered_ref, bf16[512,512]{1,0:T(8,128)(2,1)S(1)} %bitcast.12, bf16[4,16,1024]{2,1,0:T(8,128)(2,1)S(1)} %shard_map.104.refs_0_, ...), custom_call_target="tpu_custom_call" | custom-call | tf_op jit(solution)/shard_map/pallas_call | solution.py:259
  (41 shorter events, 22.0 us)
Async XLA Ops:
  8.5 16.5 %all-to-all-start = ((bf16[8,16,512]{2,1,0:T(8,128)(2,1)}), bf16[8,16,512]{2,1,0:T(8,128)(2,1)S(1)}, u32[]{:S(2)}, u32[]{:S(2)}) async-start(bf16[8,16,512]{2,1,0:T(8,128)(2,1)} %broadcast_in_dim.2), calls=%async_computation | async-start | bytes 262144 | tf_op jit(solution)/shard_map/all_to_all | solution.py:37
  18.7 140.4 %all-gather.2.cloned.1.call-start = ((), (), s32[]{:S(2)}) async-start(), calls=%async_computation.5 | async-start | bytes 8519680 | tf_op jit(solution)/shard_map/all_gather | solution.py:284
  25.7 42.4 %all-to-all-start.1 = ((bf16[8,128,1536]{2,1,0:T(8,128)(2,1)}), bf16[8,128,1536]{2,1,0:T(8,128)(2,1)S(1)}, u32[]{:S(2)}, u32[]{:S(2)}) async-start(bf16[8,128,1536]{2,1,0:T(8,128)(2,1)} %get-tuple-element.34), calls=%async_computation.1 | async-start | bytes 6291456 | tf_op jit(solution)/shard_map/all_to_all | solution.py:37
  32.0 9.3 %collective-permute-start = (bf16[16,1024]{1,0:T(8,128)(2,1)}, bf16[16,1024]{1,0:T(8,128)(2,1)S(1)}, u32[]{:S(2)}, u32[]{:S(2)}) collective-permute-start(bf16[16,1024]{1,0:T(8,128)(2,1)} %shard_map.103.refs_0_), channel_id=1, source_target_pairs={{0,128},{128,0},{256,384},{384,256},{1,129},{129,1},{257,385},{385... | collective-permute-start | bytes 98312 | tf_op jit(solution)/shard_map/ppermute | solution.py:195
  33.9 7.4 %collective-permute-start.1 = (bf16[16,1024]{1,0:T(8,128)(2,1)}, bf16[16,1024]{1,0:T(8,128)(2,1)S(1)}, u32[]{:S(2)}, u32[]{:S(2)}) collective-permute-start(bf16[16,1024]{1,0:T(8,128)(2,1)} %shard_map.103.refs_0_), channel_id=1, source_target_pairs={{0,256},{128,384},{256,0},{384,128},{1,257},{129,385},{257,1},{385... | collective-permute-start | bytes 98312 | tf_op jit(solution)/shard_map/ppermute | solution.py:195
  35.8 7.1 %collective-permute-start.2 = (bf16[16,1024]{1,0:T(8,128)(2,1)}, bf16[16,1024]{1,0:T(8,128)(2,1)S(1)}, u32[]{:S(2)}, u32[]{:S(2)}) collective-permute-start(bf16[16,1024]{1,0:T(8,128)(2,1)} %shard_map.103.refs_0_), channel_id=1, source_target_pairs={{0,384},{128,256},{256,128},{384,0},{1,385},{129,257},{257,129},{3... | collective-permute-start | bytes 98312 | tf_op jit(solution)/shard_map/ppermute | solution.py:195
  42.9 0.8 copy-start.3
  69.9 1.0 copy-start
  70.9 52.3 %all-to-all-start.2 = ((bf16[64,16,512]{2,1,0:T(8,128)(2,1)}), bf16[64,16,512]{2,1,0:T(8,128)(2,1)S(1)}, u32[]{:S(2)}, u32[]{:S(2)}) async-start(bf16[64,16,512]{2,1,0:T(8,128)(2,1)} %bitcast.11), calls=%async_computation.2 | async-start | bytes 2097152 | tf_op jit(solution)/shard_map/all_to_all | solution.py:37
  82.8 15.7 %collective-permute-start.3 = (bf16[4,16,1024]{2,1,0:T(8,128)(2,1)S(1)}, bf16[4,16,1024]{2,1,0:T(8,128)(2,1)S(1)}, u32[]{:S(2)}, u32[]{:S(2)}) collective-permute-start(bf16[4,16,1024]{2,1,0:T(8,128)(2,1)S(1)} %shard_map.104.refs_0_), channel_id=1, source_target_pairs={{0,16},{16,0},{32,48},{48,32},{64,80},{80,64},{96,112},{112,96},{1... | collective-permute-start | bytes 393224 | tf_op jit(solution)/shard_map/ppermute | solution.py:195
  85.9 15.5 %collective-permute-start.4 = (bf16[4,16,1024]{2,1,0:T(8,128)(2,1)S(1)}, bf16[4,16,1024]{2,1,0:T(8,128)(2,1)S(1)}, u32[]{:S(2)}, u32[]{:S(2)}) collective-permute-start(bf16[4,16,1024]{2,1,0:T(8,128)(2,1)S(1)} %shard_map.104.refs_0_), channel_id=1, source_target_pairs={{0,32},{16,48},{32,0},{48,16},{64,96},{80,112},{96,64},{112,80},{1... | collective-permute-start | bytes 393224 | tf_op jit(solution)/shard_map/ppermute | solution.py:195
  88.1 17.2 %collective-permute-start.5 = (bf16[4,16,1024]{2,1,0:T(8,128)(2,1)S(1)}, bf16[4,16,1024]{2,1,0:T(8,128)(2,1)S(1)}, u32[]{:S(2)}, u32[]{:S(2)}) collective-permute-start(bf16[4,16,1024]{2,1,0:T(8,128)(2,1)S(1)} %shard_map.104.refs_0_), channel_id=1, source_target_pairs={{0,48},{16,32},{32,16},{48,0},{64,112},{80,96},{96,80},{112,64},{1... | collective-permute-start | bytes 393224 | tf_op jit(solution)/shard_map/ppermute | solution.py:195
  91.4 13.9 %collective-permute-start.6 = (bf16[4,16,1024]{2,1,0:T(8,128)(2,1)S(1)}, bf16[4,16,1024]{2,1,0:T(8,128)(2,1)S(1)}, u32[]{:S(2)}, u32[]{:S(2)}) collective-permute-start(bf16[4,16,1024]{2,1,0:T(8,128)(2,1)S(1)} %shard_map.104.refs_0_), channel_id=1, source_target_pairs={{0,64},{16,80},{32,96},{48,112},{64,0},{80,16},{96,32},{112,48},{1... | collective-permute-start | bytes 393224 | tf_op jit(solution)/shard_map/ppermute | solution.py:195
  93.7 11.6 %collective-permute-start.7 = (bf16[4,16,1024]{2,1,0:T(8,128)(2,1)S(1)}, bf16[4,16,1024]{2,1,0:T(8,128)(2,1)S(1)}, u32[]{:S(2)}, u32[]{:S(2)}) collective-permute-start(bf16[4,16,1024]{2,1,0:T(8,128)(2,1)S(1)} %shard_map.104.refs_0_), channel_id=1, source_target_pairs={{0,80},{16,64},{32,112},{48,96},{64,16},{80,0},{96,48},{112,32},{1... | collective-permute-start | bytes 393224 | tf_op jit(solution)/shard_map/ppermute | solution.py:195
  98.6 8.3 %collective-permute-start.8 = (bf16[4,16,1024]{2,1,0:T(8,128)(2,1)S(1)}, bf16[4,16,1024]{2,1,0:T(8,128)(2,1)S(1)}, u32[]{:S(2)}, u32[]{:S(2)}) collective-permute-start(bf16[4,16,1024]{2,1,0:T(8,128)(2,1)S(1)} %shard_map.104.refs_0_), channel_id=1, source_target_pairs={{0,96},{16,112},{32,64},{48,80},{64,32},{80,48},{96,0},{112,16},{1... | collective-permute-start | bytes 393224 | tf_op jit(solution)/shard_map/ppermute | solution.py:195
  101.4 8.9 %collective-permute-start.9 = (bf16[4,16,1024]{2,1,0:T(8,128)(2,1)S(1)}, bf16[4,16,1024]{2,1,0:T(8,128)(2,1)S(1)}, u32[]{:S(2)}, u32[]{:S(2)}) collective-permute-start(bf16[4,16,1024]{2,1,0:T(8,128)(2,1)S(1)} %shard_map.104.refs_0_), channel_id=1, source_target_pairs={{0,112},{16,96},{32,80},{48,64},{64,48},{80,32},{96,16},{112,0},{1... | collective-permute-start | bytes 393224 | tf_op jit(solution)/shard_map/ppermute | solution.py:195
  124.1 13.5 %collective-permute-start.10 = (f32[16,512]{1,0:T(8,128)S(1)}, f32[16,512]{1,0:T(8,128)S(1)}, u32[]{:S(2)}, u32[]{:S(2)}) collective-permute-start(f32[16,512]{1,0:T(8,128)S(1)} %get-tuple-element.42), channel_id=1, source_target_pairs={{0,0},{2,16},{4,32},{6,48},{8,64},{10,80},{12,96},{14,112},{16,2},... | collective-permute-start | bytes 98312 | tf_op jit(solution)/shard_map/ppermute | solution.py:300
  130.6 17.9 %all-to-all-start.3 = ((f32[64,1,128]{2,1,0:T(1,128)}), f32[64,1,128]{2,1,0:T(1,128)S(1)}, u32[]{:S(2)}, u32[]{:S(2)}) async-start(f32[64,1,128]{2,1,0:T(1,128)} %bitcast.5), calls=%async_computation.3 | async-start | bytes 65536 | tf_op jit(solution)/shard_map/all_to_all | solution.py:37
  137.6 10.9 %collective-permute-start.11 = (f32[16,512]{1,0:T(8,128)S(1)}, f32[16,512]{1,0:T(8,128)S(1)}, u32[]{:S(2)}, u32[]{:S(2)}) collective-permute-start(f32[16,512]{1,0:T(8,128)S(1)} %collective-permute-done.10.s0_ref.refs_8_), channel_id=1, source_target_pairs={{0,128},{128,0},{256,384},{384,256},{1,129},{129,1},{257,385},{385... | collective-permute-start | bytes 98312 | tf_op jit(solution)/shard_map/ppermute | solution.py:195
  140.5 8.0 %collective-permute-start.12 = (f32[16,512]{1,0:T(8,128)S(1)}, f32[16,512]{1,0:T(8,128)S(1)}, u32[]{:S(2)}, u32[]{:S(2)}) collective-permute-start(f32[16,512]{1,0:T(8,128)S(1)} %collective-permute-done.10.s0_ref.refs_8_), channel_id=1, source_target_pairs={{0,256},{128,384},{256,0},{384,128},{1,257},{129,385},{257,1},{385... | collective-permute-start | bytes 98312 | tf_op jit(solution)/shard_map/ppermute | solution.py:195
  144.7 7.1 %collective-permute-start.13 = (f32[16,512]{1,0:T(8,128)S(1)}, f32[16,512]{1,0:T(8,128)S(1)}, u32[]{:S(2)}, u32[]{:S(2)}) collective-permute-start(f32[16,512]{1,0:T(8,128)S(1)} %collective-permute-done.10.s0_ref.refs_8_), channel_id=1, source_target_pairs={{0,384},{128,256},{256,128},{384,0},{1,385},{129,257},{257,129},{3... | collective-permute-start | bytes 98312 | tf_op jit(solution)/shard_map/ppermute | solution.py:195
  152.8 17.1 %all-to-all-start.4 = ((bf16[8,64,640]{2,1,0:T(8,128)(2,1)}), bf16[8,64,640]{2,1,0:T(8,128)(2,1)S(1)}, u32[]{:S(2)}, u32[]{:S(2)}) async-start(bf16[8,64,640]{2,1,0:T(8,128)(2,1)} %shard_map.107), calls=%async_computation.4 | async-start | bytes 1310720 | tf_op jit(solution)/shard_map/all_to_all | solution.py:37
  159.1 10.8 %copy-start.1 = (f32[16,512]{1,0:T(8,128)S(1)}, f32[16,512]{1,0:T(8,128)}, u32[]{:S(2)}) copy-start(f32[16,512]{1,0:T(8,128)} %refs_9_.1) | copy-start | bytes 98308
  159.1 10.8 %copy-start.2 = (f32[16,512]{1,0:T(8,128)S(1)}, f32[16,512]{1,0:T(8,128)}, u32[]{:S(2)}) copy-start(f32[16,512]{1,0:T(8,128)} %refs_10_.1) | copy-start | bytes 98308
  (1 other events, 0.7 us)
Sparse Core Ops, SparseCore 0:
  25.8 124.8 all-gather.1

commit v8 on v5

--- a/solution.py
+++ b/solution.py
@@ -296,7 +296,7 @@
     grad_shard = lax.ppermute(piece, ("x", "c", "z"), swap)
     shards = [grad_shard, *from_others(grad_shard, "yl")]
     late = late_rows(exchange(square, PLANE), shards)
-    late, weights = lax.optimization_barrier((late, weights))
+    weights, _ = lax.optimization_barrier((weights, late))
     gathered = exchange(late, GROUP)
     input_grad = backward(keys, weights, norm_input, scale, gain)
     weights, input_grad = lax.optimization_barrier((weights, input_grad))

time: 178 us -> 178 us (level)
  starting transfers between devices: 54.1 us -> 56.6 us
  waiting for transfers between devices: 36.3 us -> 33.8 us
    all_gather x1, waiting for transfers between devices: 2.54 us -> 0.01 us  [body(): lax.all_gather(state[:, :512], ('yh', 'yl', 'z'), axis=0, tiled=True)]
    all_to_all x4, starting transfers between devices: 26.3 us -> 28.9 us  [exchange(): return lax.all_to_all(x, axes, split_axis=0, concat_axis=0, tiled=True)]
  transfers between devices with their start and end apart: 12 -> 12, of which waited for: 8 -> 7; matrix products, arithmetic and copies ran while one was open for 2% -> 2% of each run, Pallas kernels for 9% -> 9%
where the time goes in v8:
time: 178 us; the launch traced here: 177 us
  starting transfers between devices  56.6 us (32%)
  blocking collectives  46.2 us (26%)
  waiting for transfers between devices  33.8 us (19%)
  Pallas kernels  19.8 us (11%)
  between operations  14.2 us (8%)
  local copies, waits for them, and re-layouts  4.96 us (3%)
    all_to_all x1, blocking collectives, exchange(): return lax.all_to_all(x, axes, split_axis=0, concat_axis=0, tiled=True)  46.2 us
    all_to_all x4, starting transfers between devices, exchange(): return lax.all_to_all(x, axes, split_axis=0, concat_axis=0, tiled=True)  28.9 us
    ppermute x6, waiting for transfers between devices, from_others(): lax.ppermute(x, axis, [(i, i ^ k) for i in range(count)])  18.8 us
    ppermute x6, starting transfers between devices, from_others(): lax.ppermute(x, axis, [(i, i ^ k) for i in range(count)])  18.6 us
    all_to_all x4, waiting for transfers between devices, exchange(): return lax.all_to_all(x, axes, split_axis=0, concat_axis=0, tiled=True)  14.9 us
    ppermute x1, starting transfers between devices, body(): grad_shard = lax.ppermute(piece, ('x', 'c', 'z'), swap)  9.18 us
    pallas_call x1, Pallas kernels, backward(): pl.pallas_call(backward_kernel, grid=(steps,), in_specs=[whole(keys), pl....  8.05 us
    pallas_call x1, Pallas kernels, prepare(): pl.pallas_call(prepare_kernel, grid=(tokens // tile,), in_specs=[pl.Block...  4.75 us
  transfers between devices with their start and end apart: 12, of which 7 were waited for; matrix products, arithmetic and copies ran while one was open for 2% of the time, Pallas kernels for 9%

profile of v8, /device:TPU:1, one launch (start us, length us, event | category | flops | bytes accessed | tf_op | source)
XLA Modules:
  0.0 177.1 jit_solution(11113733589316929020)
XLA Ops:
  7.2 1.6 shard_map.103
  8.7 10.2 %all-to-all-start = ((bf16[8,16,1536]{2,1,0:T(8,128)(2,1)}), bf16[8,16,1536]{2,1,0:T(8,128)(2,1)S(1)}, u32[]{:S(2)}, u32[]{:S(2)}) async-start(bf16[8,16,1536]{2,1,0:T(8,128)(2,1)} %shard_map.103), calls=%async_computation | async-start | bytes 786432 | tf_op jit(solution)/shard_map/all_to_all | solution.py:37
  20.6 4.8 %shard_map.102 = (bf16[8,128,1536]{2,1,0:T(8,128)(2,1)}, bf16[128,512]{1,0:T(8,128)(2,1)}, f32[128,128]{1,0:T(8,128)}, f32[64,128]{1,0:T(8,128)}) custom-call(bf16[128,8192]{1,0:T(8,128)(2,1)} %x_ref.3, bf16[128,512]{1,0:T(8,128)(2,1)} %key_ref.1, f32[128,64]{1,0:T(8,128)} %get-tuple-element.43.cos_ref, f32[128,64]{1,0:T(8,128)} %get-tuple-element.42.sin_ref, ...), custom_call_target="tpu_custom_call" | custom-call | flops 8388608 | bytes 6291456 | tf_op jit(solution)/shard_map/pallas_call | solution.py:73
  25.4 1.7 all-to-all-done
  27.9 4.4 %all-to-all-start.1 = ((bf16[8,128,1536]{2,1,0:T(8,128)(2,1)}), bf16[8,128,1536]{2,1,0:T(8,128)(2,1)S(1)}, u32[]{:S(2)}, u32[]{:S(2)}) async-start(bf16[8,128,1536]{2,1,0:T(8,128)(2,1)} %get-tuple-element.25), calls=%async_computation.1 | async-start | bytes 6291456 | tf_op jit(solution)/shard_map/all_to_all | solution.py:37
  33.2 1.9 %collective-permute-start = (bf16[128,1024]{1,0:T(8,128)(2,1)S(1)}, bf16[128,1024]{1,0:T(8,128)(2,1)S(1)}, u32[]{:S(2)}, u32[]{:S(2)}) collective-permute-start(bf16[128,1024]{1,0:T(8,128)(2,1)S(1)} %slice.7.m0_ref), channel_id=1, source_target_pairs={{0,128},{128,0},{256,384},{384,256},{1,129},{129,1},{257,385},{385... | collective-permute-start | bytes 786440 | tf_op jit(solution)/shard_map/ppermute | solution.py:195
  35.2 1.9 %collective-permute-start.1 = (bf16[128,1024]{1,0:T(8,128)(2,1)S(1)}, bf16[128,1024]{1,0:T(8,128)(2,1)S(1)}, u32[]{:S(2)}, u32[]{:S(2)}) collective-permute-start(bf16[128,1024]{1,0:T(8,128)(2,1)S(1)} %slice.7.m0_ref), channel_id=1, source_target_pairs={{0,256},{128,384},{256,0},{384,128},{1,257},{129,385},{257,1},{385... | collective-permute-start | bytes 786440 | tf_op jit(solution)/shard_map/ppermute | solution.py:195
  37.1 5.5 %collective-permute-start.2 = (bf16[128,1024]{1,0:T(8,128)(2,1)S(1)}, bf16[128,1024]{1,0:T(8,128)(2,1)S(1)}, u32[]{:S(2)}, u32[]{:S(2)}) collective-permute-start(bf16[128,1024]{1,0:T(8,128)(2,1)S(1)} %slice.7.m0_ref), channel_id=1, source_target_pairs={{0,384},{128,256},{256,128},{384,0},{1,385},{129,257},{257,129},{3... | collective-permute-start | bytes 786440 | tf_op jit(solution)/shard_map/ppermute | solution.py:195
  42.6 1.7 collective-permute-done.m1_ref
  44.9 13.6 %collective-permute-done.1.m2_ref = bf16[128,1024]{1,0:T(8,128)(2,1)S(1)} collective-permute-done((bf16[128,1024]{1,0:T(8,128)(2,1)S(1)}, bf16[128,1024]{1,0:T(8,128)(2,1)S(1)}, u32[]{:S(2)}, u32[]{:S(2)}) %collective-permute-start.1) | collective-permute-done | bytes 262176 | tf_op jit(solution)/shard_map/ppermute | solution.py:195
  60.0 9.9 %all-to-all-done.1.key_ref.normed_ref = bf16[8,128,1536]{2,1,0:T(8,128)(2,1)S(1)} async-done(((bf16[8,128,1536]{2,1,0:T(8,128)(2,1)}), bf16[8,128,1536]{2,1,0:T(8,128)(2,1)S(1)}, u32[]{:S(2)}, u32[]{:S(2)}) %all-to-all-start.1) | async-done | bytes 3145760 | tf_op jit(solution)/shard_map/all_to_all | solution.py:37
  69.9 1.8 %shard_map.104 = bf16[32,2,16,512]{3,2,1,0:T(8,128)(2,1)S(1)} custom-call(bf16[8,128,1536]{2,1,0:T(8,128)(2,1)S(1)} %all-to-all-done.1.key_ref.normed_ref, bf16[8,128,1536]{2,1,0:T(8,128)(2,1)S(1)} %all-to-all-done.1.key_ref.normed_ref), custom_call_target="tpu_custom_call" | custom-call | flops 1073741824 | bytes 4194304 | tf_op jit(solution)/shard_map/pallas_call | solution.py:111
  71.6 46.2 %all_to_all.31.pieces_ref = bf16[64,16,512]{2,1,0:T(8,128)(2,1)S(1)} all-to-all(bf16[64,16,512]{2,1,0:T(8,128)(2,1)S(1)} %bitcast.10), channel_id=1, replica_groups=mesh['yl'=4,'x'=4,'c'=2,'z'=8,'yh'=2] {'yl','z','yh'}, dimensions={0} | all-to-all | bytes 2097152 | tf_op jit(solution)/shard_map/all_to_all | solution.py:37
  118.7 9.2 %collective-permute-start.3 = (f32[16,512]{1,0:T(8,128)S(1)}, f32[16,512]{1,0:T(8,128)S(1)}, u32[]{:S(2)}, u32[]{:S(2)}) collective-permute-start(f32[16,512]{1,0:T(8,128)S(1)} %get-tuple-element.28), channel_id=1, source_target_pairs={{0,0},{2,16},{4,32},{6,48},{8,64},{10,80},{12,96},{14,112},{16,2},... | collective-permute-start | bytes 98312 | tf_op jit(solution)/shard_map/ppermute | solution.py:296
  127.9 6.9 %all-to-all-start.3 = ((f32[64,1,128]{2,1,0:T(1,128)}), f32[64,1,128]{2,1,0:T(1,128)S(1)}, u32[]{:S(2)}, u32[]{:S(2)}) async-start(f32[64,1,128]{2,1,0:T(1,128)} %bitcast.5), calls=%async_computation.3 | async-start | bytes 65536 | tf_op jit(solution)/shard_map/all_to_all | solution.py:37
  134.8 2.9 %collective-permute-start.4 = (f32[16,512]{1,0:T(8,128)S(1)}, f32[16,512]{1,0:T(8,128)S(1)}, u32[]{:S(2)}, u32[]{:S(2)}) collective-permute-start(f32[16,512]{1,0:T(8,128)S(1)} %collective-permute-done.3.s0_ref.shard_ref), channel_id=1, source_target_pairs={{0,128},{128,0},{256,384},{384,256},{1,129},{129,1},{257,385},{385... | collective-permute-start | bytes 98312 | tf_op jit(solution)/shard_map/ppermute | solution.py:195
  137.8 4.2 %collective-permute-start.5 = (f32[16,512]{1,0:T(8,128)S(1)}, f32[16,512]{1,0:T(8,128)S(1)}, u32[]{:S(2)}, u32[]{:S(2)}) collective-permute-start(f32[16,512]{1,0:T(8,128)S(1)} %collective-permute-done.3.s0_ref.shard_ref), channel_id=1, source_target_pairs={{0,256},{128,384},{256,0},{384,128},{1,257},{129,385},{257,1},{385... | collective-permute-start | bytes 98312 | tf_op jit(solution)/shard_map/ppermute | solution.py:195
  142.0 2.2 %collective-permute-start.6 = (f32[16,512]{1,0:T(8,128)S(1)}, f32[16,512]{1,0:T(8,128)S(1)}, u32[]{:S(2)}, u32[]{:S(2)}) collective-permute-start(f32[16,512]{1,0:T(8,128)S(1)} %collective-permute-done.3.s0_ref.shard_ref), channel_id=1, source_target_pairs={{0,384},{128,256},{256,128},{384,0},{1,385},{129,257},{257,129},{3... | collective-permute-start | bytes 98312 | tf_op jit(solution)/shard_map/ppermute | solution.py:195
  144.1 1.6 all-to-all-done.3
  145.7 3.6 %collective-permute-done.6.s3_ref = f32[16,512]{1,0:T(8,128)S(1)} collective-permute-done((f32[16,512]{1,0:T(8,128)S(1)}, f32[16,512]{1,0:T(8,128)S(1)}, u32[]{:S(2)}, u32[]{:S(2)}) %collective-permute-start.6) | collective-permute-done | bytes 32800 | tf_op jit(solution)/shard_map/ppermute | solution.py:195
  150.3 7.3 %all-to-all-start.4 = ((bf16[8,64,640]{2,1,0:T(8,128)(2,1)}), bf16[8,64,640]{2,1,0:T(8,128)(2,1)S(1)}, u32[]{:S(2)}, u32[]{:S(2)}) async-start(bf16[8,64,640]{2,1,0:T(8,128)(2,1)} %shard_map.106), calls=%async_computation.4 | async-start | bytes 1310720 | tf_op jit(solution)/shard_map/all_to_all | solution.py:37
  157.6 8.0 %shard_map.107 = bf16[128,8192]{1,0:T(8,128)(2,1)} custom-call(bf16[128,512]{1,0:T(8,128)(2,1)} %get-tuple-element.30.key_ref, bf16[2,4,8,128,512]{4,3,2,1,0:T(8,128)(2,1)} %bitcast.13, bf16[128,8192]{1,0:T(8,128)(2,1)} %x_ref.3, f32[128,128]{1,0:T(8,128)} %get-tuple-element.31.scale_ref, f32[64,128]{1,0:T(8,128)} %get-tuple-element.32.gain_ref), custom_call_target="tpu_custom_call" | custom-call | flops 1073741824 | bytes 12582912 | tf_op jit(solution)/shard_map/pallas_call | solution.py:165
  166.8 1.7 all-to-all-done.4.gathered_ref
  168.5 1.8 shard_map.108
  (33 shorter events, 8.5 us)
Async XLA Ops:
  8.7 18.3 %all-to-all-start = ((bf16[8,16,1536]{2,1,0:T(8,128)(2,1)}), bf16[8,16,1536]{2,1,0:T(8,128)(2,1)S(1)}, u32[]{:S(2)}, u32[]{:S(2)}) async-start(bf16[8,16,1536]{2,1,0:T(8,128)(2,1)} %shard_map.103), calls=%async_computation | async-start | bytes 786432 | tf_op jit(solution)/shard_map/all_to_all | solution.py:37
  19.0 138.6 %all-gather.2.cloned.1.call-start = ((), (), s32[]{:S(2)}) async-start(), calls=%async_computation.5 | async-start | bytes 8519680 | tf_op jit(solution)/shard_map/all_gather | solution.py:285
  27.1 0.8 copy-start.8
  27.9 42.0 %all-to-all-start.1 = ((bf16[8,128,1536]{2,1,0:T(8,128)(2,1)}), bf16[8,128,1536]{2,1,0:T(8,128)(2,1)S(1)}, u32[]{:S(2)}, u32[]{:S(2)}) async-start(bf16[8,128,1536]{2,1,0:T(8,128)(2,1)} %get-tuple-element.25), calls=%async_computation.1 | async-start | bytes 6291456 | tf_op jit(solution)/shard_map/all_to_all | solution.py:37
  33.2 11.0 %collective-permute-start = (bf16[128,1024]{1,0:T(8,128)(2,1)S(1)}, bf16[128,1024]{1,0:T(8,128)(2,1)S(1)}, u32[]{:S(2)}, u32[]{:S(2)}) collective-permute-start(bf16[128,1024]{1,0:T(8,128)(2,1)S(1)} %slice.7.m0_ref), channel_id=1, source_target_pairs={{0,128},{128,0},{256,384},{384,256},{1,129},{129,1},{257,385},{385... | collective-permute-start | bytes 786440 | tf_op jit(solution)/shard_map/ppermute | solution.py:195
  35.2 23.4 %collective-permute-start.1 = (bf16[128,1024]{1,0:T(8,128)(2,1)S(1)}, bf16[128,1024]{1,0:T(8,128)(2,1)S(1)}, u32[]{:S(2)}, u32[]{:S(2)}) collective-permute-start(bf16[128,1024]{1,0:T(8,128)(2,1)S(1)} %slice.7.m0_ref), channel_id=1, source_target_pairs={{0,256},{128,384},{256,0},{384,128},{1,257},{129,385},{257,1},{385... | collective-permute-start | bytes 786440 | tf_op jit(solution)/shard_map/ppermute | solution.py:195
  37.1 22.1 %collective-permute-start.2 = (bf16[128,1024]{1,0:T(8,128)(2,1)S(1)}, bf16[128,1024]{1,0:T(8,128)(2,1)S(1)}, u32[]{:S(2)}, u32[]{:S(2)}) collective-permute-start(bf16[128,1024]{1,0:T(8,128)(2,1)S(1)} %slice.7.m0_ref), channel_id=1, source_target_pairs={{0,384},{128,256},{256,128},{384,0},{1,385},{129,257},{257,129},{3... | collective-permute-start | bytes 786440 | tf_op jit(solution)/shard_map/ppermute | solution.py:195
  44.2 0.7 copy-start
  58.5 0.7 copy-start.2
  59.2 0.7 copy-start.4
  118.7 16.1 %collective-permute-start.3 = (f32[16,512]{1,0:T(8,128)S(1)}, f32[16,512]{1,0:T(8,128)S(1)}, u32[]{:S(2)}, u32[]{:S(2)}) collective-permute-start(f32[16,512]{1,0:T(8,128)S(1)} %get-tuple-element.28), channel_id=1, source_target_pairs={{0,0},{2,16},{4,32},{6,48},{8,64},{10,80},{12,96},{14,112},{16,2},... | collective-permute-start | bytes 98312 | tf_op jit(solution)/shard_map/ppermute | solution.py:296
  127.9 17.8 %all-to-all-start.3 = ((f32[64,1,128]{2,1,0:T(1,128)}), f32[64,1,128]{2,1,0:T(1,128)S(1)}, u32[]{:S(2)}, u32[]{:S(2)}) async-start(f32[64,1,128]{2,1,0:T(1,128)} %bitcast.5), calls=%async_computation.3 | async-start | bytes 65536 | tf_op jit(solution)/shard_map/all_to_all | solution.py:37
  134.8 10.9 %collective-permute-start.4 = (f32[16,512]{1,0:T(8,128)S(1)}, f32[16,512]{1,0:T(8,128)S(1)}, u32[]{:S(2)}, u32[]{:S(2)}) collective-permute-start(f32[16,512]{1,0:T(8,128)S(1)} %collective-permute-done.3.s0_ref.shard_ref), channel_id=1, source_target_pairs={{0,128},{128,0},{256,384},{384,256},{1,129},{129,1},{257,385},{385... | collective-permute-start | bytes 98312 | tf_op jit(solution)/shard_map/ppermute | solution.py:195
  137.8 7.9 %collective-permute-start.5 = (f32[16,512]{1,0:T(8,128)S(1)}, f32[16,512]{1,0:T(8,128)S(1)}, u32[]{:S(2)}, u32[]{:S(2)}) collective-permute-start(f32[16,512]{1,0:T(8,128)S(1)} %collective-permute-done.3.s0_ref.shard_ref), channel_id=1, source_target_pairs={{0,256},{128,384},{256,0},{384,128},{1,257},{129,385},{257,1},{385... | collective-permute-start | bytes 98312 | tf_op jit(solution)/shard_map/ppermute | solution.py:195
  142.0 7.3 %collective-permute-start.6 = (f32[16,512]{1,0:T(8,128)S(1)}, f32[16,512]{1,0:T(8,128)S(1)}, u32[]{:S(2)}, u32[]{:S(2)}) collective-permute-start(f32[16,512]{1,0:T(8,128)S(1)} %collective-permute-done.3.s0_ref.shard_ref), channel_id=1, source_target_pairs={{0,384},{128,256},{256,128},{384,0},{1,385},{129,257},{257,129},{3... | collective-permute-start | bytes 98312 | tf_op jit(solution)/shard_map/ppermute | solution.py:195
  150.3 18.2 %all-to-all-start.4 = ((bf16[8,64,640]{2,1,0:T(8,128)(2,1)}), bf16[8,64,640]{2,1,0:T(8,128)(2,1)S(1)}, u32[]{:S(2)}, u32[]{:S(2)}) async-start(bf16[8,64,640]{2,1,0:T(8,128)(2,1)} %shard_map.106), calls=%async_computation.4 | async-start | bytes 1310720 | tf_op jit(solution)/shard_map/all_to_all | solution.py:37
  157.6 10.9 %copy-start.1 = (bf16[128,1024]{1,0:T(8,128)(2,1)S(1)}, bf16[128,1024]{1,0:T(8,128)(2,1)}, u32[]{:S(2)}) copy-start(bf16[128,1024]{1,0:T(8,128)(2,1)} %copy-done) | copy-start | bytes 786436
  157.6 10.9 %copy-start.3 = (bf16[128,1024]{1,0:T(8,128)(2,1)S(1)}, bf16[128,1024]{1,0:T(8,128)(2,1)}, u32[]{:S(2)}) copy-start(bf16[128,1024]{1,0:T(8,128)(2,1)} %copy-done.2) | copy-start | bytes 786436
  157.6 10.9 %copy-start.5 = (bf16[128,1024]{1,0:T(8,128)(2,1)S(1)}, bf16[128,1024]{1,0:T(8,128)(2,1)}, u32[]{:S(2)}) copy-start(bf16[128,1024]{1,0:T(8,128)(2,1)} %copy-done.4) | copy-start | bytes 786436
  157.6 10.9 %copy-start.6 = (f32[16,512]{1,0:T(8,128)S(1)}, f32[16,512]{1,0:T(8,128)}, u32[]{:S(2)}) copy-start(f32[16,512]{1,0:T(8,128)} %first_ref.3) | copy-start | bytes 98308
  157.6 10.9 %copy-start.7 = (f32[16,512]{1,0:T(8,128)S(1)}, f32[16,512]{1,0:T(8,128)}, u32[]{:S(2)}) copy-start(f32[16,512]{1,0:T(8,128)} %second_ref.3) | copy-start | bytes 98308
Sparse Core Ops, SparseCore 0:
  27.9 124.8 all-gather.1

commit v9 on v8

--- a/solution.py
+++ b/solution.py
@@ -126,7 +126,7 @@
 
 def backward_kernel(key_ref, weight_ref, x_ref, scale_ref, gain_ref, out_ref, held, cross):
     step = pl.program_id(0)
-    deep, width = weight_ref.shape[2], weight_ref.shape[4]
+    deep, width = weight_ref.shape[0], weight_ref.shape[4]
 
     @pl.when(step == 0)
     def _():
@@ -136,7 +136,7 @@
     for z in range(deep):
         for yh in range(2):
             block = (step * deep + z) * 2 + yh
-            up = jnp.dot(key_ref[...], weight_ref[yh, :, z].reshape(KV, width), preferred_element_type=f32)
+            up = jnp.dot(key_ref[...], weight_ref[z, yh].reshape(KV, width), preferred_element_type=f32)
             for k in range(width // HEAD):
                 group = block * (width // HEAD) + k
                 columns = pl.ds(pl.multiple_of(group * HEAD, HEAD), HEAD)
@@ -167,7 +167,7 @@
         grid=(steps,),
         in_specs=[
             whole(keys),
-            pl.BlockSpec((2, 4, deep, 128, width), lambda t: (0, 0, t, 0, 0)),
+            pl.BlockSpec((deep, 2, 4, 128, width), lambda t: (t, 0, 0, 0, 0)),
             whole(x),
             whole(scale),
             whole(gain),
@@ -282,7 +282,7 @@
     send, keys, scale, gain = prepare(norm_input, key_grad, cosine, sine, norm_gain.reshape(D // HEAD, HEAD))
     send, state = lax.optimization_barrier((send, state))
 
-    weights = lax.all_gather(state[:, :512], ("yh", "yl", "z"), axis=0, tiled=True).reshape(2, 4, 8, 128, 512)
+    weights = lax.all_gather(state[:, :512], ("z", "yh", "yl"), axis=0, tiled=True).reshape(8, 2, 4, 128, 512)
 
     received = exchange(send, GROUP)
     moments = state[:, 512:]
@@ -300,8 +300,8 @@
     gathered = exchange(late, GROUP)
     input_grad = backward(keys, weights, norm_input, scale, gain)
     weights, input_grad = lax.optimization_barrier((weights, input_grad))
-    at = (lax.axis_index("yh"), 0, lax.axis_index("z"), 0, 0)
-    weight = lax.dynamic_slice(weights, at, (1, 4, 1, 128, 512)).reshape(KV, 512)
+    at = (lax.axis_index("z"), lax.axis_index("yh"), 0, 0, 0)
+    weight = lax.dynamic_slice(weights, at, (1, 1, 4, 128, 512)).reshape(KV, 512)
     place = lax.axis_index("yl").astype(jnp.int32).reshape(1)
     new_weight, new_first, new_second = update(
         place, gathered, weight, *moments, grad_shard, first_moment, second_moment

time: 178 us -> 178 us (level)
  no operation moved by 1% of the time
where the time goes in v9:
time: 178 us; the launch traced here: 177 us
  starting transfers between devices  56.6 us (32%)
  blocking collectives  46.2 us (26%)
  waiting for transfers between devices  33.8 us (19%)
  Pallas kernels  19.8 us (11%)
  between operations  14.2 us (8%)
  local copies, waits for them, and re-layouts  4.96 us (3%)
    all_to_all x1, blocking collectives, exchange(): return lax.all_to_all(x, axes, split_axis=0, concat_axis=0, tiled=True)  46.2 us
    all_to_all x4, starting transfers between devices, exchange(): return lax.all_to_all(x, axes, split_axis=0, concat_axis=0, tiled=True)  28.9 us
    ppermute x6, waiting for transfers between devices, from_others(): lax.ppermute(x, axis, [(i, i ^ k) for i in range(count)])  18.9 us
    ppermute x6, starting transfers between devices, from_others(): lax.ppermute(x, axis, [(i, i ^ k) for i in range(count)])  18.6 us
    all_to_all x4, waiting for transfers between devices, exchange(): return lax.all_to_all(x, axes, split_axis=0, concat_axis=0, tiled=True)  14.9 us
    ppermute x1, starting transfers between devices, body(): grad_shard = lax.ppermute(piece, ('x', 'c', 'z'), swap)  9.13 us
    pallas_call x1, Pallas kernels, backward(): pl.pallas_call(backward_kernel, grid=(steps,), in_specs=[whole(keys), pl....  8.03 us
    pallas_call x1, Pallas kernels, prepare(): pl.pallas_call(prepare_kernel, grid=(tokens // tile,), in_specs=[pl.Block...  4.75 us
  transfers between devices with their start and end apart: 12, of which 7 were waited for; matrix products, arithmetic and copies ran while one was open for 2% of the time, Pallas kernels for 9%

profile of v9, /device:TPU:1, one launch (start us, length us, event | category | flops | bytes accessed | tf_op | source)
XLA Modules:
  0.0 177.1 jit_solution(8652951221323267112)
XLA Ops:
  7.2 1.6 shard_map.103
  8.7 10.2 %all-to-all-start = ((bf16[8,16,1536]{2,1,0:T(8,128)(2,1)}), bf16[8,16,1536]{2,1,0:T(8,128)(2,1)S(1)}, u32[]{:S(2)}, u32[]{:S(2)}) async-start(bf16[8,16,1536]{2,1,0:T(8,128)(2,1)} %shard_map.103), calls=%async_computation | async-start | bytes 786432 | tf_op jit(solution)/shard_map/all_to_all | solution.py:37
  20.6 4.8 %shard_map.102 = (bf16[8,128,1536]{2,1,0:T(8,128)(2,1)}, bf16[128,512]{1,0:T(8,128)(2,1)}, f32[128,128]{1,0:T(8,128)}, f32[64,128]{1,0:T(8,128)}) custom-call(bf16[128,8192]{1,0:T(8,128)(2,1)} %x_ref.3, bf16[128,512]{1,0:T(8,128)(2,1)} %key_ref.1, f32[128,64]{1,0:T(8,128)} %get-tuple-element.43.cos_ref, f32[128,64]{1,0:T(8,128)} %get-tuple-element.42.sin_ref, ...), custom_call_target="tpu_custom_call" | custom-call | flops 8388608 | bytes 6291456 | tf_op jit(solution)/shard_map/pallas_call | solution.py:73
  25.4 1.7 all-to-all-done
  27.9 4.4 %all-to-all-start.1 = ((bf16[8,128,1536]{2,1,0:T(8,128)(2,1)}), bf16[8,128,1536]{2,1,0:T(8,128)(2,1)S(1)}, u32[]{:S(2)}, u32[]{:S(2)}) async-start(bf16[8,128,1536]{2,1,0:T(8,128)(2,1)} %get-tuple-element.25), calls=%async_computation.1 | async-start | bytes 6291456 | tf_op jit(solution)/shard_map/all_to_all | solution.py:37
  33.2 1.9 %collective-permute-start = (bf16[128,1024]{1,0:T(8,128)(2,1)S(1)}, bf16[128,1024]{1,0:T(8,128)(2,1)S(1)}, u32[]{:S(2)}, u32[]{:S(2)}) collective-permute-start(bf16[128,1024]{1,0:T(8,128)(2,1)S(1)} %slice.7.m0_ref), channel_id=1, source_target_pairs={{0,128},{128,0},{256,384},{384,256},{1,129},{129,1},{257,385},{385... | collective-permute-start | bytes 786440 | tf_op jit(solution)/shard_map/ppermute | solution.py:195
  35.2 1.9 %collective-permute-start.1 = (bf16[128,1024]{1,0:T(8,128)(2,1)S(1)}, bf16[128,1024]{1,0:T(8,128)(2,1)S(1)}, u32[]{:S(2)}, u32[]{:S(2)}) collective-permute-start(bf16[128,1024]{1,0:T(8,128)(2,1)S(1)} %slice.7.m0_ref), channel_id=1, source_target_pairs={{0,256},{128,384},{256,0},{384,128},{1,257},{129,385},{257,1},{385... | collective-permute-start | bytes 786440 | tf_op jit(solution)/shard_map/ppermute | solution.py:195
  37.1 5.5 %collective-permute-start.2 = (bf16[128,1024]{1,0:T(8,128)(2,1)S(1)}, bf16[128,1024]{1,0:T(8,128)(2,1)S(1)}, u32[]{:S(2)}, u32[]{:S(2)}) collective-permute-start(bf16[128,1024]{1,0:T(8,128)(2,1)S(1)} %slice.7.m0_ref), channel_id=1, source_target_pairs={{0,384},{128,256},{256,128},{384,0},{1,385},{129,257},{257,129},{3... | collective-permute-start | bytes 786440 | tf_op jit(solution)/shard_map/ppermute | solution.py:195
  42.6 1.7 collective-permute-done.m1_ref
  44.9 13.6 %collective-permute-done.1.m2_ref = bf16[128,1024]{1,0:T(8,128)(2,1)S(1)} collective-permute-done((bf16[128,1024]{1,0:T(8,128)(2,1)S(1)}, bf16[128,1024]{1,0:T(8,128)(2,1)S(1)}, u32[]{:S(2)}, u32[]{:S(2)}) %collective-permute-start.1) | collective-permute-done | bytes 262176 | tf_op jit(solution)/shard_map/ppermute | solution.py:195
  60.0 9.9 %all-to-all-done.1.key_ref.normed_ref = bf16[8,128,1536]{2,1,0:T(8,128)(2,1)S(1)} async-done(((bf16[8,128,1536]{2,1,0:T(8,128)(2,1)}), bf16[8,128,1536]{2,1,0:T(8,128)(2,1)S(1)}, u32[]{:S(2)}, u32[]{:S(2)}) %all-to-all-start.1) | async-done | bytes 3145760 | tf_op jit(solution)/shard_map/all_to_all | solution.py:37
  69.9 1.8 %shard_map.104 = bf16[32,2,16,512]{3,2,1,0:T(8,128)(2,1)S(1)} custom-call(bf16[8,128,1536]{2,1,0:T(8,128)(2,1)S(1)} %all-to-all-done.1.key_ref.normed_ref, bf16[8,128,1536]{2,1,0:T(8,128)(2,1)S(1)} %all-to-all-done.1.key_ref.normed_ref), custom_call_target="tpu_custom_call" | custom-call | flops 1073741824 | bytes 4194304 | tf_op jit(solution)/shard_map/pallas_call | solution.py:111
  71.6 46.2 %all_to_all.31.pieces_ref = bf16[64,16,512]{2,1,0:T(8,128)(2,1)S(1)} all-to-all(bf16[64,16,512]{2,1,0:T(8,128)(2,1)S(1)} %bitcast.10), channel_id=1, replica_groups=mesh['yl'=4,'x'=4,'c'=2,'z'=8,'yh'=2] {'yl','z','yh'}, dimensions={0} | all-to-all | bytes 2097152 | tf_op jit(solution)/shard_map/all_to_all | solution.py:37
  118.7 9.1 %collective-permute-start.3 = (f32[16,512]{1,0:T(8,128)S(1)}, f32[16,512]{1,0:T(8,128)S(1)}, u32[]{:S(2)}, u32[]{:S(2)}) collective-permute-start(f32[16,512]{1,0:T(8,128)S(1)} %get-tuple-element.28), channel_id=1, source_target_pairs={{0,0},{2,16},{4,32},{6,48},{8,64},{10,80},{12,96},{14,112},{16,2},... | collective-permute-start | bytes 98312 | tf_op jit(solution)/shard_map/ppermute | solution.py:296
  127.8 7.0 %all-to-all-start.3 = ((f32[64,1,128]{2,1,0:T(1,128)}), f32[64,1,128]{2,1,0:T(1,128)S(1)}, u32[]{:S(2)}, u32[]{:S(2)}) async-start(f32[64,1,128]{2,1,0:T(1,128)} %bitcast.5), calls=%async_computation.3 | async-start | bytes 65536 | tf_op jit(solution)/shard_map/all_to_all | solution.py:37
  134.8 2.9 %collective-permute-start.4 = (f32[16,512]{1,0:T(8,128)S(1)}, f32[16,512]{1,0:T(8,128)S(1)}, u32[]{:S(2)}, u32[]{:S(2)}) collective-permute-start(f32[16,512]{1,0:T(8,128)S(1)} %collective-permute-done.3.s0_ref.shard_ref), channel_id=1, source_target_pairs={{0,128},{128,0},{256,384},{384,256},{1,129},{129,1},{257,385},{385... | collective-permute-start | bytes 98312 | tf_op jit(solution)/shard_map/ppermute | solution.py:195
  137.8 4.2 %collective-permute-start.5 = (f32[16,512]{1,0:T(8,128)S(1)}, f32[16,512]{1,0:T(8,128)S(1)}, u32[]{:S(2)}, u32[]{:S(2)}) collective-permute-start(f32[16,512]{1,0:T(8,128)S(1)} %collective-permute-done.3.s0_ref.shard_ref), channel_id=1, source_target_pairs={{0,256},{128,384},{256,0},{384,128},{1,257},{129,385},{257,1},{385... | collective-permute-start | bytes 98312 | tf_op jit(solution)/shard_map/ppermute | solution.py:195
  142.0 2.2 %collective-permute-start.6 = (f32[16,512]{1,0:T(8,128)S(1)}, f32[16,512]{1,0:T(8,128)S(1)}, u32[]{:S(2)}, u32[]{:S(2)}) collective-permute-start(f32[16,512]{1,0:T(8,128)S(1)} %collective-permute-done.3.s0_ref.shard_ref), channel_id=1, source_target_pairs={{0,384},{128,256},{256,128},{384,0},{1,385},{129,257},{257,129},{3... | collective-permute-start | bytes 98312 | tf_op jit(solution)/shard_map/ppermute | solution.py:195
  144.1 1.6 all-to-all-done.3
  145.7 3.6 %collective-permute-done.6.s3_ref = f32[16,512]{1,0:T(8,128)S(1)} collective-permute-done((f32[16,512]{1,0:T(8,128)S(1)}, f32[16,512]{1,0:T(8,128)S(1)}, u32[]{:S(2)}, u32[]{:S(2)}) %collective-permute-start.6) | collective-permute-done | bytes 32800 | tf_op jit(solution)/shard_map/ppermute | solution.py:195
  150.3 7.3 %all-to-all-start.4 = ((bf16[8,64,640]{2,1,0:T(8,128)(2,1)}), bf16[8,64,640]{2,1,0:T(8,128)(2,1)S(1)}, u32[]{:S(2)}, u32[]{:S(2)}) async-start(bf16[8,64,640]{2,1,0:T(8,128)(2,1)} %shard_map.106), calls=%async_computation.4 | async-start | bytes 1310720 | tf_op jit(solution)/shard_map/all_to_all | solution.py:37
  157.6 8.0 %shard_map.107 = bf16[128,8192]{1,0:T(8,128)(2,1)} custom-call(bf16[128,512]{1,0:T(8,128)(2,1)} %get-tuple-element.30.key_ref, bf16[8,2,4,128,512]{4,3,2,1,0:T(8,128)(2,1)} %bitcast.13, bf16[128,8192]{1,0:T(8,128)(2,1)} %x_ref.3, f32[128,128]{1,0:T(8,128)} %get-tuple-element.31.scale_ref, f32[64,128]{1,0:T(8,128)} %get-tuple-element.32.gain_ref), custom_call_target="tpu_custom_call" | custom-call | flops 1073741824 | bytes 12582912 | tf_op jit(solution)/shard_map/pallas_call | solution.py:165
  166.7 1.8 all-to-all-done.4.gathered_ref
  168.5 1.8 shard_map.108
  (33 shorter events, 8.5 us)
Async XLA Ops:
  8.7 18.3 %all-to-all-start = ((bf16[8,16,1536]{2,1,0:T(8,128)(2,1)}), bf16[8,16,1536]{2,1,0:T(8,128)(2,1)S(1)}, u32[]{:S(2)}, u32[]{:S(2)}) async-start(bf16[8,16,1536]{2,1,0:T(8,128)(2,1)} %shard_map.103), calls=%async_computation | async-start | bytes 786432 | tf_op jit(solution)/shard_map/all_to_all | solution.py:37
  19.0 138.6 %all-gather.2.cloned.1.call-start = ((), (), s32[]{:S(2)}) async-start(), calls=%async_computation.5 | async-start | bytes 8519680 | tf_op jit(solution)/shard_map/all_gather | solution.py:285
  27.1 0.8 copy-start.8
  27.9 42.0 %all-to-all-start.1 = ((bf16[8,128,1536]{2,1,0:T(8,128)(2,1)}), bf16[8,128,1536]{2,1,0:T(8,128)(2,1)S(1)}, u32[]{:S(2)}, u32[]{:S(2)}) async-start(bf16[8,128,1536]{2,1,0:T(8,128)(2,1)} %get-tuple-element.25), calls=%async_computation.1 | async-start | bytes 6291456 | tf_op jit(solution)/shard_map/all_to_all | solution.py:37
  33.2 11.0 %collective-permute-start = (bf16[128,1024]{1,0:T(8,128)(2,1)S(1)}, bf16[128,1024]{1,0:T(8,128)(2,1)S(1)}, u32[]{:S(2)}, u32[]{:S(2)}) collective-permute-start(bf16[128,1024]{1,0:T(8,128)(2,1)S(1)} %slice.7.m0_ref), channel_id=1, source_target_pairs={{0,128},{128,0},{256,384},{384,256},{1,129},{129,1},{257,385},{385... | collective-permute-start | bytes 786440 | tf_op jit(solution)/shard_map/ppermute | solution.py:195
  35.2 23.4 %collective-permute-start.1 = (bf16[128,1024]{1,0:T(8,128)(2,1)S(1)}, bf16[128,1024]{1,0:T(8,128)(2,1)S(1)}, u32[]{:S(2)}, u32[]{:S(2)}) collective-permute-start(bf16[128,1024]{1,0:T(8,128)(2,1)S(1)} %slice.7.m0_ref), channel_id=1, source_target_pairs={{0,256},{128,384},{256,0},{384,128},{1,257},{129,385},{257,1},{385... | collective-permute-start | bytes 786440 | tf_op jit(solution)/shard_map/ppermute | solution.py:195
  37.1 22.1 %collective-permute-start.2 = (bf16[128,1024]{1,0:T(8,128)(2,1)S(1)}, bf16[128,1024]{1,0:T(8,128)(2,1)S(1)}, u32[]{:S(2)}, u32[]{:S(2)}) collective-permute-start(bf16[128,1024]{1,0:T(8,128)(2,1)S(1)} %slice.7.m0_ref), channel_id=1, source_target_pairs={{0,384},{128,256},{256,128},{384,0},{1,385},{129,257},{257,129},{3... | collective-permute-start | bytes 786440 | tf_op jit(solution)/shard_map/ppermute | solution.py:195
  44.2 0.7 copy-start
  58.5 0.7 copy-start.2
  59.2 0.7 copy-start.4
  118.7 16.1 %collective-permute-start.3 = (f32[16,512]{1,0:T(8,128)S(1)}, f32[16,512]{1,0:T(8,128)S(1)}, u32[]{:S(2)}, u32[]{:S(2)}) collective-permute-start(f32[16,512]{1,0:T(8,128)S(1)} %get-tuple-element.28), channel_id=1, source_target_pairs={{0,0},{2,16},{4,32},{6,48},{8,64},{10,80},{12,96},{14,112},{16,2},... | collective-permute-start | bytes 98312 | tf_op jit(solution)/shard_map/ppermute | solution.py:296
  127.8 17.8 %all-to-all-start.3 = ((f32[64,1,128]{2,1,0:T(1,128)}), f32[64,1,128]{2,1,0:T(1,128)S(1)}, u32[]{:S(2)}, u32[]{:S(2)}) async-start(f32[64,1,128]{2,1,0:T(1,128)} %bitcast.5), calls=%async_computation.3 | async-start | bytes 65536 | tf_op jit(solution)/shard_map/all_to_all | solution.py:37
  134.8 10.9 %collective-permute-start.4 = (f32[16,512]{1,0:T(8,128)S(1)}, f32[16,512]{1,0:T(8,128)S(1)}, u32[]{:S(2)}, u32[]{:S(2)}) collective-permute-start(f32[16,512]{1,0:T(8,128)S(1)} %collective-permute-done.3.s0_ref.shard_ref), channel_id=1, source_target_pairs={{0,128},{128,0},{256,384},{384,256},{1,129},{129,1},{257,385},{385... | collective-permute-start | bytes 98312 | tf_op jit(solution)/shard_map/ppermute | solution.py:195
  137.8 7.9 %collective-permute-start.5 = (f32[16,512]{1,0:T(8,128)S(1)}, f32[16,512]{1,0:T(8,128)S(1)}, u32[]{:S(2)}, u32[]{:S(2)}) collective-permute-start(f32[16,512]{1,0:T(8,128)S(1)} %collective-permute-done.3.s0_ref.shard_ref), channel_id=1, source_target_pairs={{0,256},{128,384},{256,0},{384,128},{1,257},{129,385},{257,1},{385... | collective-permute-start | bytes 98312 | tf_op jit(solution)/shard_map/ppermute | solution.py:195
  142.0 7.3 %collective-permute-start.6 = (f32[16,512]{1,0:T(8,128)S(1)}, f32[16,512]{1,0:T(8,128)S(1)}, u32[]{:S(2)}, u32[]{:S(2)}) collective-permute-start(f32[16,512]{1,0:T(8,128)S(1)} %collective-permute-done.3.s0_ref.shard_ref), channel_id=1, source_target_pairs={{0,384},{128,256},{256,128},{384,0},{1,385},{129,257},{257,129},{3... | collective-permute-start | bytes 98312 | tf_op jit(solution)/shard_map/ppermute | solution.py:195
  150.3 18.2 %all-to-all-start.4 = ((bf16[8,64,640]{2,1,0:T(8,128)(2,1)}), bf16[8,64,640]{2,1,0:T(8,128)(2,1)S(1)}, u32[]{:S(2)}, u32[]{:S(2)}) async-start(bf16[8,64,640]{2,1,0:T(8,128)(2,1)} %shard_map.106), calls=%async_computation.4 | async-start | bytes 1310720 | tf_op jit(solution)/shard_map/all_to_all | solution.py:37
  157.6 10.9 %copy-start.1 = (bf16[128,1024]{1,0:T(8,128)(2,1)S(1)}, bf16[128,1024]{1,0:T(8,128)(2,1)}, u32[]{:S(2)}) copy-start(bf16[128,1024]{1,0:T(8,128)(2,1)} %copy-done) | copy-start | bytes 786436
  157.6 10.9 %copy-start.3 = (bf16[128,1024]{1,0:T(8,128)(2,1)S(1)}, bf16[128,1024]{1,0:T(8,128)(2,1)}, u32[]{:S(2)}) copy-start(bf16[128,1024]{1,0:T(8,128)(2,1)} %copy-done.2) | copy-start | bytes 786436
  157.6 10.9 %copy-start.5 = (bf16[128,1024]{1,0:T(8,128)(2,1)S(1)}, bf16[128,1024]{1,0:T(8,128)(2,1)}, u32[]{:S(2)}) copy-start(bf16[128,1024]{1,0:T(8,128)(2,1)} %copy-done.4) | copy-start | bytes 786436
  157.6 10.9 %copy-start.6 = (f32[16,512]{1,0:T(8,128)S(1)}, f32[16,512]{1,0:T(8,128)}, u32[]{:S(2)}) copy-start(f32[16,512]{1,0:T(8,128)} %first_ref.3) | copy-start | bytes 98308
  157.6 10.9 %copy-start.7 = (f32[16,512]{1,0:T(8,128)S(1)}, f32[16,512]{1,0:T(8,128)}, u32[]{:S(2)}) copy-start(f32[16,512]{1,0:T(8,128)} %second_ref.3) | copy-start | bytes 98308
Sparse Core Ops, SparseCore 0:
  27.9 124.8 all-gather.1
